TPU v7x, 32 devices: a whole 2x2x4 slice. The times are simulated.
32 devices in a mesh: row: 4 (over z), rep: 4 (over y, x), feat: 2 (over core).
Axes of the slice: x: 2, y: 2, z: 4, core: 2. Of those that a mesh axis runs over, the one named last changes fastest.
Arguments:
- features: bfloat16 [8192, 128], P(('row', 'rep')), may hold values from -6 to 6
- weight: bfloat16 [128, 256], P(None, 'feat'), may hold values from -0.5 to 0.5
- pair_tiles: int32 [16, 4, 8], P(('row', 'rep')), may hold values from 0 to 63, as said below
- pair_count: int32 [16, 4], P(('row', 'rep')), may hold values from 0 to 8, as said below
- tile_vals: bfloat16 [16, 4, 8, 128, 128], P(('row', 'rep')), may hold values from 0 to 1, as said below
- cotangent: bfloat16 [8192, 256], P(('row', 'rep'), 'feat'), may hold values from -0.0625 to 0.0625
Outputs:
- activated: bfloat16 [8192, 256], P(('row', 'rep'), 'feat')
- grad_weight: float32 [128, 256], P(None, 'feat')
Inputs may be any that keep to these rules, and one draw needn't show every extreme that they name: The 8 positions of each list pair_tiles[b, j] are distinct. Every block b has an owner j with pair_count[b, j] = 8. `tile_vals`: entries are 0 or 1.
All inputs are finite; a program needn't handle non-finite values.
Results may differ from a plain program's by a relative error of at most 0.001.
Values may be sent and summed in bfloat16 or wider, within the bound.
No kernel may reach another device: no remote copies, remote signals or barrier semaphores. Data moves between devices by JAX's collectives and lax.ppermute only.
A program may use at most 128 MiB of HBM per device.

v0:
```python
import jax
import jax.numpy as jnp
from jax import lax
from jax.sharding import PartitionSpec as P

highest = lax.Precision.HIGHEST


def local_degrees(tile_pos, counts, values, row_tiles, col_tiles):
    slot_ids = jnp.arange(tile_pos.shape[1])
    active = (slot_ids[None, :] < counts[:, None]).astype(jnp.float32)
    row_sums = jnp.sum(values, axis=-1, dtype=jnp.float32) * active[:, :, None]
    placing = (tile_pos[:, :, None] // col_tiles == jnp.arange(row_tiles)).astype(jnp.float32)
    return jnp.einsum("jpr,jpu->ru", placing, row_sums, precision=highest).reshape(-1)


def forward_fold(accumulator, portion, offset, tile_pos, counts, values, col_tiles):
    tile_size = values.shape[-1]
    feat_width = portion.shape[1]
    portion_tiles = portion.shape[0] // tile_size
    first_tile = offset // tile_size
    slot_ids = jnp.arange(tile_pos.shape[1])
    tile_ids = jnp.arange(accumulator.shape[0])
    blocked = portion.reshape(portion_tiles, tile_size, feat_width)

    def forward_add_owner(owner_index, summed):
        positions = tile_pos[owner_index]
        local_tile = owner_index * col_tiles + positions % col_tiles
        usable = (slot_ids < counts[owner_index]) & (local_tile >= 0) & (local_tile < portion_tiles)
        sources = blocked[jnp.clip(local_tile, 0, portion_tiles - 1)]
        entries = values[owner_index].astype(portion.dtype) * usable[:, None, None].astype(
            portion.dtype
        )
        products = jnp.einsum(
            "puv,pvf->puf", entries, sources, preferred_element_type=jnp.float32, precision=highest
        )
        placing = (positions[:, None] // col_tiles == tile_ids).astype(jnp.float32)
        return summed + jnp.einsum("pr,puf->ruf", placing, products, precision=highest)

    lowest = first_tile // col_tiles
    beyond = (first_tile + portion_tiles - 1) // col_tiles + 1
    return lax.fori_loop(lowest, beyond, forward_add_owner, accumulator)


def adjoint_term(offset, extent, tile_pos, counts, values, col_tiles, slopes_all):
    tile_size = values.shape[-1]
    feat_width = slopes_all.shape[1]
    span_tiles = extent // tile_size
    first_tile = offset // tile_size
    slot_ids = jnp.arange(tile_pos.shape[1])
    target_ids = jnp.arange(span_tiles)
    row_blocked = slopes_all.reshape(-1, tile_size, feat_width)

    def adjoint_add_owner(owner_index, summed):
        positions = tile_pos[owner_index]
        local_tile = owner_index * col_tiles + positions % col_tiles
        usable = slot_ids < counts[owner_index]
        sources = row_blocked[positions // col_tiles]
        entries = values[owner_index].astype(jnp.float32) * usable[:, None, None].astype(
            jnp.float32
        )
        products = jnp.einsum("puv,puf->pvf", entries, sources, precision=highest)
        placing = ((local_tile[:, None] == target_ids) & usable[:, None]).astype(jnp.float32)
        return summed + jnp.einsum("pl,pvf->lvf", placing, products, precision=highest)

    lowest = first_tile // col_tiles
    beyond = (first_tile + span_tiles - 1) // col_tiles + 1
    start_sum = jnp.zeros((span_tiles, tile_size, feat_width), jnp.float32)
    result = lax.fori_loop(lowest, beyond, adjoint_add_owner, start_sum)
    return result.reshape(extent, feat_width)


def activate(preact, row_scale, cotangent):
    sigmoid_z = jax.nn.sigmoid(preact)
    activated = (preact * sigmoid_z).astype(jnp.bfloat16)
    slopes = (
        row_scale * cotangent.astype(jnp.float32) * sigmoid_z * (1.0 + preact * (1.0 - sigmoid_z))
    )
    return (activated, slopes)


def shards(features, weight, pair_tiles, pair_count, tile_vals, cotangent):
    shard_rows = features.shape[0]
    tile_size = tile_vals.shape[-1]
    col_tiles = shard_rows // tile_size
    row_tiles = lax.axis_size("rep") * col_tiles
    tile_pos = pair_tiles[0]
    counts = pair_count[0]
    values = tile_vals[0]
    degree_part = local_degrees(tile_pos, counts, values, row_tiles, col_tiles)
    projected = jnp.dot(features, weight, preferred_element_type=jnp.float32)
    feat_width = projected.shape[1]
    start_acc = jnp.zeros((row_tiles, tile_size, feat_width), jnp.float32)
    gathered = forward_fold(
        start_acc,
        lax.all_gather(projected, "row", axis=0, tiled=True),
        jnp.int32(0),
        tile_pos,
        counts,
        values,
        col_tiles,
    )
    summed, degree_sum = (
        lax.psum_scatter(gathered.reshape(-1, feat_width), "rep", scatter_dimension=0, tiled=True),
        lax.psum_scatter(degree_part, "rep", scatter_dimension=0, tiled=True),
    )
    row_scale = lax.rsqrt(degree_sum + 1.0)[:, None]
    activated, slopes = activate(row_scale * (summed + projected), row_scale, cotangent)
    slopes_all = lax.all_gather(slopes, "rep", axis=0, tiled=True)
    incoming = lax.psum_scatter(
        adjoint_term(
            jnp.int32(0),
            lax.axis_size("row") * shard_rows,
            tile_pos,
            counts,
            values,
            col_tiles,
            slopes_all,
        ),
        "row",
        scatter_dimension=0,
        tiled=True,
    )
    local_grad = jnp.dot(features.astype(jnp.float32).T, incoming + slopes, precision=highest)
    grad_weight = lax.psum(local_grad, ("row", "rep"))
    return (activated, grad_weight)


def solution(mesh):
    return jax.shard_map(
        shards,
        mesh=mesh,
        in_specs=(
            P(("row", "rep"), None),
            P(None, "feat"),
            P(("row", "rep"), None, None),
            P(("row", "rep"), None),
            P(("row", "rep"), None, None, None, None),
            P(("row", "rep"), "feat"),
        ),
        out_specs=(P(("row", "rep"), "feat"), P(None, "feat")),
        check_vma=False,
    )
```

profile of v0, /device:TPU:0, one launch (start us, length us, event | category | flops | bytes accessed | tf_op | source)
XLA Modules:
  0.0 290.2 jit_solution(4464882729234447639)
XLA Ops:
  7.2 0.8 copy-done
  8.1 1.7 fusion.45
  9.8 30.7 %all-gather.3.cloned.1.call-done = f32[2048,128]{1,0:T(8,128)} async-done(((f32[512,128]{1,0:T(8,128)}), f32[2048,128]{1,0:T(8,128)}) %all-gather.3.cloned.1.call-update) | async-done | bytes 1048592 | tf_op jit(solution)/shard_map/all_gather | solution.py:96
  40.5 27.3 %while.28 = (s32[]{:T(128)}, f32[16,128,128]{2,0,1:T(8,128)S(1)}, s32[4,8]{1,0:T(4,128)}, bf16[4,8,128,128]{3,2,1,0:T(8,128)(2,1)}, s32[4]{0:T(128)}, /*index=5*...) while((s32[]{:T(128)}, f32[16,128,128]{2,0,1:T(8,128)S(1)}, s32[4,8]{1,0:T(4,128)}, ...), condition=%wide.region_3.4_spmd.clone, body=%wide.region_2.3_spmd.clone.sunk | while | flops 227280384 | bytes 4985947 | solution.py:42
  40.5 0.8 fusion.65
  41.3 1.8 gather_fusion
  43.1 0.6 dynamic_slice.85
  43.7 0.7 and_convert_fusion.2
  44.4 1.7 fusion.66
  46.1 1.2 convolution_add_fusion.4
  47.4 0.8 fusion.65
  48.2 1.8 gather_fusion
  50.0 0.6 dynamic_slice.85
  50.6 0.7 and_convert_fusion.2
  51.2 1.7 fusion.66
  52.9 1.2 convolution_add_fusion.4
  54.2 0.8 fusion.65
  55.0 1.8 gather_fusion
  56.8 0.6 dynamic_slice.85
  57.4 0.7 and_convert_fusion.2
  58.1 1.7 fusion.66
  59.8 1.2 convolution_add_fusion.4
  61.1 0.8 fusion.65
  61.8 1.8 gather_fusion
  63.7 0.6 dynamic_slice.85
  64.3 0.7 and_convert_fusion.2
  64.9 1.7 fusion.66
  66.6 1.2 convolution_add_fusion.4
  67.9 1.3 copy.11
  69.3 0.5 copy-done.9
  69.8 0.6 dynamic-slice
  71.1 0.3 convert_reduce_fusion
  71.5 0.3 convolution_bitcast_fusion.1
  71.8 10.3 %all-reduce = f32[2048]{0:T(1024)S(1)} all-reduce(f32[2048]{0:T(1024)S(1)} %convolution_bitcast_fusion.1), channel_id=2, replica_groups=mesh['row'=4,'rep'=4,'feat'=2] {'rep'}, use_global_device_ids=true, to_apply=%region_1.2.clone | all-reduce | flops 2048 | bytes 16384
  82.1 0.1 fusion.42
  82.2 14.5 %reduce-scatter.3.cloned.1.call-done = f32[512,128]{1,0:T(8,128)} async-done(((f32[2048,128]{1,0:T(8,128)}), f32[512,128]{1,0:T(8,128)}) %reduce-scatter.3.cloned.1.call-update) | async-done | bytes 262160 | tf_op jit(solution)/shard_map/reduce_scatter | solution.py:104
  96.7 1.9 add_multiply_fusion
  98.7 26.7 %all-gather.5.cloned.1.call-done = f32[2048,128]{1,0:T(8,128)} async-done(((f32[512,128]{1,0:T(8,128)}), f32[2048,128]{1,0:T(8,128)}) %all-gather.5.cloned.1.call-update) | async-done | bytes 1048592 | tf_op jit(solution)/shard_map/all_gather | solution.py:109
  125.4 21.5 %while.29 = (s32[]{:T(128)}, f32[16,128,128]{2,0,1:T(8,128)S(1)}, s32[4,8]{1,0:T(4,128)S(1)}, s32[4]{0:T(128)S(1)}, bf16[4,8,128,128]{3,2,1,0:T(8,128)(2,1)S(1)}...) while((s32[]{:T(128)}, f32[16,128,128]{2,0,1:T(8,128)S(1)}, ...), condition=%wide.region_6.7_spmd.clone, body=%wide.region_5.6_spmd.clone.sunk | while | flops 227280384 | bytes 4985771 | solution.py:69
  125.4 1.8 gather_fusion.1
  127.3 0.6 dynamic_slice.89
  127.8 0.6 iota_compare_fusion.7
  128.4 1.1 fusion.71
  129.5 1.2 convolution_add_fusion.5
  130.8 1.8 gather_fusion.1
  132.6 0.6 dynamic_slice.89
  133.2 0.6 iota_compare_fusion.7
  133.8 1.1 fusion.71
  134.9 1.2 convolution_add_fusion.5
  136.2 1.8 gather_fusion.1
  138.0 0.6 dynamic_slice.89
  138.6 0.6 iota_compare_fusion.7
  139.2 1.1 fusion.71
  140.3 1.2 convolution_add_fusion.5
  141.6 1.8 gather_fusion.1
  143.4 0.6 dynamic_slice.89
  144.0 0.6 iota_compare_fusion.7
  144.5 1.1 fusion.71
  145.7 1.2 convolution_add_fusion.5
  146.9 1.3 copy.12
  148.3 27.2 %reduce-scatter.5.cloned.1.call-done = f32[512,128]{1,0:T(8,128)} async-done(((f32[2048,128]{1,0:T(8,128)}), f32[512,128]{1,0:T(8,128)}) %reduce-scatter.5.cloned.1.call-update) | async-done | bytes 262160 | tf_op jit(solution)/shard_map/reduce_scatter | solution.py:110
  175.5 2.0 convolution_bitcast_fusion
  177.5 104.5 %all-reduce.3.cloned.1.call-done = f32[128,128]{0,1:T(8,128)} async-done(((f32[128,128]{0,1:T(8,128)}), f32[128,128]{0,1:T(8,128)}) %all-reduce.3.cloned.1.call-update) | async-done | bytes 65552 | tf_op jit(solution)/shard_map/psum | solution.py:125
  282.1 1.6 copy.13
  (64 shorter events, 0.7 us)
Async XLA Ops:
  7.2 0.9 copy-start
  7.2 33.4 %all-gather.3.cloned.1.call-start = ((), (), s32[]{:S(2)}) async-start(), calls=%async_computation.2 | async-start | bytes 1310720 | tf_op jit(solution)/shard_map/all_gather | solution.py:96
  9.8 86.9 %reduce-scatter.3.cloned.1.call-start = ((), (), s32[]{:S(2)}) async-start(), calls=%async_computation.3 | async-start | bytes 1310720 | tf_op jit(solution)/shard_map/reduce_scatter | solution.py:104
  40.5 2.6 copy-start.7
  40.5 3.2 %copy-start.5 = (s32[4,8]{1,0:T(4,128)S(1)}, s32[4,8]{1,0:T(4,128)}, u32[]{:S(2)}) copy-start(s32[4,8]{1,0:T(4,128)} %get-tuple-element.468) | copy-start | bytes 388 | tf_op jit(solution)/shard_map/while
  47.4 2.6 copy-start.7
  47.4 3.2 %copy-start.5 = (s32[4,8]{1,0:T(4,128)S(1)}, s32[4,8]{1,0:T(4,128)}, u32[]{:S(2)}) copy-start(s32[4,8]{1,0:T(4,128)} %get-tuple-element.468) | copy-start | bytes 388 | tf_op jit(solution)/shard_map/while
  54.2 2.6 copy-start.7
  54.2 3.2 %copy-start.5 = (s32[4,8]{1,0:T(4,128)S(1)}, s32[4,8]{1,0:T(4,128)}, u32[]{:S(2)}) copy-start(s32[4,8]{1,0:T(4,128)} %get-tuple-element.468) | copy-start | bytes 388 | tf_op jit(solution)/shard_map/while
  61.0 2.6 copy-start.7
  61.1 3.2 %copy-start.5 = (s32[4,8]{1,0:T(4,128)S(1)}, s32[4,8]{1,0:T(4,128)}, u32[]{:S(2)}) copy-start(s32[4,8]{1,0:T(4,128)} %get-tuple-element.468) | copy-start | bytes 388 | tf_op jit(solution)/shard_map/while
  69.2 0.7 copy-start.9
  69.2 1.9 copy-start.1
  69.2 2.2 copy-start.8
  69.2 2.3 copy-start.6
  69.2 27.5 %copy-start.2 = (f32[512,128]{1,0:T(8,128)S(1)}, f32[512,128]{1,0:T(8,128)}, u32[]{:S(2)}) copy-start(f32[512,128]{1,0:T(8,128)} %fusion.45) | copy-start | bytes 786436
  69.2 27.5 %copy-start.4 = (bf16[512,128]{1,0:T(8,128)(2,1)S(1)}, bf16[512,128]{1,0:T(8,128)(2,1)}, u32[]{:S(2)}) copy-start(bf16[512,128]{1,0:T(8,128)(2,1)} %param.15) | copy-start | bytes 393220
  69.2 56.2 %all-gather.5.cloned.1.call-start = ((), (), s32[]{:S(2)}) async-start(), calls=%async_computation.4 | async-start | bytes 1310720 | tf_op jit(solution)/shard_map/all_gather | solution.py:109
  98.6 76.9 %reduce-scatter.5.cloned.1.call-start = ((), (), s32[]{:S(2)}) async-start(), calls=%async_computation.5 | async-start | bytes 1310720 | tf_op jit(solution)/shard_map/reduce_scatter | solution.py:110
  148.2 27.3 %copy-start.3 = (f32[512,128]{1,0:T(8,128)S(1)}, f32[512,128]{1,0:T(8,128)}, u32[]{:S(2)}) copy-start(f32[512,128]{1,0:T(8,128)} %get-tuple-element.368) | copy-start | bytes 786436
  148.2 133.8 %all-reduce.3.cloned.1.call-start = ((), (), s32[]{:S(2)}) async-start(), calls=%async_computation.6 | async-start | bytes 131072 | tf_op jit(solution)/shard_map/psum | solution.py:125
Sparse Core Ops, SparseCore 0:
  9.9 30.6 all-gather.2
  69.4 27.2 reduce-scatter.2
  98.7 26.6 all-gather.4
  148.4 27.1 reduce-scatter.4
  181.4 100.5 all-reduce.2
where the time goes:
time: 291 us; the launch traced here: 290 us
  waiting for transfers between devices  204 us (70%)
  local copies, waits for them, and re-layouts  25.4 us (9%)
  matrix products  24.8 us (9%)
  between operations  14.5 us (5%)
  other arithmetic  10.6 us (4%)
  blocking collectives  10.3 us (4%)
    psum x1, waiting for transfers between devices, shards(): grad_weight = lax.psum(local_grad, ('row', 'rep'))  105 us
    all_gather x1, waiting for transfers between devices, shards(): lax.all_gather(projected, 'row', axis=0, tiled=True)  30.7 us
    reduce_scatter x1, waiting for transfers between devices, shards(): lax.psum_scatter(adjoint_term(jnp.int32(0), lax.axis_size('row') * shard_...  27.2 us
    all_gather x1, waiting for transfers between devices, shards(): slopes_all = lax.all_gather(slopes, 'rep', axis=0, tiled=True)  26.7 us
    reduce_scatter x1, waiting for transfers between devices, shards(): lax.psum_scatter(gathered.reshape(-1, feat_width), 'rep', scatter_dimensi...  14.5 us
    unnamed x1, blocking collectives  10.3 us
    gather x4, local copies, waits for them, and re-layouts, adjoint_add_owner(): sources = row_blocked[positions // col_tiles]  7.22 us
    gather x4, local copies, waits for them, and re-layouts, forward_add_owner(): sources = blocked[jnp.clip(local_tile, 0, portion_tiles - 1)]  7.22 us
  transfers between devices with their start and end apart: 5, of which 5 were waited for; matrix products, arithmetic and copies ran while one was open for 0% of the time, Pallas kernels for 0%

commit v1 on v0

v1 whole, which is shorter than its diff:
```python
import functools

import jax
import jax.numpy as jnp
from jax import lax
from jax.experimental import pallas as pl
from jax.experimental.pallas import tpu as pltpu
from jax.sharding import PartitionSpec as P

f32 = jnp.float32
bf16 = jnp.bfloat16
LONGEST = 8


def vmem(n):
    return [pl.BlockSpec(memory_space=pltpu.VMEM)] * n


def smem(n):
    return [pl.BlockSpec(memory_space=pltpu.SMEM)] * n


def lower_half(shape):
    lane = lax.broadcasted_iota(jnp.int32, shape, len(shape) - 1)
    return lane < shape[-1] // 2


def pack_kernel(x_ref, out_ref):
    half = x_ref.shape[0] // 2
    width = x_ref.shape[1]
    first = lax.axis_index("feat") == 0
    top = x_ref[:half].astype(f32)
    low = x_ref[half:].astype(f32)
    kept = jnp.where(first, top, low)
    moved = pltpu.roll(jnp.where(first, low, top), width // 2, 1)
    left = lower_half(kept.shape)
    out_ref[...] = jnp.where(left == first, kept, moved).astype(bf16)


def spread(block_ref, at, sources_ref, tile):
    half = block_ref.shape[0] if at is None else block_ref.shape[1]
    x = (block_ref[...] if at is None else block_ref[at]).astype(f32)
    left = lower_half(x.shape)
    top = jnp.where(left, x, 0.0).astype(bf16)
    low = jnp.where(left, pltpu.roll(x, x.shape[1] // 2, 1), 0.0).astype(bf16)
    n = half // tile
    for c in range(n):
        sources_ref[c] = top[c * tile : (c + 1) * tile]
        sources_ref[n + c] = low[c * tile : (c + 1) * tile]


def add_tiles(j, tiles_ref, pos_ref, count_ref, sources_ref, acc_ref, col_tiles):
    spare = acc_ref.shape[0] - 1
    for p in range(tiles_ref.shape[1]):
        t = pos_ref[j, p]
        i = jnp.where(p < count_ref[0, j], t // col_tiles, spare)
        acc_ref[i] += jnp.dot(
            tiles_ref[j, p], sources_ref[t % col_tiles], preferred_element_type=f32
        )


def own_kernel(tiles_ref, pos_ref, count_ref, x_ref, acc_ref, deg_ref, sources_ref):
    n_own, slots, tile, _ = tiles_ref.shape
    col_tiles = sources_ref.shape[0]
    row_tiles = acc_ref.shape[0] - 1
    acc_ref[...] = jnp.zeros_like(acc_ref)
    spread(x_ref, None, sources_ref, tile)
    add_tiles(
        lax.axis_index("row"), tiles_ref, pos_ref, count_ref, sources_ref, acc_ref, col_tiles
    )
    lane = lax.broadcasted_iota(jnp.int32, (tile, 128), 1)

    def sums_of(j, total):
        for p in range(slots):
            i = jnp.where(p < count_ref[0, j], pos_ref[j, p] // col_tiles, -1)
            mark = (lane == i).astype(f32).astype(bf16)
            total = total + jnp.dot(tiles_ref[j, p], mark, preferred_element_type=f32)
        return total

    total = jnp.zeros((tile, 128), f32)
    if n_own <= LONGEST:
        for j in range(n_own):
            total = sums_of(j, total)
    else:
        total = lax.fori_loop(0, n_own, sums_of, total)
    deg_ref[...] = total.T[:row_tiles]


def fold_kernel(n_blocks, *refs):
    tiles_ref, pos_ref, count_ref, start_ref, deg_ref = refs[:5]
    blocks = refs[5 : 5 + n_blocks]
    outs = refs[5 + n_blocks : -2]
    acc_ref, sources_ref = refs[-2:]
    n_own, slots, tile, _ = tiles_ref.shape
    col_tiles = sources_ref.shape[0]
    me = lax.axis_index("row")
    rep = lax.axis_index("rep")
    acc_ref[...] = start_ref[...]
    if n_blocks == n_own - 1:
        for k, block in enumerate(blocks):
            j = lax.rem(me + n_own - 1 - k, n_own)
            spread(block, None, sources_ref, tile)
            add_tiles(j, tiles_ref, pos_ref, count_ref, sources_ref, acc_ref, col_tiles)
    else:

        @pl.loop(1, n_own)
        def _(k):
            j = lax.rem(me + k, n_own)
            spread(blocks[0], j, sources_ref, tile)
            add_tiles(j, tiles_ref, pos_ref, count_ref, sources_ref, acc_ref, col_tiles)

    n_rep = len(outs)
    for k, out in enumerate(outs):
        q = lax.rem(rep + k, n_rep)
        n = col_tiles // 2
        for c in range(n):
            top = acc_ref[q * col_tiles + c]
            low = acc_ref[q * col_tiles + n + c]
            out[c * tile : (c + 1) * tile] = jnp.where(
                lower_half(top.shape), top, pltpu.roll(low, top.shape[1] // 2, 1)
            )
        rows = out.shape[0] - n * tile
        out[n * tile :] = jnp.zeros((rows, out.shape[1]), f32)
        for c in range(col_tiles):
            out[n * tile + c : n * tile + c + 1] = deg_ref[pl.ds(q * col_tiles + c, 1)]


def sum_kernel(*refs):
    total = refs[0][...]
    for ref in refs[1:-1]:
        total = total + ref[...]
    refs[-1][...] = total


def split(x):
    high = x.astype(bf16)
    return high, (x - high.astype(f32)).astype(bf16)


def layer_kernel(mine_ref, other_ref, x_ref, w_ref, cot_ref, act_ref, grad_ref):
    half = other_ref.shape[0]
    width = other_ref.shape[1]
    tile = 128
    first = lax.axis_index("feat") == 0
    mine = mine_ref[:half]
    other = other_ref[...]
    here = jnp.where(first, mine, other)
    there = jnp.where(first, other, mine)
    left = lower_half(here.shape)
    top = jnp.where(left, here, pltpu.roll(there, width // 2, 1)) + x_ref[:half].astype(f32)
    low = jnp.where(left, pltpu.roll(here, width // 2, 1), there) + x_ref[half:].astype(f32)
    agg = jnp.concatenate([top, low], axis=0)
    scales = lax.rsqrt(mine_ref[half:] + 1.0)
    rows = scales.shape[0]
    turned = jnp.concatenate([scales] * (128 // rows), axis=0).T
    scale = jnp.concatenate(
        [jnp.broadcast_to(turned[:, c : c + 1], (tile, 128)) for c in range(2 * half // tile)],
        axis=0,
    )
    high, rest = split(agg)
    w = w_ref[...]
    preact = jnp.dot(high, w, preferred_element_type=f32)
    preact = scale * (preact + jnp.dot(rest, w, preferred_element_type=f32))
    sig = 1.0 / (1.0 + jnp.exp(-preact))
    act_ref[...] = (preact * sig).astype(bf16)
    slopes = scale * cot_ref[...].astype(f32) * sig * (1.0 + preact * (1.0 - sig))
    s_high, s_rest = split(slopes)

    def turned_dot(a, b):
        return lax.dot_general(a, b, (((0,), (0,)), ((), ())), preferred_element_type=f32)

    grad_ref[...] = (
        turned_dot(high, s_high) + turned_dot(high, s_rest) + turned_dot(rest, s_high)
    )


def shape(*dims, dtype=f32):
    return jax.ShapeDtypeStruct(dims, dtype)


def call(kernel, outs, in_specs, scratch=(), cost=None):
    return pl.pallas_call(
        kernel,
        out_shape=outs,
        in_specs=in_specs,
        out_specs=vmem(1)[0] if not isinstance(outs, (list, tuple)) else vmem(len(outs)),
        scratch_shapes=list(scratch),
        compiler_params=pltpu.CompilerParams(vmem_limit_bytes=48 * 1024 * 1024),
        cost_estimate=cost,
    )


def total_over(x, axis):
    n = lax.axis_size(axis)
    if n > LONGEST:
        return lax.psum(x, axis)
    parts = [lax.ppermute(x, axis, [(i, (i + k) % n) for i in range(n)]) for k in range(1, n)]
    return call(sum_kernel, shape(*x.shape), vmem(n))(x, *parts)


def shards(features, weight, pair_tiles, pair_count, tile_vals, cotangent):
    rows, width = features.shape
    _, n_own, slots, tile, _ = tile_vals.shape
    col_tiles = rows // tile
    half = rows // 2
    n_rep = lax.axis_size("rep")
    row_tiles = n_rep * col_tiles
    pos, counts, tiles = pair_tiles[0], pair_count, tile_vals[0]

    packed = call(pack_kernel, shape(half, width, dtype=bf16), vmem(1))(features)
    if n_own <= LONGEST:
        blocks = [
            lax.ppermute(packed, "row", [(i, (i + k) % n_own) for i in range(n_own)])
            for k in range(1, n_own)
        ]
    else:
        blocks = [lax.all_gather(packed, "row")]
    sources = pltpu.VMEM((col_tiles, tile, width), bf16)
    start, degrees = call(
        own_kernel,
        [shape(row_tiles + 1, tile, width), shape(row_tiles, tile)],
        vmem(1) + smem(2) + vmem(1),
        [sources],
        pl.CostEstimate(flops=10**8, bytes_accessed=3 * 10**6, transcendentals=0),
    )(tiles, pos, counts, packed)
    message = shape(half + 8, width)
    mine, *sends = call(
        functools.partial(fold_kernel, len(blocks)),
        [message] * n_rep,
        vmem(1) + smem(2) + vmem(2 + len(blocks)),
        [pltpu.VMEM((row_tiles + 1, tile, width), f32), sources],
    )(tiles, pos, counts, start, degrees, *blocks)
    parts = [
        lax.ppermute(sent, "rep", [(i, (i + k + 1) % n_rep) for i in range(n_rep)])
        for k, sent in enumerate(sends)
    ]
    mine = call(sum_kernel, message, vmem(n_rep))(mine, *parts)
    other = lax.ppermute(mine[:half], "feat", [(0, 1), (1, 0)])
    activated, grad = call(
        layer_kernel,
        [shape(rows, weight.shape[1], dtype=bf16), shape(width, weight.shape[1])],
        vmem(5),
    )(mine, other, features, weight, cotangent)
    grad = total_over(grad, "rep")
    grad = total_over(grad, "row")
    return activated, grad


def solution(mesh):
    return jax.shard_map(
        shards,
        mesh=mesh,
        in_specs=(
            P(("row", "rep"), None),
            P(None, "feat"),
            P(("row", "rep"), None, None),
            P(("row", "rep"), None),
            P(("row", "rep"), None, None, None, None),
            P(("row", "rep"), "feat"),
        ),
        out_specs=(P(("row", "rep"), "feat"), P(None, "feat")),
        check_vma=False,
    )
```

time: 291 us -> 43.2 us (0.15)
  waiting for transfers between devices: 204 us -> 16.8 us
  matrix products: 24.8 us -> 0 us
  local copies, waits for them, and re-layouts: 25.4 us -> 3.49 us
  starting transfers between devices: 0.21 us -> 17.7 us
  between operations: 14.5 us -> 0.71 us
  other arithmetic: 10.6 us -> 0 us
  blocking collectives: 10.3 us -> 0 us
  Pallas kernels: 0 us -> 4.37 us
    psum x1 -> x0, waiting for transfers between devices: 105 us -> none  [shards(): grad_weight = lax.psum(local_grad, ('row', 'rep'))]
    all_gather x2 -> x0, waiting for transfers between devices: 57.5 us -> none  [the longest x1 30.7 us: shards(): lax.all_gather(projected, 'row', axis=0, tiled=True)]
    reduce_scatter x2 -> x0, waiting for transfers between devices: 41.7 us -> none  [the longest x1 27.2 us: shards(): lax.psum_scatter(adjoint_term(jnp.int32(0), lax.axis_size('row') * shard_...]
    dot_general x19 -> x0, matrix products: 24.8 us -> none  [the longest x4 6.68 us: forward_add_owner(): jnp.einsum('puv,pvf->puf', entries, sources, preferred_element_type=jnp.f...]
    ppermute x0 -> x13, starting transfers between devices: none -> 17.7 us  [the longest x6 6.98 us: total_over(): lax.ppermute(x, axis, [(i, (i + k) % n) for i in range(n)])]
    ppermute x0 -> x13, waiting for transfers between devices: none -> 16.8 us  [the longest x6 9 us: total_over(): lax.ppermute(x, axis, [(i, (i + k) % n) for i in range(n)])]
    gather x8 -> x0, local copies, waits for them, and re-layouts: 14.4 us -> none  [the longest x4 7.22 us: adjoint_add_owner(): sources = row_blocked[positions // col_tiles]]
    unnamed x1 -> x0, blocking collectives: 10.3 us -> none
  transfers between devices with their start and end apart: 5 -> 13, of which waited for: 5 -> 11; matrix products, arithmetic and copies ran while one was open for 0% -> 0% of each run, Pallas kernels for 0% -> 3%
where the time goes in v1:
time: 43.2 us; the launch traced here: 43 us
  starting transfers between devices  17.7 us (41%)
  waiting for transfers between devices  16.8 us (39%)
  Pallas kernels  4.37 us (10%)
  local copies, waits for them, and re-layouts  3.49 us (8%)
  between operations  0.71 us (2%)
    ppermute x6, waiting for transfers between devices, total_over(): lax.ppermute(x, axis, [(i, (i + k) % n) for i in range(n)])  9 us
    ppermute x6, starting transfers between devices, total_over(): lax.ppermute(x, axis, [(i, (i + k) % n) for i in range(n)])  6.98 us
    ppermute x3, starting transfers between devices, shards(): lax.ppermute(packed, 'row', [(i, (i + k) % n_own) for i in range(n_own)])  6.11 us
    ppermute x3, waiting for transfers between devices, shards(): lax.ppermute(sent, 'rep', [(i, (i + k + 1) % n_rep) for i in range(n_rep)])  4.72 us
    ppermute x3, starting transfers between devices, shards(): lax.ppermute(sent, 'rep', [(i, (i + k + 1) % n_rep) for i in range(n_rep)])  4.49 us
    unnamed x16, local copies, waits for them, and re-layouts  3.48 us
    ppermute x3, waiting for transfers between devices, shards(): lax.ppermute(packed, 'row', [(i, (i + k) % n_own) for i in range(n_own)])  1.71 us
    ppermute x1, waiting for transfers between devices, shards(): other = lax.ppermute(mine[:half], 'feat', [(0, 1), (1, 0)])  1.33 us
  transfers between devices with their start and end apart: 13, of which 11 were waited for; matrix products, arithmetic and copies ran while one was open for 0% of the time, Pallas kernels for 3%

profile of v1, /device:TPU:0, one launch (start us, length us, event | category | flops | bytes accessed | tf_op | source)
XLA Modules:
  0.0 43.0 jit_solution(12628874851904072642)
XLA Ops:
  0.6 0.0 copy-start.2
  0.6 0.9 %copy-done.2 = bf16[512,128]{1,0:T(8,128)(2,1)S(1)} copy-done((bf16[512,128]{1,0:T(8,128)(2,1)S(1)}, bf16[512,128]{1,0:T(8,128)(2,1)}, u32[]{:S(2)}) %copy-start.2) | copy-done | bytes 131096
  1.5 0.1 shard_map.77.x_ref
  1.6 5.1 %collective-permute-start.2 = (bf16[256,128]{1,0:T(8,128)(2,1)S(1)}, bf16[256,128]{1,0:T(8,128)(2,1)S(1)}, u32[]{:S(2)}, u32[]{:S(2)}) collective-permute-start(bf16[256,128]{1,0:T(8,128)(2,1)S(1)} %shard_map.77.x_ref), channel_id=1, source_target_pairs={{0,24},{8,0},{16,8},{24,16},{1,25},{9,1},{17,9},{25,17},{2,26},{10... | collective-permute-start | bytes 196616 | tf_op jit(solution)/shard_map/ppermute | solution.py:213
  6.7 0.0 collective-permute-start.1
  6.7 1.0 %collective-permute-start = (bf16[256,128]{1,0:T(8,128)(2,1)S(1)}, bf16[256,128]{1,0:T(8,128)(2,1)S(1)}, u32[]{:S(2)}, u32[]{:S(2)}) collective-permute-start(bf16[256,128]{1,0:T(8,128)(2,1)S(1)} %shard_map.77.x_ref), channel_id=1, source_target_pairs={{0,8},{8,16},{16,24},{24,0},{1,9},{9,17},{17,25},{25,1},{2,10},{10... | collective-permute-start | bytes 196616 | tf_op jit(solution)/shard_map/ppermute | solution.py:213
  7.8 0.0 copy-start
  7.8 1.2 %copy-done = bf16[1,4,8,128,128]{4,3,2,1,0:T(8,128)(2,1)S(1)} copy-done((bf16[1,4,8,128,128]{4,3,2,1,0:T(8,128)(2,1)S(1)}, bf16[1,4,8,128,128]{4,3,2,1,0:T(8,128)(2,1)}, u32[]{:S(2)}) %copy-start) | copy-done | bytes 1048600
  9.0 0.0 copy-start.6
  9.0 0.7 %copy-done.6 = s32[1,4,8]{2,1,0:T(4,128)S(1)} copy-done((s32[1,4,8]{2,1,0:T(4,128)S(1)}, s32[1,4,8]{2,1,0:T(4,128)}, u32[]{:S(2)}) %copy-start.6) | copy-done | bytes 152
  9.7 0.0 copy-start.7
  9.7 0.7 %copy-done.7 = s32[1,4]{1,0:T(1,128)S(1)} copy-done((s32[1,4]{1,0:T(1,128)S(1)}, s32[1,4]{1,0:T(1,128)}, u32[]{:S(2)}) %copy-start.7) | copy-done | bytes 40
  10.3 0.0 copy-start.1
  10.3 1.2 %shard_map.78 = (f32[17,128,128]{2,1,0:T(8,128)S(1)}, f32[16,128]{1,0:T(8,128)S(1)}) custom-call(bf16[4,8,128,128]{3,2,1,0:T(8,128)(2,1)S(1)} %bitcast.2, s32[4,8]{1,0:T(4,128)S(1)} %bitcast.4, s32[1,4]{1,0:T(1,128)S(1)} %copy-done.7, bf16[256,128]{1,0:T(8,128)(2,1)S(1)} %shard_map.77.x_ref), custom_call_target="tpu_custom_call" | custom-call | flops 100000000 | bytes 3000000 | tf_op jit(solution)/shard_map/pallas_call | solution.py:219
  11.5 0.0 collective-permute-done.2.refs_7_
  11.5 1.7 %collective-permute-done.1.refs_6_ = bf16[256,128]{1,0:T(8,128)(2,1)S(1)} collective-permute-done((bf16[256,128]{1,0:T(8,128)(2,1)S(1)}, bf16[256,128]{1,0:T(8,128)(2,1)S(1)}, u32[]{:S(2)}, u32[]{:S(2)}) %collective-permute-start.1) | collective-permute-done | bytes 65568 | tf_op jit(solution)/shard_map/ppermute | solution.py:213
  13.2 0.0 collective-permute-done.refs_5_
  13.2 0.0 copy-done.1
  13.2 0.0 copy-start.3
  13.2 0.0 copy-start.4
  13.2 0.0 copy-start.5
  13.2 1.3 %shard_map.79 = (f32[264,128]{1,0:T(8,128)S(1)}, f32[264,128]{1,0:T(8,128)S(1)}, f32[264,128]{1,0:T(8,128)S(1)}, f32[264,128]{1,0:T(8,128)S(1)}) custom-call(bf16[4,8,128,128]{3,2,1,0:T(8,128)(2,1)S(1)} %bitcast.3, s32[4,8]{1,0:T(4,128)S(1)} %bitcast.5, s32[1,4]{1,0:T(1,128)S(1)} %copy-done.7, f32[17,128,128]{2,1,0:T(8,128)S(1)} %get-tuple-element.10.refs_3_, ...), custom_call_target="tpu_custom_call" | custom-call | tf_op jit(solution)/shard_map/pallas_call | solution.py:227
  14.5 1.5 %collective-permute-start.3 = (f32[264,128]{1,0:T(8,128)S(1)}, f32[264,128]{1,0:T(8,128)S(1)}, u32[]{:S(2)}, u32[]{:S(2)}) collective-permute-start(f32[264,128]{1,0:T(8,128)S(1)} %get-tuple-element.13), channel_id=1, source_target_pairs={{0,2},{2,4},{4,6},{6,0},{1,3},{3,5},{5,7},{7,1},{8,10},{10,12},{12... | collective-permute-start | bytes 405512 | tf_op jit(solution)/shard_map/ppermute | solution.py:234
  16.1 1.5 %collective-permute-start.4 = (f32[264,128]{1,0:T(8,128)S(1)}, f32[264,128]{1,0:T(8,128)S(1)}, u32[]{:S(2)}, u32[]{:S(2)}) collective-permute-start(f32[264,128]{1,0:T(8,128)S(1)} %get-tuple-element.14), channel_id=1, source_target_pairs={{0,4},{2,6},{4,0},{6,2},{1,5},{3,7},{5,1},{7,3},{8,12},{10,14},{12... | collective-permute-start | bytes 405512 | tf_op jit(solution)/shard_map/ppermute | solution.py:234
  17.6 1.4 %collective-permute-start.5 = (f32[264,128]{1,0:T(8,128)S(1)}, f32[264,128]{1,0:T(8,128)S(1)}, u32[]{:S(2)}, u32[]{:S(2)}) collective-permute-start(f32[264,128]{1,0:T(8,128)S(1)} %get-tuple-element.15), channel_id=1, source_target_pairs={{0,6},{2,0},{4,2},{6,4},{1,7},{3,1},{5,3},{7,5},{8,14},{10,8},{12,... | collective-permute-start | bytes 405512 | tf_op jit(solution)/shard_map/ppermute | solution.py:234
  19.0 2.9 %collective-permute-done.3.refs_1_ = f32[264,128]{1,0:T(8,128)S(1)} collective-permute-done((f32[264,128]{1,0:T(8,128)S(1)}, f32[264,128]{1,0:T(8,128)S(1)}, u32[]{:S(2)}, u32[]{:S(2)}) %collective-permute-start.3) | collective-permute-done | bytes 135200 | tf_op jit(solution)/shard_map/ppermute | solution.py:234
  22.0 1.7 %collective-permute-done.4.refs_2_ = f32[264,128]{1,0:T(8,128)S(1)} collective-permute-done((f32[264,128]{1,0:T(8,128)S(1)}, f32[264,128]{1,0:T(8,128)S(1)}, u32[]{:S(2)}, u32[]{:S(2)}) %collective-permute-start.4) | collective-permute-done | bytes 135200 | tf_op jit(solution)/shard_map/ppermute | solution.py:234
  23.7 0.1 collective-permute-done.5.refs_3_
  23.8 0.1 collective-permute-start.6
  23.9 1.3 %collective-permute-done.6.other_ref = f32[256,128]{1,0:T(8,128)S(1)} collective-permute-done((f32[256,128]{1,0:T(8,128)S(1)}, f32[256,128]{1,0:T(8,128)S(1)}, u32[]{:S(2)}, u32[]{:S(2)}) %collective-permute-start.6) | collective-permute-done | bytes 131104 | tf_op jit(solution)/shard_map/ppermute | solution.py:238
  25.2 0.0 copy-done.3
  25.2 0.0 copy-done.4
  25.3 0.0 copy-done.5
  25.3 1.1 %shard_map.81 = (bf16[512,128]{1,0:T(8,128)(2,1)}, f32[128,128]{1,0:T(8,128)S(1)}) custom-call(f32[264,128]{1,0:T(8,128)S(1)} %shard_map.80.mine_ref, f32[256,128]{1,0:T(8,128)S(1)} %collective-permute-done.6.other_ref, bf16[512,128]{1,0:T(8,128)(2,1)S(1)} %copy-done.3, bf16[128,128]{1,0:T(8,128)(2,1)S(1)} %copy-done.5, bf16[512,128]{1,0:T(8,128)(2,1)S(1)} %copy-done.4), custom_call_target="tpu_custom_call" | custom-call | tf_op jit(solution)/shard_map/pallas_call | solution.py:239
  26.3 1.7 %collective-permute-start.9 = (f32[128,128]{1,0:T(8,128)S(1)}, f32[128,128]{1,0:T(8,128)S(1)}, u32[]{:S(2)}, u32[]{:S(2)}) collective-permute-start(f32[128,128]{1,0:T(8,128)S(1)} %get-tuple-element.17.refs_0_), channel_id=1, source_target_pairs={{0,6},{2,0},{4,2},{6,4},{1,7},{3,1},{5,3},{7,5},{8,14},{10,8},{12,... | collective-permute-start | bytes 196616 | tf_op jit(solution)/shard_map/ppermute | solution.py:197
  28.0 1.5 %collective-permute-start.8 = (f32[128,128]{1,0:T(8,128)S(1)}, f32[128,128]{1,0:T(8,128)S(1)}, u32[]{:S(2)}, u32[]{:S(2)}) collective-permute-start(f32[128,128]{1,0:T(8,128)S(1)} %get-tuple-element.17.refs_0_), channel_id=1, source_target_pairs={{0,4},{2,6},{4,0},{6,2},{1,5},{3,7},{5,1},{7,3},{8,12},{10,14},{12... | collective-permute-start | bytes 196616 | tf_op jit(solution)/shard_map/ppermute | solution.py:197
  29.6 0.3 collective-permute-start.7
  29.8 0.8 %collective-permute-done.9.refs_3_ = f32[128,128]{1,0:T(8,128)S(1)} collective-permute-done((f32[128,128]{1,0:T(8,128)S(1)}, f32[128,128]{1,0:T(8,128)S(1)}, u32[]{:S(2)}, u32[]{:S(2)}) %collective-permute-start.9) | collective-permute-done | bytes 65568 | tf_op jit(solution)/shard_map/ppermute | solution.py:197
  30.6 1.7 %collective-permute-done.8.refs_2_ = f32[128,128]{1,0:T(8,128)S(1)} collective-permute-done((f32[128,128]{1,0:T(8,128)S(1)}, f32[128,128]{1,0:T(8,128)S(1)}, u32[]{:S(2)}, u32[]{:S(2)}) %collective-permute-start.8) | collective-permute-done | bytes 65568 | tf_op jit(solution)/shard_map/ppermute | solution.py:197
  32.3 2.4 %collective-permute-done.7.refs_1_ = f32[128,128]{1,0:T(8,128)S(1)} collective-permute-done((f32[128,128]{1,0:T(8,128)S(1)}, f32[128,128]{1,0:T(8,128)S(1)}, u32[]{:S(2)}, u32[]{:S(2)}) %collective-permute-start.7) | collective-permute-done | bytes 65568 | tf_op jit(solution)/shard_map/ppermute | solution.py:197
  34.7 0.7 %collective-permute-start.12 = (f32[128,128]{1,0:T(8,128)S(1)}, f32[128,128]{1,0:T(8,128)S(1)}, u32[]{:S(2)}, u32[]{:S(2)}) collective-permute-start(f32[128,128]{1,0:T(8,128)S(1)} %shard_map.82.refs_0_), channel_id=1, source_target_pairs={{0,24},{8,0},{16,8},{24,16},{1,25},{9,1},{17,9},{25,17},{2,26},{10... | collective-permute-start | bytes 196616 | tf_op jit(solution)/shard_map/ppermute | solution.py:197
  35.4 0.9 %collective-permute-start.11 = (f32[128,128]{1,0:T(8,128)S(1)}, f32[128,128]{1,0:T(8,128)S(1)}, u32[]{:S(2)}, u32[]{:S(2)}) collective-permute-start(f32[128,128]{1,0:T(8,128)S(1)} %shard_map.82.refs_0_), channel_id=1, source_target_pairs={{0,16},{8,24},{16,0},{24,8},{1,17},{9,25},{17,1},{25,9},{2,18},{10... | collective-permute-start | bytes 196616 | tf_op jit(solution)/shard_map/ppermute | solution.py:197
  36.3 1.9 %collective-permute-start.10 = (f32[128,128]{1,0:T(8,128)S(1)}, f32[128,128]{1,0:T(8,128)S(1)}, u32[]{:S(2)}, u32[]{:S(2)}) collective-permute-start(f32[128,128]{1,0:T(8,128)S(1)} %shard_map.82.refs_0_), channel_id=1, source_target_pairs={{0,8},{8,16},{16,24},{24,0},{1,9},{9,17},{17,25},{25,1},{2,10},{10... | collective-permute-start | bytes 196616 | tf_op jit(solution)/shard_map/ppermute | solution.py:197
  38.2 1.3 %collective-permute-done.12.refs_3_ = f32[128,128]{1,0:T(8,128)S(1)} collective-permute-done((f32[128,128]{1,0:T(8,128)S(1)}, f32[128,128]{1,0:T(8,128)S(1)}, u32[]{:S(2)}, u32[]{:S(2)}) %collective-permute-start.12) | collective-permute-done | bytes 65568 | tf_op jit(solution)/shard_map/ppermute | solution.py:197
  39.6 1.1 %collective-permute-done.11.refs_2_ = f32[128,128]{1,0:T(8,128)S(1)} collective-permute-done((f32[128,128]{1,0:T(8,128)S(1)}, f32[128,128]{1,0:T(8,128)S(1)}, u32[]{:S(2)}, u32[]{:S(2)}) %collective-permute-start.11) | collective-permute-done | bytes 65568 | tf_op jit(solution)/shard_map/ppermute | solution.py:197
  40.7 1.7 %collective-permute-done.10.refs_1_ = f32[128,128]{1,0:T(8,128)S(1)} collective-permute-done((f32[128,128]{1,0:T(8,128)S(1)}, f32[128,128]{1,0:T(8,128)S(1)}, u32[]{:S(2)}, u32[]{:S(2)}) %collective-permute-start.10) | collective-permute-done | bytes 65568 | tf_op jit(solution)/shard_map/ppermute | solution.py:197
  42.4 0.6 %shard_map.83 = f32[128,128]{1,0:T(8,128)} custom-call(f32[128,128]{1,0:T(8,128)S(1)} %shard_map.82.refs_0_, f32[128,128]{1,0:T(8,128)S(1)} %collective-permute-done.10.refs_1_, f32[128,128]{1,0:T(8,128)S(1)} %collective-permute-done.11.refs_2_, f32[128,128]{1,0:T(8,128)S(1)} %collective-permute-done.12.refs_3_), custom_call_target="tpu_custom_call" | custom-call | tf_op jit(solution)/shard_map/pallas_call | solution.py:198
  (3 shorter events, 0.1 us)
Async XLA Ops:
  0.6 0.9 %copy-start.2 = (bf16[512,128]{1,0:T(8,128)(2,1)S(1)}, bf16[512,128]{1,0:T(8,128)(2,1)}, u32[]{:S(2)}) copy-start(bf16[512,128]{1,0:T(8,128)(2,1)} %x_ref.3) | copy-start | bytes 393220
  1.6 9.9 %collective-permute-start.2 = (bf16[256,128]{1,0:T(8,128)(2,1)S(1)}, bf16[256,128]{1,0:T(8,128)(2,1)S(1)}, u32[]{:S(2)}, u32[]{:S(2)}) collective-permute-start(bf16[256,128]{1,0:T(8,128)(2,1)S(1)} %shard_map.77.x_ref), channel_id=1, source_target_pairs={{0,24},{8,0},{16,8},{24,16},{1,25},{9,1},{17,9},{25,17},{2,26},{10... | collective-permute-start | bytes 196616 | tf_op jit(solution)/shard_map/ppermute | solution.py:213
  6.7 6.5 %collective-permute-start.1 = (bf16[256,128]{1,0:T(8,128)(2,1)S(1)}, bf16[256,128]{1,0:T(8,128)(2,1)S(1)}, u32[]{:S(2)}, u32[]{:S(2)}) collective-permute-start(bf16[256,128]{1,0:T(8,128)(2,1)S(1)} %shard_map.77.x_ref), channel_id=1, source_target_pairs={{0,16},{8,24},{16,0},{24,8},{1,17},{9,25},{17,1},{25,9},{2,18},{10... | collective-permute-start | bytes 196616 | tf_op jit(solution)/shard_map/ppermute | solution.py:213
  6.7 6.5 %collective-permute-start = (bf16[256,128]{1,0:T(8,128)(2,1)S(1)}, bf16[256,128]{1,0:T(8,128)(2,1)S(1)}, u32[]{:S(2)}, u32[]{:S(2)}) collective-permute-start(bf16[256,128]{1,0:T(8,128)(2,1)S(1)} %shard_map.77.x_ref), channel_id=1, source_target_pairs={{0,8},{8,16},{16,24},{24,0},{1,9},{9,17},{17,25},{25,1},{2,10},{10... | collective-permute-start | bytes 196616 | tf_op jit(solution)/shard_map/ppermute | solution.py:213
  7.8 1.2 %copy-start = (bf16[1,4,8,128,128]{4,3,2,1,0:T(8,128)(2,1)S(1)}, bf16[1,4,8,128,128]{4,3,2,1,0:T(8,128)(2,1)}, u32[]{:S(2)}) copy-start(bf16[1,4,8,128,128]{4,3,2,1,0:T(8,128)(2,1)} %param.10) | copy-start | bytes 3145732
  9.0 0.7 %copy-start.6 = (s32[1,4,8]{2,1,0:T(4,128)S(1)}, s32[1,4,8]{2,1,0:T(4,128)}, u32[]{:S(2)}) copy-start(s32[1,4,8]{2,1,0:T(4,128)} %param.8) | copy-start | bytes 388
  9.7 0.7 %copy-start.7 = (s32[1,4]{1,0:T(1,128)S(1)}, s32[1,4]{1,0:T(1,128)}, u32[]{:S(2)}) copy-start(s32[1,4]{1,0:T(1,128)} %refs_2_.1) | copy-start | bytes 52
  10.3 2.9 %copy-start.1 = (bf16[1,4,8,128,128]{4,3,2,1,0:T(8,128)(2,1)S(1)}, bf16[1,4,8,128,128]{4,3,2,1,0:T(8,128)(2,1)}, u32[]{:S(2)}) copy-start(bf16[1,4,8,128,128]{4,3,2,1,0:T(8,128)(2,1)} %param.10) | copy-start | bytes 3145732
  13.2 12.0 %copy-start.3 = (bf16[512,128]{1,0:T(8,128)(2,1)S(1)}, bf16[512,128]{1,0:T(8,128)(2,1)}, u32[]{:S(2)}) copy-start(bf16[512,128]{1,0:T(8,128)(2,1)} %x_ref.3) | copy-start | bytes 393220
  13.2 12.0 %copy-start.4 = (bf16[512,128]{1,0:T(8,128)(2,1)S(1)}, bf16[512,128]{1,0:T(8,128)(2,1)}, u32[]{:S(2)}) copy-start(bf16[512,128]{1,0:T(8,128)(2,1)} %cot_ref.1) | copy-start | bytes 393220
  13.2 12.0 %copy-start.5 = (bf16[128,128]{1,0:T(8,128)(2,1)S(1)}, bf16[128,128]{1,0:T(8,128)(2,1)}, u32[]{:S(2)}) copy-start(bf16[128,128]{1,0:T(8,128)(2,1)} %w_ref.1) | copy-start | bytes 98308
  14.5 7.4 %collective-permute-start.3 = (f32[264,128]{1,0:T(8,128)S(1)}, f32[264,128]{1,0:T(8,128)S(1)}, u32[]{:S(2)}, u32[]{:S(2)}) collective-permute-start(f32[264,128]{1,0:T(8,128)S(1)} %get-tuple-element.13), channel_id=1, source_target_pairs={{0,2},{2,4},{4,6},{6,0},{1,3},{3,5},{5,7},{7,1},{8,10},{10,12},{12... | collective-permute-start | bytes 405512 | tf_op jit(solution)/shard_map/ppermute | solution.py:234
  16.1 7.6 %collective-permute-start.4 = (f32[264,128]{1,0:T(8,128)S(1)}, f32[264,128]{1,0:T(8,128)S(1)}, u32[]{:S(2)}, u32[]{:S(2)}) collective-permute-start(f32[264,128]{1,0:T(8,128)S(1)} %get-tuple-element.14), channel_id=1, source_target_pairs={{0,4},{2,6},{4,0},{6,2},{1,5},{3,7},{5,1},{7,3},{8,12},{10,14},{12... | collective-permute-start | bytes 405512 | tf_op jit(solution)/shard_map/ppermute | solution.py:234
  17.6 6.2 %collective-permute-start.5 = (f32[264,128]{1,0:T(8,128)S(1)}, f32[264,128]{1,0:T(8,128)S(1)}, u32[]{:S(2)}, u32[]{:S(2)}) collective-permute-start(f32[264,128]{1,0:T(8,128)S(1)} %get-tuple-element.15), channel_id=1, source_target_pairs={{0,6},{2,0},{4,2},{6,4},{1,7},{3,1},{5,3},{7,5},{8,14},{10,8},{12,... | collective-permute-start | bytes 405512 | tf_op jit(solution)/shard_map/ppermute | solution.py:234
  23.8 1.4 %collective-permute-start.6 = (f32[256,128]{1,0:T(8,128)S(1)}, f32[256,128]{1,0:T(8,128)S(1)}, u32[]{:S(2)}, u32[]{:S(2)}) collective-permute-start(f32[256,128]{1,0:T(8,128)S(1)} %slice.4), channel_id=1, source_target_pairs={{0,1},{1,0},{2,3},{3,2},{4,5},{5,4},{6,7},{7,6},{8,9},{9,8},{10,11... | collective-permute-start | bytes 393224 | tf_op jit(solution)/shard_map/ppermute | solution.py:238
  26.3 4.3 %collective-permute-start.9 = (f32[128,128]{1,0:T(8,128)S(1)}, f32[128,128]{1,0:T(8,128)S(1)}, u32[]{:S(2)}, u32[]{:S(2)}) collective-permute-start(f32[128,128]{1,0:T(8,128)S(1)} %get-tuple-element.17.refs_0_), channel_id=1, source_target_pairs={{0,6},{2,0},{4,2},{6,4},{1,7},{3,1},{5,3},{7,5},{8,14},{10,8},{12,... | collective-permute-start | bytes 196616 | tf_op jit(solution)/shard_map/ppermute | solution.py:197
  28.0 4.3 %collective-permute-start.8 = (f32[128,128]{1,0:T(8,128)S(1)}, f32[128,128]{1,0:T(8,128)S(1)}, u32[]{:S(2)}, u32[]{:S(2)}) collective-permute-start(f32[128,128]{1,0:T(8,128)S(1)} %get-tuple-element.17.refs_0_), channel_id=1, source_target_pairs={{0,4},{2,6},{4,0},{6,2},{1,5},{3,7},{5,1},{7,3},{8,12},{10,14},{12... | collective-permute-start | bytes 196616 | tf_op jit(solution)/shard_map/ppermute | solution.py:197
  29.6 5.2 %collective-permute-start.7 = (f32[128,128]{1,0:T(8,128)S(1)}, f32[128,128]{1,0:T(8,128)S(1)}, u32[]{:S(2)}, u32[]{:S(2)}) collective-permute-start(f32[128,128]{1,0:T(8,128)S(1)} %get-tuple-element.17.refs_0_), channel_id=1, source_target_pairs={{0,2},{2,4},{4,6},{6,0},{1,3},{3,5},{5,7},{7,1},{8,10},{10,12},{12... | collective-permute-start | bytes 196616 | tf_op jit(solution)/shard_map/ppermute | solution.py:197
  34.7 4.8 %collective-permute-start.12 = (f32[128,128]{1,0:T(8,128)S(1)}, f32[128,128]{1,0:T(8,128)S(1)}, u32[]{:S(2)}, u32[]{:S(2)}) collective-permute-start(f32[128,128]{1,0:T(8,128)S(1)} %shard_map.82.refs_0_), channel_id=1, source_target_pairs={{0,24},{8,0},{16,8},{24,16},{1,25},{9,1},{17,9},{25,17},{2,26},{10... | collective-permute-start | bytes 196616 | tf_op jit(solution)/shard_map/ppermute | solution.py:197
  35.4 5.3 %collective-permute-start.11 = (f32[128,128]{1,0:T(8,128)S(1)}, f32[128,128]{1,0:T(8,128)S(1)}, u32[]{:S(2)}, u32[]{:S(2)}) collective-permute-start(f32[128,128]{1,0:T(8,128)S(1)} %shard_map.82.refs_0_), channel_id=1, source_target_pairs={{0,16},{8,24},{16,0},{24,8},{1,17},{9,25},{17,1},{25,9},{2,18},{10... | collective-permute-start | bytes 196616 | tf_op jit(solution)/shard_map/ppermute | solution.py:197
  36.3 6.1 %collective-permute-start.10 = (f32[128,128]{1,0:T(8,128)S(1)}, f32[128,128]{1,0:T(8,128)S(1)}, u32[]{:S(2)}, u32[]{:S(2)}) collective-permute-start(f32[128,128]{1,0:T(8,128)S(1)} %shard_map.82.refs_0_), channel_id=1, source_target_pairs={{0,8},{8,16},{16,24},{24,0},{1,9},{9,17},{17,25},{25,1},{2,10},{10... | collective-permute-start | bytes 196616 | tf_op jit(solution)/shard_map/ppermute | solution.py:197

commit v2 on v1

--- a/solution.py
+++ b/solution.py
@@ -10,14 +10,11 @@
 f32 = jnp.float32
 bf16 = jnp.bfloat16
 LONGEST = 8
+ORDER = (0, 3, 2, 1)
 
 
 def vmem(n):
     return [pl.BlockSpec(memory_space=pltpu.VMEM)] * n
-
-
-def smem(n):
-    return [pl.BlockSpec(memory_space=pltpu.SMEM)] * n
 
 
 def lower_half(shape):
@@ -37,23 +34,27 @@
     out_ref[...] = jnp.where(left == first, kept, moved).astype(bf16)
 
 
-def spread(block_ref, at, sources_ref, tile):
-    half = block_ref.shape[0] if at is None else block_ref.shape[1]
-    x = (block_ref[...] if at is None else block_ref[at]).astype(f32)
+def spread(x, sources_ref, tile):
+    x = x.astype(f32)
     left = lower_half(x.shape)
     top = jnp.where(left, x, 0.0).astype(bf16)
     low = jnp.where(left, pltpu.roll(x, x.shape[1] // 2, 1), 0.0).astype(bf16)
-    n = half // tile
+    n = x.shape[0] // tile
     for c in range(n):
         sources_ref[c] = top[c * tile : (c + 1) * tile]
         sources_ref[n + c] = low[c * tile : (c + 1) * tile]
 
 
-def add_tiles(j, tiles_ref, pos_ref, count_ref, sources_ref, acc_ref, col_tiles):
+def add_tiles(j, tiles_ref, pos_ref, count_ref, sources_ref, acc_ref):
+    col_tiles = sources_ref.shape[0]
     spare = acc_ref.shape[0] - 1
+    listed = pos_ref[pl.ds(j, 1)]
+    live = jnp.sum(
+        jnp.where(lax.broadcasted_iota(jnp.int32, count_ref.shape, 1) == j, count_ref[...], 0)
+    )
     for p in range(tiles_ref.shape[1]):
-        t = pos_ref[j, p]
-        i = jnp.where(p < count_ref[0, j], t // col_tiles, spare)
+        t = listed[0, p]
+        i = jnp.where(p < live, t // col_tiles, spare)
         acc_ref[i] += jnp.dot(
             tiles_ref[j, p], sources_ref[t % col_tiles], preferred_element_type=f32
         )
@@ -64,16 +65,18 @@
     col_tiles = sources_ref.shape[0]
     row_tiles = acc_ref.shape[0] - 1
     acc_ref[...] = jnp.zeros_like(acc_ref)
-    spread(x_ref, None, sources_ref, tile)
-    add_tiles(
-        lax.axis_index("row"), tiles_ref, pos_ref, count_ref, sources_ref, acc_ref, col_tiles
-    )
+    spread(x_ref[...], sources_ref, tile)
+    add_tiles(lax.axis_index("row"), tiles_ref, pos_ref, count_ref, sources_ref, acc_ref)
     lane = lax.broadcasted_iota(jnp.int32, (tile, 128), 1)
 
+    slot = lax.broadcasted_iota(jnp.int32, (1, slots), 1)
+    owner = lax.broadcasted_iota(jnp.int32, count_ref.shape, 1)
+
     def sums_of(j, total):
+        live = jnp.sum(jnp.where(owner == j, count_ref[...], 0), axis=1, keepdims=True)
+        rows = jnp.where(slot < live, pos_ref[pl.ds(j, 1)] // col_tiles, -1)
         for p in range(slots):
-            i = jnp.where(p < count_ref[0, j], pos_ref[j, p] // col_tiles, -1)
-            mark = (lane == i).astype(f32).astype(bf16)
+            mark = (lane == rows[:, p : p + 1]).astype(f32).astype(bf16)
             total = total + jnp.dot(tiles_ref[j, p], mark, preferred_element_type=f32)
         return total
 
@@ -86,43 +89,56 @@
     deg_ref[...] = total.T[:row_tiles]
 
 
-def fold_kernel(n_blocks, *refs):
-    tiles_ref, pos_ref, count_ref, start_ref, deg_ref = refs[:5]
-    blocks = refs[5 : 5 + n_blocks]
-    outs = refs[5 + n_blocks : -2]
-    acc_ref, sources_ref = refs[-2:]
-    n_own, slots, tile, _ = tiles_ref.shape
-    col_tiles = sources_ref.shape[0]
+def fold_kernel(step, tiles_ref, pos_ref, count_ref, block_ref, start_ref, acc_ref, sources_ref):
+    tile = tiles_ref.shape[2]
+    spread(block_ref[...], sources_ref, tile)
+    j = sender(step, lax.axis_index("row"))
+    add_tiles(j, tiles_ref, pos_ref, count_ref, sources_ref, acc_ref)
+
+
+def fold_all_kernel(tiles_ref, pos_ref, count_ref, blocks_ref, start_ref, acc_ref, sources_ref):
+    n_own, _, tile, _ = tiles_ref.shape
     me = lax.axis_index("row")
+
+    @pl.loop(1, n_own)
+    def _(k):
+        j = lax.rem(me + k, n_own)
+        spread(blocks_ref[j], sources_ref, tile)
+        add_tiles(j, tiles_ref, pos_ref, count_ref, sources_ref, acc_ref)
+
+
+def send_kernel(acc_ref, deg_ref, *outs):
+    tile, width = acc_ref.shape[1:]
+    row_tiles = acc_ref.shape[0] - 1
     rep = lax.axis_index("rep")
-    acc_ref[...] = start_ref[...]
-    if n_blocks == n_own - 1:
-        for k, block in enumerate(blocks):
-            j = lax.rem(me + n_own - 1 - k, n_own)
-            spread(block, None, sources_ref, tile)
-            add_tiles(j, tiles_ref, pos_ref, count_ref, sources_ref, acc_ref, col_tiles)
-    else:
-
-        @pl.loop(1, n_own)
-        def _(k):
-            j = lax.rem(me + k, n_own)
-            spread(blocks[0], j, sources_ref, tile)
-            add_tiles(j, tiles_ref, pos_ref, count_ref, sources_ref, acc_ref, col_tiles)
-
     n_rep = len(outs)
+    col_tiles = row_tiles // n_rep
+    n = col_tiles // 2
+    left = lower_half((tile, width))
     for k, out in enumerate(outs):
-        q = lax.rem(rep + k, n_rep)
-        n = col_tiles // 2
+        q = rep ^ ORDER[k] if n_rep == 4 else lax.rem(rep + k, n_rep)
         for c in range(n):
             top = acc_ref[q * col_tiles + c]
             low = acc_ref[q * col_tiles + n + c]
-            out[c * tile : (c + 1) * tile] = jnp.where(
-                lower_half(top.shape), top, pltpu.roll(low, top.shape[1] // 2, 1)
-            )
+            out[c * tile : (c + 1) * tile] = jnp.where(left, top, pltpu.roll(low, width // 2, 1))
         rows = out.shape[0] - n * tile
-        out[n * tile :] = jnp.zeros((rows, out.shape[1]), f32)
+        out[n * tile :] = jnp.zeros((rows, width), f32)
         for c in range(col_tiles):
             out[n * tile + c : n * tile + c + 1] = deg_ref[pl.ds(q * col_tiles + c, 1)]
+
+
+def last_kernel(step, *refs):
+    acc_ref, sources_ref = refs[-2:]
+    tiles_ref, pos_ref, count_ref, block_ref, start_ref, deg_ref = refs[:6]
+    acc_ref[...] = start_ref[...]
+    spread(block_ref[...], sources_ref, tiles_ref.shape[2])
+    j = sender(step, lax.axis_index("row"))
+    add_tiles(j, tiles_ref, pos_ref, count_ref, sources_ref, acc_ref)
+    send_kernel(acc_ref, deg_ref, *refs[6:-2])
+
+
+def copy_kernel(x_ref, out_ref):
+    out_ref[...] = x_ref[...]
 
 
 def sum_kernel(*refs):
@@ -178,7 +194,7 @@
     return jax.ShapeDtypeStruct(dims, dtype)
 
 
-def call(kernel, outs, in_specs, scratch=(), cost=None):
+def call(kernel, outs, in_specs, scratch=(), cost=None, aliases=None):
     return pl.pallas_call(
         kernel,
         out_shape=outs,
@@ -187,14 +203,32 @@
         scratch_shapes=list(scratch),
         compiler_params=pltpu.CompilerParams(vmem_limit_bytes=48 * 1024 * 1024),
         cost_estimate=cost,
-    )
+        input_output_aliases=aliases or {},
+    )
+
+
+def pairs(n, k):
+    return [(i, i ^ k) for i in range(n)]
+
+
+def steps(n):
+    if n == 4:
+        return [(2, 3, 1, 0), (3, 2, 0, 1), (1, 0, 3, 2)]
+    return [tuple(i ^ k for i in range(n)) for k in range(n - 1, 0, -1)]
+
+
+def sender(step, me):
+    j = jnp.int32(0)
+    for i, target in enumerate(step):
+        j = jnp.where(me == target, i, j)
+    return j
 
 
 def total_over(x, axis):
     n = lax.axis_size(axis)
     if n > LONGEST:
         return lax.psum(x, axis)
-    parts = [lax.ppermute(x, axis, [(i, (i + k) % n) for i in range(n)]) for k in range(1, n)]
+    parts = [lax.ppermute(x, axis, pairs(n, k)) for k in range(n - 1, 0, -1)]
     return call(sum_kernel, shape(*x.shape), vmem(n))(x, *parts)
 
 
@@ -207,42 +241,66 @@
     row_tiles = n_rep * col_tiles
     pos, counts, tiles = pair_tiles[0], pair_count, tile_vals[0]
 
-    packed = call(pack_kernel, shape(half, width, dtype=bf16), vmem(1))(features)
+    packed = call(
+        pack_kernel,
+        shape(half, width, dtype=bf16),
+        vmem(1),
+        cost=pl.CostEstimate(flops=0, bytes_accessed=10**7, transcendentals=0),
+    )(features)
     if n_own <= LONGEST:
         blocks = [
-            lax.ppermute(packed, "row", [(i, (i + k) % n_own) for i in range(n_own)])
-            for k in range(1, n_own)
+            lax.ppermute(packed, "row", list(enumerate(step))) for step in steps(n_own)
         ]
     else:
         blocks = [lax.all_gather(packed, "row")]
     sources = pltpu.VMEM((col_tiles, tile, width), bf16)
-    start, degrees = call(
+    lists = vmem(3)
+    cost = pl.CostEstimate(flops=10**8, bytes_accessed=3 * 10**6, transcendentals=0)
+    total_shape = shape(row_tiles + 1, tile, width)
+    total, degrees = call(
         own_kernel,
-        [shape(row_tiles + 1, tile, width), shape(row_tiles, tile)],
-        vmem(1) + smem(2) + vmem(1),
+        [total_shape, shape(row_tiles, tile)],
+        lists + vmem(1),
         [sources],
-        pl.CostEstimate(flops=10**8, bytes_accessed=3 * 10**6, transcendentals=0),
+        cost,
     )(tiles, pos, counts, packed)
-    message = shape(half + 8, width)
-    mine, *sends = call(
-        functools.partial(fold_kernel, len(blocks)),
-        [message] * n_rep,
-        vmem(1) + smem(2) + vmem(2 + len(blocks)),
-        [pltpu.VMEM((row_tiles + 1, tile, width), f32), sources],
-    )(tiles, pos, counts, start, degrees, *blocks)
+    messages = [shape(half + 8, width)] * n_rep
+    if n_own <= LONGEST:
+        for step, block in zip(steps(n_own)[:-1], blocks):
+            total = call(
+                functools.partial(fold_kernel, step),
+                total_shape,
+                lists + vmem(2),
+                [sources],
+                cost,
+                {4: 0},
+            )(tiles, pos, counts, block, total)
+        mine, *sends = call(
+            functools.partial(last_kernel, steps(n_own)[-1]),
+            messages,
+            lists + vmem(3),
+            [pltpu.VMEM(total_shape.shape, f32), sources],
+        )(tiles, pos, counts, blocks[-1], total, degrees)
+    else:
+        total = call(fold_all_kernel, total_shape, lists + vmem(2), [sources], cost, {4: 0})(
+            tiles, pos, counts, blocks[0], total
+        )
+        mine, *sends = call(send_kernel, messages, vmem(2))(total, degrees)
     parts = [
-        lax.ppermute(sent, "rep", [(i, (i + k + 1) % n_rep) for i in range(n_rep)])
+        lax.ppermute(sent, "rep", pairs(n_rep, ORDER[k + 1]))
         for k, sent in enumerate(sends)
     ]
-    mine = call(sum_kernel, message, vmem(n_rep))(mine, *parts)
+    mine = call(sum_kernel, messages[0], vmem(n_rep))(mine, *parts)
     other = lax.ppermute(mine[:half], "feat", [(0, 1), (1, 0)])
+    activated_shape = shape(rows, weight.shape[1], dtype=bf16)
     activated, grad = call(
         layer_kernel,
-        [shape(rows, weight.shape[1], dtype=bf16), shape(width, weight.shape[1])],
+        [activated_shape, shape(width, weight.shape[1])],
         vmem(5),
     )(mine, other, features, weight, cotangent)
     grad = total_over(grad, "rep")
     grad = total_over(grad, "row")
+    activated = call(copy_kernel, activated_shape, vmem(1))(activated)
     return activated, grad
 
 

time: 43.2 us -> 41.1 us (0.951)
  waiting for transfers between devices: 16.8 us -> 14.6 us
  local copies, waits for them, and re-layouts: 3.49 us -> 3.95 us
    ppermute x12, waiting for transfers between devices: 15.4 us -> 13.3 us  [the longest x6 7.56 us: total_over(): parts = [lax.ppermute(x, axis, pairs(n, k)) for k in range(n - 1, 0, -1)]]
    unnamed x16, local copies, waits for them, and re-layouts: 3.48 us -> 3.94 us
    pallas_call x5 -> x8, Pallas kernels: 3.72 us -> 3.59 us  [the longest x1 0.76 us: shards(): call(own_kernel, [total_shape, shape(row_tiles, tile)], lists + vmem(1),...]
  transfers between devices with their start and end apart: 13 -> 13, of which waited for: 11 -> 10; matrix products, arithmetic and copies ran while one was open for 0% -> 0% of each run, Pallas kernels for 3% -> 5%
where the time goes in v2:
time: 41.1 us; the launch traced here: 40.9 us
  starting transfers between devices  17.3 us (42%)
  waiting for transfers between devices  14.6 us (36%)
  Pallas kernels  4.25 us (10%)
  local copies, waits for them, and re-layouts  3.95 us (10%)
  between operations  0.74 us (2%)
    ppermute x6, starting transfers between devices, total_over(): parts = [lax.ppermute(x, axis, pairs(n, k)) for k in range(n - 1, 0, -1)]  8.01 us
    ppermute x6, waiting for transfers between devices, total_over(): parts = [lax.ppermute(x, axis, pairs(n, k)) for k in range(n - 1, 0, -1)]  7.56 us
    ppermute x3, starting transfers between devices, shards(): lax.ppermute(packed, 'row', list(enumerate(step)))  5.67 us
    ppermute x3, waiting for transfers between devices, shards(): lax.ppermute(sent, 'rep', pairs(n_rep, ORDER[k + 1]))  4.87 us
    unnamed x16, local copies, waits for them, and re-layouts  3.94 us
    ppermute x3, starting transfers between devices, shards(): lax.ppermute(sent, 'rep', pairs(n_rep, ORDER[k + 1]))  3.55 us
    ppermute x1, waiting for transfers between devices, shards(): other = lax.ppermute(mine[:half], 'feat', [(0, 1), (1, 0)])  1.33 us
    ppermute x3, waiting for transfers between devices, shards(): lax.ppermute(packed, 'row', list(enumerate(step)))  0.87 us
  transfers between devices with their start and end apart: 13, of which 10 were waited for; matrix products, arithmetic and copies ran while one was open for 0% of the time, Pallas kernels for 5%

profile of v2, /device:TPU:0, one launch (start us, length us, event | category | flops | bytes accessed | tf_op | source)
XLA Modules:
  0.0 40.9 jit_solution(2865953106681466397)
XLA Ops:
  0.6 0.0 copy-start.2
  0.6 0.9 %copy-done.2 = bf16[512,128]{1,0:T(8,128)(2,1)S(1)} copy-done((bf16[512,128]{1,0:T(8,128)(2,1)S(1)}, bf16[512,128]{1,0:T(8,128)(2,1)}, u32[]{:S(2)}) %copy-start.2) | copy-done | bytes 131096
  1.5 0.1 shard_map.77.x_ref
  1.6 4.1 %collective-permute-start.2 = (bf16[256,128]{1,0:T(8,128)(2,1)S(1)}, bf16[256,128]{1,0:T(8,128)(2,1)S(1)}, u32[]{:S(2)}, u32[]{:S(2)}) collective-permute-start(bf16[256,128]{1,0:T(8,128)(2,1)S(1)} %shard_map.77.x_ref), channel_id=1, source_target_pairs={{0,16},{8,24},{16,8},{24,0},{1,17},{9,25},{17,9},{25,1},{2,18},{10... | collective-permute-start | bytes 196616 | tf_op jit(solution)/shard_map/ppermute | solution.py:252
  5.7 1.1 %collective-permute-start.1 = (bf16[256,128]{1,0:T(8,128)(2,1)S(1)}, bf16[256,128]{1,0:T(8,128)(2,1)S(1)}, u32[]{:S(2)}, u32[]{:S(2)}) collective-permute-start(bf16[256,128]{1,0:T(8,128)(2,1)S(1)} %shard_map.77.x_ref), channel_id=1, source_target_pairs={{0,24},{8,16},{16,0},{24,8},{1,25},{9,17},{17,1},{25,9},{2,26},{10... | collective-permute-start | bytes 196616 | tf_op jit(solution)/shard_map/ppermute | solution.py:252
  6.8 0.5 %collective-permute-start = (bf16[256,128]{1,0:T(8,128)(2,1)S(1)}, bf16[256,128]{1,0:T(8,128)(2,1)S(1)}, u32[]{:S(2)}, u32[]{:S(2)}) collective-permute-start(bf16[256,128]{1,0:T(8,128)(2,1)S(1)} %shard_map.77.x_ref), channel_id=1, source_target_pairs={{0,8},{8,0},{16,24},{24,16},{1,9},{9,1},{17,25},{25,17},{2,10},{10... | collective-permute-start | bytes 196616 | tf_op jit(solution)/shard_map/ppermute | solution.py:252
  7.3 0.0 copy-start
  7.3 1.2 %copy-done = bf16[1,4,8,128,128]{4,3,2,1,0:T(8,128)(2,1)S(1)} copy-done((bf16[1,4,8,128,128]{4,3,2,1,0:T(8,128)(2,1)S(1)}, bf16[1,4,8,128,128]{4,3,2,1,0:T(8,128)(2,1)}, u32[]{:S(2)}) %copy-start) | copy-done | bytes 1048600
  8.5 0.0 copy-start.6
  8.5 0.7 %copy-done.6 = s32[1,4,8]{2,1,0:T(4,128)S(1)} copy-done((s32[1,4,8]{2,1,0:T(4,128)S(1)}, s32[1,4,8]{2,1,0:T(4,128)}, u32[]{:S(2)}) %copy-start.6) | copy-done | bytes 152
  9.2 0.0 copy-start.7
  9.2 0.7 %copy-done.7 = s32[1,4]{1,0:T(1,128)S(1)} copy-done((s32[1,4]{1,0:T(1,128)S(1)}, s32[1,4]{1,0:T(1,128)}, u32[]{:S(2)}) %copy-start.7) | copy-done | bytes 40
  9.9 0.0 copy-start.1
  9.9 0.8 %shard_map.78 = (f32[17,128,128]{2,1,0:T(8,128)S(1)}, f32[16,128]{1,0:T(8,128)S(1)}) custom-call(bf16[4,8,128,128]{3,2,1,0:T(8,128)(2,1)S(1)} %bitcast.2, s32[4,8]{1,0:T(4,128)S(1)} %bitcast.6, s32[1,4]{1,0:T(1,128)S(1)} %copy-done.7, bf16[256,128]{1,0:T(8,128)(2,1)S(1)} %shard_map.77.x_ref), custom_call_target="tpu_custom_call" | custom-call | flops 100000000 | bytes 3000000 | tf_op jit(solution)/shard_map/pallas_call | solution.py:260
  10.6 0.0 collective-permute-done.2.block_ref
  10.6 0.5 %copy-done.1 = bf16[1,4,8,128,128]{4,3,2,1,0:T(8,128)(2,1)S(1)} copy-done((bf16[1,4,8,128,128]{4,3,2,1,0:T(8,128)(2,1)S(1)}, bf16[1,4,8,128,128]{4,3,2,1,0:T(8,128)(2,1)}, u32[]{:S(2)}) %copy-start.1) | copy-done | bytes 1048600
  11.1 0.4 shard_map.79.start_ref
  11.5 0.9 %collective-permute-done.1.block_ref = bf16[256,128]{1,0:T(8,128)(2,1)S(1)} collective-permute-done((bf16[256,128]{1,0:T(8,128)(2,1)S(1)}, bf16[256,128]{1,0:T(8,128)(2,1)S(1)}, u32[]{:S(2)}, u32[]{:S(2)}) %collective-permute-start.1) | collective-permute-done | bytes 65568 | tf_op jit(solution)/shard_map/ppermute | solution.py:252
  12.3 0.4 shard_map.80.refs_4_
  12.7 0.0 collective-permute-done.refs_3_
  12.7 0.0 copy-start.3
  12.7 0.0 copy-start.4
  12.8 0.0 copy-start.5
  12.8 0.6 %shard_map.81 = (f32[264,128]{1,0:T(8,128)S(1)}, f32[264,128]{1,0:T(8,128)S(1)}, f32[264,128]{1,0:T(8,128)S(1)}, f32[264,128]{1,0:T(8,128)S(1)}) custom-call(bf16[4,8,128,128]{3,2,1,0:T(8,128)(2,1)S(1)} %bitcast.5, s32[4,8]{1,0:T(4,128)S(1)} %bitcast.9, s32[1,4]{1,0:T(1,128)S(1)} %copy-done.7, bf16[256,128]{1,0:T(8,128)(2,1)S(1)} %collective-permute-done.refs_3_, ...), custom_call_target="tpu_custom_call" | custom-call | tf_op jit(solution)/shard_map/pallas_call | solution.py:278
  13.3 2.5 %collective-permute-start.3 = (f32[264,128]{1,0:T(8,128)S(1)}, f32[264,128]{1,0:T(8,128)S(1)}, u32[]{:S(2)}, u32[]{:S(2)}) collective-permute-start(f32[264,128]{1,0:T(8,128)S(1)} %get-tuple-element.13), channel_id=1, source_target_pairs={{0,6},{2,4},{4,2},{6,0},{1,7},{3,5},{5,3},{7,1},{8,14},{10,12},{12... | collective-permute-start | bytes 405512 | tf_op jit(solution)/shard_map/ppermute | solution.py:290
  15.9 0.5 %collective-permute-start.4 = (f32[264,128]{1,0:T(8,128)S(1)}, f32[264,128]{1,0:T(8,128)S(1)}, u32[]{:S(2)}, u32[]{:S(2)}) collective-permute-start(f32[264,128]{1,0:T(8,128)S(1)} %get-tuple-element.14), channel_id=1, source_target_pairs={{0,4},{2,6},{4,0},{6,2},{1,5},{3,7},{5,1},{7,3},{8,12},{10,14},{12... | collective-permute-start | bytes 405512 | tf_op jit(solution)/shard_map/ppermute | solution.py:290
  16.4 0.5 %collective-permute-start.5 = (f32[264,128]{1,0:T(8,128)S(1)}, f32[264,128]{1,0:T(8,128)S(1)}, u32[]{:S(2)}, u32[]{:S(2)}) collective-permute-start(f32[264,128]{1,0:T(8,128)S(1)} %get-tuple-element.15), channel_id=1, source_target_pairs={{0,2},{2,0},{4,6},{6,4},{1,3},{3,1},{5,7},{7,5},{8,10},{10,8},{12,... | collective-permute-start | bytes 405512 | tf_op jit(solution)/shard_map/ppermute | solution.py:290
  16.9 3.4 %collective-permute-done.3.refs_1_ = f32[264,128]{1,0:T(8,128)S(1)} collective-permute-done((f32[264,128]{1,0:T(8,128)S(1)}, f32[264,128]{1,0:T(8,128)S(1)}, u32[]{:S(2)}, u32[]{:S(2)}) %collective-permute-start.3) | collective-permute-done | bytes 135200 | tf_op jit(solution)/shard_map/ppermute | solution.py:290
  20.3 1.3 %collective-permute-done.4.refs_2_ = f32[264,128]{1,0:T(8,128)S(1)} collective-permute-done((f32[264,128]{1,0:T(8,128)S(1)}, f32[264,128]{1,0:T(8,128)S(1)}, u32[]{:S(2)}, u32[]{:S(2)}) %collective-permute-start.4) | collective-permute-done | bytes 135200 | tf_op jit(solution)/shard_map/ppermute | solution.py:290
  21.6 0.2 collective-permute-done.5.refs_3_
  21.8 0.1 shard_map.82.mine_ref
  21.8 0.1 collective-permute-start.6
  21.9 1.3 %collective-permute-done.6.other_ref = f32[256,128]{1,0:T(8,128)S(1)} collective-permute-done((f32[256,128]{1,0:T(8,128)S(1)}, f32[256,128]{1,0:T(8,128)S(1)}, u32[]{:S(2)}, u32[]{:S(2)}) %collective-permute-start.6) | collective-permute-done | bytes 131104 | tf_op jit(solution)/shard_map/ppermute | solution.py:294
  23.3 0.0 copy-done.3
  23.3 0.0 copy-done.4
  23.3 0.0 copy-done.5
  23.3 0.7 %shard_map.83 = (bf16[512,128]{1,0:T(8,128)(2,1)S(1)}, f32[128,128]{1,0:T(8,128)S(1)}) custom-call(f32[264,128]{1,0:T(8,128)S(1)} %shard_map.82.mine_ref, f32[256,128]{1,0:T(8,128)S(1)} %collective-permute-done.6.other_ref, bf16[512,128]{1,0:T(8,128)(2,1)S(1)} %copy-done.3, bf16[128,128]{1,0:T(8,128)(2,1)S(1)} %copy-done.5, bf16[512,128]{1,0:T(8,128)(2,1)S(1)} %copy-done.4), custom_call_target="tpu_custom_call" | custom-call | tf_op jit(solution)/shard_map/pallas_call | solution.py:296
  24.0 1.7 %collective-permute-start.7 = (f32[128,128]{1,0:T(8,128)S(1)}, f32[128,128]{1,0:T(8,128)S(1)}, u32[]{:S(2)}, u32[]{:S(2)}) collective-permute-start(f32[128,128]{1,0:T(8,128)S(1)} %get-tuple-element.17.refs_0_), channel_id=1, source_target_pairs={{0,6},{2,4},{4,2},{6,0},{1,7},{3,5},{5,3},{7,1},{8,14},{10,12},{12... | collective-permute-start | bytes 196616 | tf_op jit(solution)/shard_map/ppermute | solution.py:231
  25.6 1.4 %collective-permute-start.8 = (f32[128,128]{1,0:T(8,128)S(1)}, f32[128,128]{1,0:T(8,128)S(1)}, u32[]{:S(2)}, u32[]{:S(2)}) collective-permute-start(f32[128,128]{1,0:T(8,128)S(1)} %get-tuple-element.17.refs_0_), channel_id=1, source_target_pairs={{0,4},{2,6},{4,0},{6,2},{1,5},{3,7},{5,1},{7,3},{8,12},{10,14},{12... | collective-permute-start | bytes 196616 | tf_op jit(solution)/shard_map/ppermute | solution.py:231
  27.0 0.5 %collective-permute-start.9 = (f32[128,128]{1,0:T(8,128)S(1)}, f32[128,128]{1,0:T(8,128)S(1)}, u32[]{:S(2)}, u32[]{:S(2)}) collective-permute-start(f32[128,128]{1,0:T(8,128)S(1)} %get-tuple-element.17.refs_0_), channel_id=1, source_target_pairs={{0,2},{2,0},{4,6},{6,4},{1,3},{3,1},{5,7},{7,5},{8,10},{10,8},{12,... | collective-permute-start | bytes 196616 | tf_op jit(solution)/shard_map/ppermute | solution.py:231
  27.5 1.7 %collective-permute-done.7.refs_1_ = f32[128,128]{1,0:T(8,128)S(1)} collective-permute-done((f32[128,128]{1,0:T(8,128)S(1)}, f32[128,128]{1,0:T(8,128)S(1)}, u32[]{:S(2)}, u32[]{:S(2)}) %collective-permute-start.7) | collective-permute-done | bytes 65568 | tf_op jit(solution)/shard_map/ppermute | solution.py:231
  29.3 1.2 %collective-permute-done.8.refs_2_ = f32[128,128]{1,0:T(8,128)S(1)} collective-permute-done((f32[128,128]{1,0:T(8,128)S(1)}, f32[128,128]{1,0:T(8,128)S(1)}, u32[]{:S(2)}, u32[]{:S(2)}) %collective-permute-start.8) | collective-permute-done | bytes 65568 | tf_op jit(solution)/shard_map/ppermute | solution.py:231
  30.5 0.8 %collective-permute-done.9.refs_3_ = f32[128,128]{1,0:T(8,128)S(1)} collective-permute-done((f32[128,128]{1,0:T(8,128)S(1)}, f32[128,128]{1,0:T(8,128)S(1)}, u32[]{:S(2)}, u32[]{:S(2)}) %collective-permute-start.9) | collective-permute-done | bytes 65568 | tf_op jit(solution)/shard_map/ppermute | solution.py:231
  31.3 2.9 %collective-permute-start.10 = (f32[128,128]{1,0:T(8,128)S(1)}, f32[128,128]{1,0:T(8,128)S(1)}, u32[]{:S(2)}, u32[]{:S(2)}) collective-permute-start(f32[128,128]{1,0:T(8,128)S(1)} %shard_map.85.refs_0_), channel_id=1, source_target_pairs={{0,24},{8,16},{16,8},{24,0},{1,25},{9,17},{17,9},{25,1},{2,26},{10... | collective-permute-start | bytes 196616 | tf_op jit(solution)/shard_map/ppermute | solution.py:231
  34.3 0.3 collective-permute-start.11
  34.5 1.2 %collective-permute-start.12 = (f32[128,128]{1,0:T(8,128)S(1)}, f32[128,128]{1,0:T(8,128)S(1)}, u32[]{:S(2)}, u32[]{:S(2)}) collective-permute-start(f32[128,128]{1,0:T(8,128)S(1)} %shard_map.85.refs_0_), channel_id=1, source_target_pairs={{0,8},{8,0},{16,24},{24,16},{1,9},{9,1},{17,25},{25,17},{2,10},{10... | collective-permute-start | bytes 196616 | tf_op jit(solution)/shard_map/ppermute | solution.py:231
  35.8 0.7 %shard_map.84 = bf16[512,128]{1,0:T(8,128)(2,1)} custom-call(bf16[512,128]{1,0:T(8,128)(2,1)S(1)} %get-tuple-element.16.x_ref), custom_call_target="tpu_custom_call" | custom-call | tf_op jit(solution)/shard_map/pallas_call | solution.py:303
  36.4 1.8 %collective-permute-done.10.refs_1_ = f32[128,128]{1,0:T(8,128)S(1)} collective-permute-done((f32[128,128]{1,0:T(8,128)S(1)}, f32[128,128]{1,0:T(8,128)S(1)}, u32[]{:S(2)}, u32[]{:S(2)}) %collective-permute-start.10) | collective-permute-done | bytes 65568 | tf_op jit(solution)/shard_map/ppermute | solution.py:231
  38.3 2.0 %collective-permute-done.11.refs_2_ = f32[128,128]{1,0:T(8,128)S(1)} collective-permute-done((f32[128,128]{1,0:T(8,128)S(1)}, f32[128,128]{1,0:T(8,128)S(1)}, u32[]{:S(2)}, u32[]{:S(2)}) %collective-permute-start.11) | collective-permute-done | bytes 65568 | tf_op jit(solution)/shard_map/ppermute | solution.py:231
  40.2 0.0 collective-permute-done.12.refs_3_
  40.2 0.6 %shard_map.86 = f32[128,128]{1,0:T(8,128)} custom-call(f32[128,128]{1,0:T(8,128)S(1)} %shard_map.85.refs_0_, f32[128,128]{1,0:T(8,128)S(1)} %collective-permute-done.10.refs_1_, f32[128,128]{1,0:T(8,128)S(1)} %collective-permute-done.11.refs_2_, f32[128,128]{1,0:T(8,128)S(1)} %collective-permute-done.12.refs_3_), custom_call_target="tpu_custom_call" | custom-call | tf_op jit(solution)/shard_map/pallas_call | solution.py:232
  (2 shorter events, 0.0 us)
Async XLA Ops:
  0.6 0.9 %copy-start.2 = (bf16[512,128]{1,0:T(8,128)(2,1)S(1)}, bf16[512,128]{1,0:T(8,128)(2,1)}, u32[]{:S(2)}) copy-start(bf16[512,128]{1,0:T(8,128)(2,1)} %x_ref.3) | copy-start | bytes 393220
  1.6 9.0 %collective-permute-start.2 = (bf16[256,128]{1,0:T(8,128)(2,1)S(1)}, bf16[256,128]{1,0:T(8,128)(2,1)S(1)}, u32[]{:S(2)}, u32[]{:S(2)}) collective-permute-start(bf16[256,128]{1,0:T(8,128)(2,1)S(1)} %shard_map.77.x_ref), channel_id=1, source_target_pairs={{0,16},{8,24},{16,8},{24,0},{1,17},{9,25},{17,9},{25,1},{2,18},{10... | collective-permute-start | bytes 196616 | tf_op jit(solution)/shard_map/ppermute | solution.py:252
  5.7 6.6 %collective-permute-start.1 = (bf16[256,128]{1,0:T(8,128)(2,1)S(1)}, bf16[256,128]{1,0:T(8,128)(2,1)S(1)}, u32[]{:S(2)}, u32[]{:S(2)}) collective-permute-start(bf16[256,128]{1,0:T(8,128)(2,1)S(1)} %shard_map.77.x_ref), channel_id=1, source_target_pairs={{0,24},{8,16},{16,0},{24,8},{1,25},{9,17},{17,1},{25,9},{2,26},{10... | collective-permute-start | bytes 196616 | tf_op jit(solution)/shard_map/ppermute | solution.py:252
  6.8 5.9 %collective-permute-start = (bf16[256,128]{1,0:T(8,128)(2,1)S(1)}, bf16[256,128]{1,0:T(8,128)(2,1)S(1)}, u32[]{:S(2)}, u32[]{:S(2)}) collective-permute-start(bf16[256,128]{1,0:T(8,128)(2,1)S(1)} %shard_map.77.x_ref), channel_id=1, source_target_pairs={{0,8},{8,0},{16,24},{24,16},{1,9},{9,1},{17,25},{25,17},{2,10},{10... | collective-permute-start | bytes 196616 | tf_op jit(solution)/shard_map/ppermute | solution.py:252
  7.3 1.2 %copy-start = (bf16[1,4,8,128,128]{4,3,2,1,0:T(8,128)(2,1)S(1)}, bf16[1,4,8,128,128]{4,3,2,1,0:T(8,128)(2,1)}, u32[]{:S(2)}) copy-start(bf16[1,4,8,128,128]{4,3,2,1,0:T(8,128)(2,1)} %param.10) | copy-start | bytes 3145732
  8.5 0.7 %copy-start.6 = (s32[1,4,8]{2,1,0:T(4,128)S(1)}, s32[1,4,8]{2,1,0:T(4,128)}, u32[]{:S(2)}) copy-start(s32[1,4,8]{2,1,0:T(4,128)} %param.8) | copy-start | bytes 388
  9.2 0.7 %copy-start.7 = (s32[1,4]{1,0:T(1,128)S(1)}, s32[1,4]{1,0:T(1,128)}, u32[]{:S(2)}) copy-start(s32[1,4]{1,0:T(1,128)} %refs_2_.1) | copy-start | bytes 52
  9.9 1.2 %copy-start.1 = (bf16[1,4,8,128,128]{4,3,2,1,0:T(8,128)(2,1)S(1)}, bf16[1,4,8,128,128]{4,3,2,1,0:T(8,128)(2,1)}, u32[]{:S(2)}) copy-start(bf16[1,4,8,128,128]{4,3,2,1,0:T(8,128)(2,1)} %param.10) | copy-start | bytes 3145732
  12.7 10.5 %copy-start.3 = (bf16[512,128]{1,0:T(8,128)(2,1)S(1)}, bf16[512,128]{1,0:T(8,128)(2,1)}, u32[]{:S(2)}) copy-start(bf16[512,128]{1,0:T(8,128)(2,1)} %x_ref.3) | copy-start | bytes 393220
  12.7 10.5 %copy-start.4 = (bf16[512,128]{1,0:T(8,128)(2,1)S(1)}, bf16[512,128]{1,0:T(8,128)(2,1)}, u32[]{:S(2)}) copy-start(bf16[512,128]{1,0:T(8,128)(2,1)} %cot_ref.1) | copy-start | bytes 393220
  12.8 10.5 %copy-start.5 = (bf16[128,128]{1,0:T(8,128)(2,1)S(1)}, bf16[128,128]{1,0:T(8,128)(2,1)}, u32[]{:S(2)}) copy-start(bf16[128,128]{1,0:T(8,128)(2,1)} %w_ref.1) | copy-start | bytes 98308
  13.3 7.0 %collective-permute-start.3 = (f32[264,128]{1,0:T(8,128)S(1)}, f32[264,128]{1,0:T(8,128)S(1)}, u32[]{:S(2)}, u32[]{:S(2)}) collective-permute-start(f32[264,128]{1,0:T(8,128)S(1)} %get-tuple-element.13), channel_id=1, source_target_pairs={{0,6},{2,4},{4,2},{6,0},{1,7},{3,5},{5,3},{7,1},{8,14},{10,12},{12... | collective-permute-start | bytes 405512 | tf_op jit(solution)/shard_map/ppermute | solution.py:290
  15.9 5.7 %collective-permute-start.4 = (f32[264,128]{1,0:T(8,128)S(1)}, f32[264,128]{1,0:T(8,128)S(1)}, u32[]{:S(2)}, u32[]{:S(2)}) collective-permute-start(f32[264,128]{1,0:T(8,128)S(1)} %get-tuple-element.14), channel_id=1, source_target_pairs={{0,4},{2,6},{4,0},{6,2},{1,5},{3,7},{5,1},{7,3},{8,12},{10,14},{12... | collective-permute-start | bytes 405512 | tf_op jit(solution)/shard_map/ppermute | solution.py:290
  16.4 5.4 %collective-permute-start.5 = (f32[264,128]{1,0:T(8,128)S(1)}, f32[264,128]{1,0:T(8,128)S(1)}, u32[]{:S(2)}, u32[]{:S(2)}) collective-permute-start(f32[264,128]{1,0:T(8,128)S(1)} %get-tuple-element.15), channel_id=1, source_target_pairs={{0,2},{2,0},{4,6},{6,4},{1,3},{3,1},{5,7},{7,5},{8,10},{10,8},{12,... | collective-permute-start | bytes 405512 | tf_op jit(solution)/shard_map/ppermute | solution.py:290
  21.8 1.4 %collective-permute-start.6 = (f32[256,128]{1,0:T(8,128)S(1)}, f32[256,128]{1,0:T(8,128)S(1)}, u32[]{:S(2)}, u32[]{:S(2)}) collective-permute-start(f32[256,128]{1,0:T(8,128)S(1)} %slice.4), channel_id=1, source_target_pairs={{0,1},{1,0},{2,3},{3,2},{4,5},{5,4},{6,7},{7,6},{8,9},{9,8},{10,11... | collective-permute-start | bytes 393224 | tf_op jit(solution)/shard_map/ppermute | solution.py:294
  24.0 5.3 %collective-permute-start.7 = (f32[128,128]{1,0:T(8,128)S(1)}, f32[128,128]{1,0:T(8,128)S(1)}, u32[]{:S(2)}, u32[]{:S(2)}) collective-permute-start(f32[128,128]{1,0:T(8,128)S(1)} %get-tuple-element.17.refs_0_), channel_id=1, source_target_pairs={{0,6},{2,4},{4,2},{6,0},{1,7},{3,5},{5,3},{7,1},{8,14},{10,12},{12... | collective-permute-start | bytes 196616 | tf_op jit(solution)/shard_map/ppermute | solution.py:231
  25.6 4.9 %collective-permute-start.8 = (f32[128,128]{1,0:T(8,128)S(1)}, f32[128,128]{1,0:T(8,128)S(1)}, u32[]{:S(2)}, u32[]{:S(2)}) collective-permute-start(f32[128,128]{1,0:T(8,128)S(1)} %get-tuple-element.17.refs_0_), channel_id=1, source_target_pairs={{0,4},{2,6},{4,0},{6,2},{1,5},{3,7},{5,1},{7,3},{8,12},{10,14},{12... | collective-permute-start | bytes 196616 | tf_op jit(solution)/shard_map/ppermute | solution.py:231
  27.0 4.3 %collective-permute-start.9 = (f32[128,128]{1,0:T(8,128)S(1)}, f32[128,128]{1,0:T(8,128)S(1)}, u32[]{:S(2)}, u32[]{:S(2)}) collective-permute-start(f32[128,128]{1,0:T(8,128)S(1)} %get-tuple-element.17.refs_0_), channel_id=1, source_target_pairs={{0,2},{2,0},{4,6},{6,4},{1,3},{3,1},{5,7},{7,5},{8,10},{10,8},{12,... | collective-permute-start | bytes 196616 | tf_op jit(solution)/shard_map/ppermute | solution.py:231
  31.3 6.9 %collective-permute-start.10 = (f32[128,128]{1,0:T(8,128)S(1)}, f32[128,128]{1,0:T(8,128)S(1)}, u32[]{:S(2)}, u32[]{:S(2)}) collective-permute-start(f32[128,128]{1,0:T(8,128)S(1)} %shard_map.85.refs_0_), channel_id=1, source_target_pairs={{0,24},{8,16},{16,8},{24,0},{1,25},{9,17},{17,9},{25,1},{2,26},{10... | collective-permute-start | bytes 196616 | tf_op jit(solution)/shard_map/ppermute | solution.py:231
  34.3 6.0 %collective-permute-start.11 = (f32[128,128]{1,0:T(8,128)S(1)}, f32[128,128]{1,0:T(8,128)S(1)}, u32[]{:S(2)}, u32[]{:S(2)}) collective-permute-start(f32[128,128]{1,0:T(8,128)S(1)} %shard_map.85.refs_0_), channel_id=1, source_target_pairs={{0,16},{8,24},{16,0},{24,8},{1,17},{9,25},{17,1},{25,9},{2,18},{10... | collective-permute-start | bytes 196616 | tf_op jit(solution)/shard_map/ppermute | solution.py:231
  34.5 5.7 %collective-permute-start.12 = (f32[128,128]{1,0:T(8,128)S(1)}, f32[128,128]{1,0:T(8,128)S(1)}, u32[]{:S(2)}, u32[]{:S(2)}) collective-permute-start(f32[128,128]{1,0:T(8,128)S(1)} %shard_map.85.refs_0_), channel_id=1, source_target_pairs={{0,8},{8,0},{16,24},{24,16},{1,9},{9,1},{17,25},{25,17},{2,10},{10... | collective-permute-start | bytes 196616 | tf_op jit(solution)/shard_map/ppermute | solution.py:231

commit v3 on v2

--- a/solution.py
+++ b/solution.py
@@ -10,7 +10,7 @@
 f32 = jnp.float32
 bf16 = jnp.bfloat16
 LONGEST = 8
-ORDER = (0, 3, 2, 1)
+STEPS = [(2, 3, 1, 0), (1, 0, 3, 2), (3, 2, 0, 1)]
 
 
 def vmem(n):
@@ -116,7 +116,7 @@
     n = col_tiles // 2
     left = lower_half((tile, width))
     for k, out in enumerate(outs):
-        q = rep ^ ORDER[k] if n_rep == 4 else lax.rem(rep + k, n_rep)
+        q = rep if k == 0 else target(steps(n_rep)[k - 1], rep)
         for c in range(n):
             top = acc_ref[q * col_tiles + c]
             low = acc_ref[q * col_tiles + n + c]
@@ -207,14 +207,17 @@
     )
 
 
-def pairs(n, k):
-    return [(i, i ^ k) for i in range(n)]
-
-
 def steps(n):
     if n == 4:
-        return [(2, 3, 1, 0), (3, 2, 0, 1), (1, 0, 3, 2)]
+        return STEPS
     return [tuple(i ^ k for i in range(n)) for k in range(n - 1, 0, -1)]
+
+
+def target(step, me):
+    j = jnp.int32(0)
+    for i, to in enumerate(step):
+        j = jnp.where(me == i, to, j)
+    return j
 
 
 def sender(step, me):
@@ -228,7 +231,7 @@
     n = lax.axis_size(axis)
     if n > LONGEST:
         return lax.psum(x, axis)
-    parts = [lax.ppermute(x, axis, pairs(n, k)) for k in range(n - 1, 0, -1)]
+    parts = [lax.ppermute(x, axis, list(enumerate(step))) for step in steps(n)]
     return call(sum_kernel, shape(*x.shape), vmem(n))(x, *parts)
 
 
@@ -287,8 +290,8 @@
         )
         mine, *sends = call(send_kernel, messages, vmem(2))(total, degrees)
     parts = [
-        lax.ppermute(sent, "rep", pairs(n_rep, ORDER[k + 1]))
-        for k, sent in enumerate(sends)
+        lax.ppermute(sent, "rep", list(enumerate(step)))
+        for step, sent in zip(steps(n_rep), sends)
     ]
     mine = call(sum_kernel, messages[0], vmem(n_rep))(mine, *parts)
     other = lax.ppermute(mine[:half], "feat", [(0, 1), (1, 0)])

time: 41.1 us -> 40.3 us (0.981)
  waiting for transfers between devices: 14.6 us -> 12.1 us
  starting transfers between devices: 17.3 us -> 19 us
    ppermute x9, waiting for transfers between devices: 12.4 us -> 9.92 us  [the longest x6 6.32 us: total_over(): parts = [lax.ppermute(x, axis, list(enumerate(step))) for step in steps(n)]]
    ppermute x9, starting transfers between devices: 11.6 us -> 12.9 us  [the longest x6 8.46 us: total_over(): parts = [lax.ppermute(x, axis, list(enumerate(step))) for step in steps(n)]]
  transfers between devices with their start and end apart: 13 -> 13, of which waited for: 10 -> 11; matrix products, arithmetic and copies ran while one was open for 0% -> 0% of each run, Pallas kernels for 5% -> 5%
where the time goes in v3:
time: 40.3 us; the launch traced here: 40 us
  starting transfers between devices  19 us (47%)
  waiting for transfers between devices  12.1 us (30%)
  Pallas kernels  4.24 us (11%)
  local copies, waits for them, and re-layouts  3.94 us (10%)
  between operations  0.71 us (2%)
    ppermute x6, starting transfers between devices, total_over(): parts = [lax.ppermute(x, axis, list(enumerate(step))) for step in steps(n)]  8.46 us
    ppermute x6, waiting for transfers between devices, total_over(): parts = [lax.ppermute(x, axis, list(enumerate(step))) for step in steps(n)]  6.32 us
    ppermute x3, starting transfers between devices, shards(): lax.ppermute(packed, 'row', list(enumerate(step)))  6 us
    ppermute x3, starting transfers between devices, shards(): lax.ppermute(sent, 'rep', list(enumerate(step)))  4.47 us
    unnamed x16, local copies, waits for them, and re-layouts  3.93 us
    ppermute x3, waiting for transfers between devices, shards(): lax.ppermute(sent, 'rep', list(enumerate(step)))  3.6 us
    ppermute x1, waiting for transfers between devices, shards(): other = lax.ppermute(mine[:half], 'feat', [(0, 1), (1, 0)])  1.33 us
    ppermute x3, waiting for transfers between devices, shards(): lax.ppermute(packed, 'row', list(enumerate(step)))  0.87 us
  transfers between devices with their start and end apart: 13, of which 11 were waited for; matrix products, arithmetic and copies ran while one was open for 0% of the time, Pallas kernels for 5%

profile of v3, /device:TPU:0, one launch (start us, length us, event | category | flops | bytes accessed | tf_op | source)
XLA Modules:
  0.0 40.0 jit_solution(10797353162153984003)
XLA Ops:
  0.6 0.0 copy-start.2
  0.6 0.9 %copy-done.2 = bf16[512,128]{1,0:T(8,128)(2,1)S(1)} copy-done((bf16[512,128]{1,0:T(8,128)(2,1)S(1)}, bf16[512,128]{1,0:T(8,128)(2,1)}, u32[]{:S(2)}) %copy-start.2) | copy-done | bytes 131096
  1.5 0.1 shard_map.77.x_ref
  1.6 4.1 %collective-permute-start.2 = (bf16[256,128]{1,0:T(8,128)(2,1)S(1)}, bf16[256,128]{1,0:T(8,128)(2,1)S(1)}, u32[]{:S(2)}, u32[]{:S(2)}) collective-permute-start(bf16[256,128]{1,0:T(8,128)(2,1)S(1)} %shard_map.77.x_ref), channel_id=1, source_target_pairs={{0,16},{8,24},{16,8},{24,0},{1,17},{9,25},{17,9},{25,1},{2,18},{10... | collective-permute-start | bytes 196616 | tf_op jit(solution)/shard_map/ppermute | solution.py:255
  5.7 1.6 %collective-permute-start.1 = (bf16[256,128]{1,0:T(8,128)(2,1)S(1)}, bf16[256,128]{1,0:T(8,128)(2,1)S(1)}, u32[]{:S(2)}, u32[]{:S(2)}) collective-permute-start(bf16[256,128]{1,0:T(8,128)(2,1)S(1)} %shard_map.77.x_ref), channel_id=1, source_target_pairs={{0,8},{8,0},{16,24},{24,16},{1,9},{9,1},{17,25},{25,17},{2,10},{10... | collective-permute-start | bytes 196616 | tf_op jit(solution)/shard_map/ppermute | solution.py:255
  7.3 0.3 collective-permute-start
  7.6 0.0 copy-start
  7.6 1.2 %copy-done = bf16[1,4,8,128,128]{4,3,2,1,0:T(8,128)(2,1)S(1)} copy-done((bf16[1,4,8,128,128]{4,3,2,1,0:T(8,128)(2,1)S(1)}, bf16[1,4,8,128,128]{4,3,2,1,0:T(8,128)(2,1)}, u32[]{:S(2)}) %copy-start) | copy-done | bytes 1048600
  8.9 0.0 copy-start.6
  8.9 0.7 %copy-done.6 = s32[1,4,8]{2,1,0:T(4,128)S(1)} copy-done((s32[1,4,8]{2,1,0:T(4,128)S(1)}, s32[1,4,8]{2,1,0:T(4,128)}, u32[]{:S(2)}) %copy-start.6) | copy-done | bytes 152
  9.5 0.0 copy-start.7
  9.5 0.7 %copy-done.7 = s32[1,4]{1,0:T(1,128)S(1)} copy-done((s32[1,4]{1,0:T(1,128)S(1)}, s32[1,4]{1,0:T(1,128)}, u32[]{:S(2)}) %copy-start.7) | copy-done | bytes 40
  10.2 0.0 copy-start.1
  10.2 0.8 %shard_map.78 = (f32[17,128,128]{2,1,0:T(8,128)S(1)}, f32[16,128]{1,0:T(8,128)S(1)}) custom-call(bf16[4,8,128,128]{3,2,1,0:T(8,128)(2,1)S(1)} %bitcast.2, s32[4,8]{1,0:T(4,128)S(1)} %bitcast.6, s32[1,4]{1,0:T(1,128)S(1)} %copy-done.7, bf16[256,128]{1,0:T(8,128)(2,1)S(1)} %shard_map.77.x_ref), custom_call_target="tpu_custom_call" | custom-call | flops 100000000 | bytes 3000000 | tf_op jit(solution)/shard_map/pallas_call | solution.py:263
  11.0 0.0 collective-permute-done.2.block_ref
  11.0 0.5 %copy-done.1 = bf16[1,4,8,128,128]{4,3,2,1,0:T(8,128)(2,1)S(1)} copy-done((bf16[1,4,8,128,128]{4,3,2,1,0:T(8,128)(2,1)S(1)}, bf16[1,4,8,128,128]{4,3,2,1,0:T(8,128)(2,1)}, u32[]{:S(2)}) %copy-start.1) | copy-done | bytes 1048600
  11.4 0.4 shard_map.79.start_ref
  11.8 0.0 collective-permute-done.1.block_ref
  11.8 0.4 shard_map.80.refs_4_
  12.2 0.9 %collective-permute-done.refs_3_ = bf16[256,128]{1,0:T(8,128)(2,1)S(1)} collective-permute-done((bf16[256,128]{1,0:T(8,128)(2,1)S(1)}, bf16[256,128]{1,0:T(8,128)(2,1)S(1)}, u32[]{:S(2)}, u32[]{:S(2)}) %collective-permute-start) | collective-permute-done | bytes 65568 | tf_op jit(solution)/shard_map/ppermute | solution.py:255
  13.1 0.0 copy-start.3
  13.1 0.0 copy-start.4
  13.1 0.0 copy-start.5
  13.1 0.6 %shard_map.81 = (f32[264,128]{1,0:T(8,128)S(1)}, f32[264,128]{1,0:T(8,128)S(1)}, f32[264,128]{1,0:T(8,128)S(1)}, f32[264,128]{1,0:T(8,128)S(1)}) custom-call(bf16[4,8,128,128]{3,2,1,0:T(8,128)(2,1)S(1)} %bitcast.5, s32[4,8]{1,0:T(4,128)S(1)} %bitcast.9, s32[1,4]{1,0:T(1,128)S(1)} %copy-done.7, bf16[256,128]{1,0:T(8,128)(2,1)S(1)} %collective-permute-done.refs_3_, ...), custom_call_target="tpu_custom_call" | custom-call | tf_op jit(solution)/shard_map/pallas_call | solution.py:281
  13.6 1.6 %collective-permute-start.3 = (f32[264,128]{1,0:T(8,128)S(1)}, f32[264,128]{1,0:T(8,128)S(1)}, u32[]{:S(2)}, u32[]{:S(2)}) collective-permute-start(f32[264,128]{1,0:T(8,128)S(1)} %get-tuple-element.13), channel_id=1, source_target_pairs={{0,4},{2,6},{4,2},{6,0},{1,5},{3,7},{5,3},{7,1},{8,12},{10,14},{12... | collective-permute-start | bytes 405512 | tf_op jit(solution)/shard_map/ppermute | solution.py:293
  15.2 1.5 %collective-permute-start.4 = (f32[264,128]{1,0:T(8,128)S(1)}, f32[264,128]{1,0:T(8,128)S(1)}, u32[]{:S(2)}, u32[]{:S(2)}) collective-permute-start(f32[264,128]{1,0:T(8,128)S(1)} %get-tuple-element.14), channel_id=1, source_target_pairs={{0,2},{2,0},{4,6},{6,4},{1,3},{3,1},{5,7},{7,5},{8,10},{10,8},{12,... | collective-permute-start | bytes 405512 | tf_op jit(solution)/shard_map/ppermute | solution.py:293
  16.7 1.4 %collective-permute-start.5 = (f32[264,128]{1,0:T(8,128)S(1)}, f32[264,128]{1,0:T(8,128)S(1)}, u32[]{:S(2)}, u32[]{:S(2)}) collective-permute-start(f32[264,128]{1,0:T(8,128)S(1)} %get-tuple-element.15), channel_id=1, source_target_pairs={{0,6},{2,4},{4,0},{6,2},{1,7},{3,5},{5,1},{7,3},{8,14},{10,12},{12... | collective-permute-start | bytes 405512 | tf_op jit(solution)/shard_map/ppermute | solution.py:293
  18.1 1.7 %collective-permute-done.3.refs_1_ = f32[264,128]{1,0:T(8,128)S(1)} collective-permute-done((f32[264,128]{1,0:T(8,128)S(1)}, f32[264,128]{1,0:T(8,128)S(1)}, u32[]{:S(2)}, u32[]{:S(2)}) %collective-permute-start.3) | collective-permute-done | bytes 135200 | tf_op jit(solution)/shard_map/ppermute | solution.py:293
  19.8 0.4 collective-permute-done.4.refs_2_
  20.2 1.5 %collective-permute-done.5.refs_3_ = f32[264,128]{1,0:T(8,128)S(1)} collective-permute-done((f32[264,128]{1,0:T(8,128)S(1)}, f32[264,128]{1,0:T(8,128)S(1)}, u32[]{:S(2)}, u32[]{:S(2)}) %collective-permute-start.5) | collective-permute-done | bytes 135200 | tf_op jit(solution)/shard_map/ppermute | solution.py:293
  21.7 0.1 shard_map.82.mine_ref
  21.8 0.1 collective-permute-start.6
  21.9 1.3 %collective-permute-done.6.other_ref = f32[256,128]{1,0:T(8,128)S(1)} collective-permute-done((f32[256,128]{1,0:T(8,128)S(1)}, f32[256,128]{1,0:T(8,128)S(1)}, u32[]{:S(2)}, u32[]{:S(2)}) %collective-permute-start.6) | collective-permute-done | bytes 131104 | tf_op jit(solution)/shard_map/ppermute | solution.py:297
  23.2 0.0 copy-done.3
  23.2 0.0 copy-done.4
  23.2 0.0 copy-done.5
  23.2 0.7 %shard_map.83 = (bf16[512,128]{1,0:T(8,128)(2,1)S(1)}, f32[128,128]{1,0:T(8,128)S(1)}) custom-call(f32[264,128]{1,0:T(8,128)S(1)} %shard_map.82.mine_ref, f32[256,128]{1,0:T(8,128)S(1)} %collective-permute-done.6.other_ref, bf16[512,128]{1,0:T(8,128)(2,1)S(1)} %copy-done.3, bf16[128,128]{1,0:T(8,128)(2,1)S(1)} %copy-done.5, bf16[512,128]{1,0:T(8,128)(2,1)S(1)} %copy-done.4), custom_call_target="tpu_custom_call" | custom-call | tf_op jit(solution)/shard_map/pallas_call | solution.py:299
  23.9 1.5 %collective-permute-start.7 = (f32[128,128]{1,0:T(8,128)S(1)}, f32[128,128]{1,0:T(8,128)S(1)}, u32[]{:S(2)}, u32[]{:S(2)}) collective-permute-start(f32[128,128]{1,0:T(8,128)S(1)} %get-tuple-element.17.refs_0_), channel_id=1, source_target_pairs={{0,4},{2,6},{4,2},{6,0},{1,5},{3,7},{5,3},{7,1},{8,12},{10,14},{12... | collective-permute-start | bytes 196616 | tf_op jit(solution)/shard_map/ppermute | solution.py:234
  25.4 1.5 %collective-permute-start.8 = (f32[128,128]{1,0:T(8,128)S(1)}, f32[128,128]{1,0:T(8,128)S(1)}, u32[]{:S(2)}, u32[]{:S(2)}) collective-permute-start(f32[128,128]{1,0:T(8,128)S(1)} %get-tuple-element.17.refs_0_), channel_id=1, source_target_pairs={{0,2},{2,0},{4,6},{6,4},{1,3},{3,1},{5,7},{7,5},{8,10},{10,8},{12,... | collective-permute-start | bytes 196616 | tf_op jit(solution)/shard_map/ppermute | solution.py:234
  26.9 1.0 %collective-permute-start.9 = (f32[128,128]{1,0:T(8,128)S(1)}, f32[128,128]{1,0:T(8,128)S(1)}, u32[]{:S(2)}, u32[]{:S(2)}) collective-permute-start(f32[128,128]{1,0:T(8,128)S(1)} %get-tuple-element.17.refs_0_), channel_id=1, source_target_pairs={{0,6},{2,4},{4,0},{6,2},{1,7},{3,5},{5,1},{7,3},{8,14},{10,12},{12... | collective-permute-start | bytes 196616 | tf_op jit(solution)/shard_map/ppermute | solution.py:234
  27.9 2.0 %collective-permute-done.7.refs_1_ = f32[128,128]{1,0:T(8,128)S(1)} collective-permute-done((f32[128,128]{1,0:T(8,128)S(1)}, f32[128,128]{1,0:T(8,128)S(1)}, u32[]{:S(2)}, u32[]{:S(2)}) %collective-permute-start.7) | collective-permute-done | bytes 65568 | tf_op jit(solution)/shard_map/ppermute | solution.py:234
  29.8 0.4 %collective-permute-done.8.refs_2_ = f32[128,128]{1,0:T(8,128)S(1)} collective-permute-done((f32[128,128]{1,0:T(8,128)S(1)}, f32[128,128]{1,0:T(8,128)S(1)}, u32[]{:S(2)}, u32[]{:S(2)}) %collective-permute-start.8) | collective-permute-done | bytes 65568 | tf_op jit(solution)/shard_map/ppermute | solution.py:234
  30.2 0.9 %collective-permute-done.9.refs_3_ = f32[128,128]{1,0:T(8,128)S(1)} collective-permute-done((f32[128,128]{1,0:T(8,128)S(1)}, f32[128,128]{1,0:T(8,128)S(1)}, u32[]{:S(2)}, u32[]{:S(2)}) %collective-permute-start.9) | collective-permute-done | bytes 65568 | tf_op jit(solution)/shard_map/ppermute | solution.py:234
  31.2 3.0 %collective-permute-start.10 = (f32[128,128]{1,0:T(8,128)S(1)}, f32[128,128]{1,0:T(8,128)S(1)}, u32[]{:S(2)}, u32[]{:S(2)}) collective-permute-start(f32[128,128]{1,0:T(8,128)S(1)} %shard_map.85.refs_0_), channel_id=1, source_target_pairs={{0,16},{8,24},{16,8},{24,0},{1,17},{9,25},{17,9},{25,1},{2,18},{10... | collective-permute-start | bytes 196616 | tf_op jit(solution)/shard_map/ppermute | solution.py:234
  34.1 0.0 collective-permute-start.11
  34.1 1.5 %collective-permute-start.12 = (f32[128,128]{1,0:T(8,128)S(1)}, f32[128,128]{1,0:T(8,128)S(1)}, u32[]{:S(2)}, u32[]{:S(2)}) collective-permute-start(f32[128,128]{1,0:T(8,128)S(1)} %shard_map.85.refs_0_), channel_id=1, source_target_pairs={{0,24},{8,16},{16,0},{24,8},{1,25},{9,17},{17,1},{25,9},{2,26},{10... | collective-permute-start | bytes 196616 | tf_op jit(solution)/shard_map/ppermute | solution.py:234
  35.7 0.7 %shard_map.84 = bf16[512,128]{1,0:T(8,128)(2,1)} custom-call(bf16[512,128]{1,0:T(8,128)(2,1)S(1)} %get-tuple-element.16.x_ref), custom_call_target="tpu_custom_call" | custom-call | tf_op jit(solution)/shard_map/pallas_call | solution.py:306
  36.4 1.0 %collective-permute-done.10.refs_1_ = f32[128,128]{1,0:T(8,128)S(1)} collective-permute-done((f32[128,128]{1,0:T(8,128)S(1)}, f32[128,128]{1,0:T(8,128)S(1)}, u32[]{:S(2)}, u32[]{:S(2)}) %collective-permute-start.10) | collective-permute-done | bytes 65568 | tf_op jit(solution)/shard_map/ppermute | solution.py:234
  37.4 1.3 %collective-permute-done.11.refs_2_ = f32[128,128]{1,0:T(8,128)S(1)} collective-permute-done((f32[128,128]{1,0:T(8,128)S(1)}, f32[128,128]{1,0:T(8,128)S(1)}, u32[]{:S(2)}, u32[]{:S(2)}) %collective-permute-start.11) | collective-permute-done | bytes 65568 | tf_op jit(solution)/shard_map/ppermute | solution.py:234
  38.7 0.7 %collective-permute-done.12.refs_3_ = f32[128,128]{1,0:T(8,128)S(1)} collective-permute-done((f32[128,128]{1,0:T(8,128)S(1)}, f32[128,128]{1,0:T(8,128)S(1)}, u32[]{:S(2)}, u32[]{:S(2)}) %collective-permute-start.12) | collective-permute-done | bytes 65568 | tf_op jit(solution)/shard_map/ppermute | solution.py:234
  39.4 0.6 %shard_map.86 = f32[128,128]{1,0:T(8,128)} custom-call(f32[128,128]{1,0:T(8,128)S(1)} %shard_map.85.refs_0_, f32[128,128]{1,0:T(8,128)S(1)} %collective-permute-done.10.refs_1_, f32[128,128]{1,0:T(8,128)S(1)} %collective-permute-done.11.refs_2_, f32[128,128]{1,0:T(8,128)S(1)} %collective-permute-done.12.refs_3_), custom_call_target="tpu_custom_call" | custom-call | tf_op jit(solution)/shard_map/pallas_call | solution.py:235
  (2 shorter events, 0.0 us)
Async XLA Ops:
  0.6 0.9 %copy-start.2 = (bf16[512,128]{1,0:T(8,128)(2,1)S(1)}, bf16[512,128]{1,0:T(8,128)(2,1)}, u32[]{:S(2)}) copy-start(bf16[512,128]{1,0:T(8,128)(2,1)} %x_ref.3) | copy-start | bytes 393220
  1.6 9.3 %collective-permute-start.2 = (bf16[256,128]{1,0:T(8,128)(2,1)S(1)}, bf16[256,128]{1,0:T(8,128)(2,1)S(1)}, u32[]{:S(2)}, u32[]{:S(2)}) collective-permute-start(bf16[256,128]{1,0:T(8,128)(2,1)S(1)} %shard_map.77.x_ref), channel_id=1, source_target_pairs={{0,16},{8,24},{16,8},{24,0},{1,17},{9,25},{17,9},{25,1},{2,18},{10... | collective-permute-start | bytes 196616 | tf_op jit(solution)/shard_map/ppermute | solution.py:255
  5.7 6.1 %collective-permute-start.1 = (bf16[256,128]{1,0:T(8,128)(2,1)S(1)}, bf16[256,128]{1,0:T(8,128)(2,1)S(1)}, u32[]{:S(2)}, u32[]{:S(2)}) collective-permute-start(bf16[256,128]{1,0:T(8,128)(2,1)S(1)} %shard_map.77.x_ref), channel_id=1, source_target_pairs={{0,8},{8,0},{16,24},{24,16},{1,9},{9,1},{17,25},{25,17},{2,10},{10... | collective-permute-start | bytes 196616 | tf_op jit(solution)/shard_map/ppermute | solution.py:255
  7.3 5.8 %collective-permute-start = (bf16[256,128]{1,0:T(8,128)(2,1)S(1)}, bf16[256,128]{1,0:T(8,128)(2,1)S(1)}, u32[]{:S(2)}, u32[]{:S(2)}) collective-permute-start(bf16[256,128]{1,0:T(8,128)(2,1)S(1)} %shard_map.77.x_ref), channel_id=1, source_target_pairs={{0,24},{8,16},{16,0},{24,8},{1,25},{9,17},{17,1},{25,9},{2,26},{10... | collective-permute-start | bytes 196616 | tf_op jit(solution)/shard_map/ppermute | solution.py:255
  7.6 1.2 %copy-start = (bf16[1,4,8,128,128]{4,3,2,1,0:T(8,128)(2,1)S(1)}, bf16[1,4,8,128,128]{4,3,2,1,0:T(8,128)(2,1)}, u32[]{:S(2)}) copy-start(bf16[1,4,8,128,128]{4,3,2,1,0:T(8,128)(2,1)} %param.10) | copy-start | bytes 3145732
  8.9 0.7 %copy-start.6 = (s32[1,4,8]{2,1,0:T(4,128)S(1)}, s32[1,4,8]{2,1,0:T(4,128)}, u32[]{:S(2)}) copy-start(s32[1,4,8]{2,1,0:T(4,128)} %param.8) | copy-start | bytes 388
  9.5 0.7 %copy-start.7 = (s32[1,4]{1,0:T(1,128)S(1)}, s32[1,4]{1,0:T(1,128)}, u32[]{:S(2)}) copy-start(s32[1,4]{1,0:T(1,128)} %refs_2_.1) | copy-start | bytes 52
  10.2 1.2 %copy-start.1 = (bf16[1,4,8,128,128]{4,3,2,1,0:T(8,128)(2,1)S(1)}, bf16[1,4,8,128,128]{4,3,2,1,0:T(8,128)(2,1)}, u32[]{:S(2)}) copy-start(bf16[1,4,8,128,128]{4,3,2,1,0:T(8,128)(2,1)} %param.10) | copy-start | bytes 3145732
  13.1 10.1 %copy-start.3 = (bf16[512,128]{1,0:T(8,128)(2,1)S(1)}, bf16[512,128]{1,0:T(8,128)(2,1)}, u32[]{:S(2)}) copy-start(bf16[512,128]{1,0:T(8,128)(2,1)} %x_ref.3) | copy-start | bytes 393220
  13.1 10.1 %copy-start.4 = (bf16[512,128]{1,0:T(8,128)(2,1)S(1)}, bf16[512,128]{1,0:T(8,128)(2,1)}, u32[]{:S(2)}) copy-start(bf16[512,128]{1,0:T(8,128)(2,1)} %cot_ref.1) | copy-start | bytes 393220
  13.1 10.1 %copy-start.5 = (bf16[128,128]{1,0:T(8,128)(2,1)S(1)}, bf16[128,128]{1,0:T(8,128)(2,1)}, u32[]{:S(2)}) copy-start(bf16[128,128]{1,0:T(8,128)(2,1)} %w_ref.1) | copy-start | bytes 98308
  13.6 6.2 %collective-permute-start.3 = (f32[264,128]{1,0:T(8,128)S(1)}, f32[264,128]{1,0:T(8,128)S(1)}, u32[]{:S(2)}, u32[]{:S(2)}) collective-permute-start(f32[264,128]{1,0:T(8,128)S(1)} %get-tuple-element.13), channel_id=1, source_target_pairs={{0,4},{2,6},{4,2},{6,0},{1,5},{3,7},{5,3},{7,1},{8,12},{10,14},{12... | collective-permute-start | bytes 405512 | tf_op jit(solution)/shard_map/ppermute | solution.py:293
  15.2 5.0 %collective-permute-start.4 = (f32[264,128]{1,0:T(8,128)S(1)}, f32[264,128]{1,0:T(8,128)S(1)}, u32[]{:S(2)}, u32[]{:S(2)}) collective-permute-start(f32[264,128]{1,0:T(8,128)S(1)} %get-tuple-element.14), channel_id=1, source_target_pairs={{0,2},{2,0},{4,6},{6,4},{1,3},{3,1},{5,7},{7,5},{8,10},{10,8},{12,... | collective-permute-start | bytes 405512 | tf_op jit(solution)/shard_map/ppermute | solution.py:293
  16.7 5.0 %collective-permute-start.5 = (f32[264,128]{1,0:T(8,128)S(1)}, f32[264,128]{1,0:T(8,128)S(1)}, u32[]{:S(2)}, u32[]{:S(2)}) collective-permute-start(f32[264,128]{1,0:T(8,128)S(1)} %get-tuple-element.15), channel_id=1, source_target_pairs={{0,6},{2,4},{4,0},{6,2},{1,7},{3,5},{5,1},{7,3},{8,14},{10,12},{12... | collective-permute-start | bytes 405512 | tf_op jit(solution)/shard_map/ppermute | solution.py:293
  21.8 1.4 %collective-permute-start.6 = (f32[256,128]{1,0:T(8,128)S(1)}, f32[256,128]{1,0:T(8,128)S(1)}, u32[]{:S(2)}, u32[]{:S(2)}) collective-permute-start(f32[256,128]{1,0:T(8,128)S(1)} %slice.4), channel_id=1, source_target_pairs={{0,1},{1,0},{2,3},{3,2},{4,5},{5,4},{6,7},{7,6},{8,9},{9,8},{10,11... | collective-permute-start | bytes 393224 | tf_op jit(solution)/shard_map/ppermute | solution.py:297
  23.9 5.9 %collective-permute-start.7 = (f32[128,128]{1,0:T(8,128)S(1)}, f32[128,128]{1,0:T(8,128)S(1)}, u32[]{:S(2)}, u32[]{:S(2)}) collective-permute-start(f32[128,128]{1,0:T(8,128)S(1)} %get-tuple-element.17.refs_0_), channel_id=1, source_target_pairs={{0,4},{2,6},{4,2},{6,0},{1,5},{3,7},{5,3},{7,1},{8,12},{10,14},{12... | collective-permute-start | bytes 196616 | tf_op jit(solution)/shard_map/ppermute | solution.py:234
  25.4 4.8 %collective-permute-start.8 = (f32[128,128]{1,0:T(8,128)S(1)}, f32[128,128]{1,0:T(8,128)S(1)}, u32[]{:S(2)}, u32[]{:S(2)}) collective-permute-start(f32[128,128]{1,0:T(8,128)S(1)} %get-tuple-element.17.refs_0_), channel_id=1, source_target_pairs={{0,2},{2,0},{4,6},{6,4},{1,3},{3,1},{5,7},{7,5},{8,10},{10,8},{12,... | collective-permute-start | bytes 196616 | tf_op jit(solution)/shard_map/ppermute | solution.py:234
  26.9 4.3 %collective-permute-start.9 = (f32[128,128]{1,0:T(8,128)S(1)}, f32[128,128]{1,0:T(8,128)S(1)}, u32[]{:S(2)}, u32[]{:S(2)}) collective-permute-start(f32[128,128]{1,0:T(8,128)S(1)} %get-tuple-element.17.refs_0_), channel_id=1, source_target_pairs={{0,6},{2,4},{4,0},{6,2},{1,7},{3,5},{5,1},{7,3},{8,14},{10,12},{12... | collective-permute-start | bytes 196616 | tf_op jit(solution)/shard_map/ppermute | solution.py:234
  31.2 6.2 %collective-permute-start.10 = (f32[128,128]{1,0:T(8,128)S(1)}, f32[128,128]{1,0:T(8,128)S(1)}, u32[]{:S(2)}, u32[]{:S(2)}) collective-permute-start(f32[128,128]{1,0:T(8,128)S(1)} %shard_map.85.refs_0_), channel_id=1, source_target_pairs={{0,16},{8,24},{16,8},{24,0},{1,17},{9,25},{17,9},{25,1},{2,18},{10... | collective-permute-start | bytes 196616 | tf_op jit(solution)/shard_map/ppermute | solution.py:234
  34.1 4.6 %collective-permute-start.11 = (f32[128,128]{1,0:T(8,128)S(1)}, f32[128,128]{1,0:T(8,128)S(1)}, u32[]{:S(2)}, u32[]{:S(2)}) collective-permute-start(f32[128,128]{1,0:T(8,128)S(1)} %shard_map.85.refs_0_), channel_id=1, source_target_pairs={{0,8},{8,0},{16,24},{24,16},{1,9},{9,1},{17,25},{25,17},{2,10},{10... | collective-permute-start | bytes 196616 | tf_op jit(solution)/shard_map/ppermute | solution.py:234
  34.1 5.2 %collective-permute-start.12 = (f32[128,128]{1,0:T(8,128)S(1)}, f32[128,128]{1,0:T(8,128)S(1)}, u32[]{:S(2)}, u32[]{:S(2)}) collective-permute-start(f32[128,128]{1,0:T(8,128)S(1)} %shard_map.85.refs_0_), channel_id=1, source_target_pairs={{0,24},{8,16},{16,0},{24,8},{1,25},{9,17},{17,1},{25,9},{2,26},{10... | collective-permute-start | bytes 196616 | tf_op jit(solution)/shard_map/ppermute | solution.py:234

commit v4 on v3

--- a/solution.py
+++ b/solution.py
@@ -10,7 +10,12 @@
 f32 = jnp.float32
 bf16 = jnp.bfloat16
 LONGEST = 8
-STEPS = [(2, 3, 1, 0), (1, 0, 3, 2), (3, 2, 0, 1)]
+STEPS = {
+    "gather": [(2, 3, 1, 0), (1, 0, 3, 2), (3, 2, 0, 1)],
+    "partials": [(3, 2, 1, 0), (1, 3, 0, 2), (2, 0, 3, 1)],
+    "rep": [(2, 3, 1, 0), (1, 0, 3, 2), (3, 2, 0, 1)],
+    "row": [(2, 3, 1, 0), (1, 0, 3, 2), (3, 2, 0, 1)],
+}
 
 
 def vmem(n):
@@ -45,36 +50,31 @@
         sources_ref[n + c] = low[c * tile : (c + 1) * tile]
 
 
-def add_tiles(j, tiles_ref, pos_ref, count_ref, sources_ref, acc_ref):
+def add_tiles(j, tiles_ref, list_ref, sources_ref, acc_ref):
     col_tiles = sources_ref.shape[0]
     spare = acc_ref.shape[0] - 1
-    listed = pos_ref[pl.ds(j, 1)]
-    live = jnp.sum(
-        jnp.where(lax.broadcasted_iota(jnp.int32, count_ref.shape, 1) == j, count_ref[...], 0)
-    )
+    listed = list_ref[pl.ds(j, 1)]
     for p in range(tiles_ref.shape[1]):
         t = listed[0, p]
-        i = jnp.where(p < live, t // col_tiles, spare)
+        i = jnp.where(t < 0, spare, t // col_tiles)
         acc_ref[i] += jnp.dot(
-            tiles_ref[j, p], sources_ref[t % col_tiles], preferred_element_type=f32
+            tiles_ref[j, p], sources_ref[jnp.maximum(t, 0) % col_tiles], preferred_element_type=f32
         )
 
 
-def own_kernel(tiles_ref, pos_ref, count_ref, x_ref, acc_ref, deg_ref, sources_ref):
+def own_kernel(tiles_ref, list_ref, x_ref, acc_ref, deg_ref, sources_ref):
     n_own, slots, tile, _ = tiles_ref.shape
     col_tiles = sources_ref.shape[0]
     row_tiles = acc_ref.shape[0] - 1
     acc_ref[...] = jnp.zeros_like(acc_ref)
     spread(x_ref[...], sources_ref, tile)
-    add_tiles(lax.axis_index("row"), tiles_ref, pos_ref, count_ref, sources_ref, acc_ref)
+    add_tiles(lax.axis_index("row"), tiles_ref, list_ref, sources_ref, acc_ref)
     lane = lax.broadcasted_iota(jnp.int32, (tile, 128), 1)
 
-    slot = lax.broadcasted_iota(jnp.int32, (1, slots), 1)
-    owner = lax.broadcasted_iota(jnp.int32, count_ref.shape, 1)
 
     def sums_of(j, total):
-        live = jnp.sum(jnp.where(owner == j, count_ref[...], 0), axis=1, keepdims=True)
-        rows = jnp.where(slot < live, pos_ref[pl.ds(j, 1)] // col_tiles, -1)
+        listed = list_ref[pl.ds(j, 1)]
+        rows = jnp.where(listed < 0, -1, listed // col_tiles)
         for p in range(slots):
             mark = (lane == rows[:, p : p + 1]).astype(f32).astype(bf16)
             total = total + jnp.dot(tiles_ref[j, p], mark, preferred_element_type=f32)
@@ -89,14 +89,14 @@
     deg_ref[...] = total.T[:row_tiles]
 
 
-def fold_kernel(step, tiles_ref, pos_ref, count_ref, block_ref, start_ref, acc_ref, sources_ref):
+def fold_kernel(step, tiles_ref, list_ref, block_ref, start_ref, acc_ref, sources_ref):
     tile = tiles_ref.shape[2]
     spread(block_ref[...], sources_ref, tile)
     j = sender(step, lax.axis_index("row"))
-    add_tiles(j, tiles_ref, pos_ref, count_ref, sources_ref, acc_ref)
-
-
-def fold_all_kernel(tiles_ref, pos_ref, count_ref, blocks_ref, start_ref, acc_ref, sources_ref):
+    add_tiles(j, tiles_ref, list_ref, sources_ref, acc_ref)
+
+
+def fold_all_kernel(tiles_ref, list_ref, blocks_ref, start_ref, acc_ref, sources_ref):
     n_own, _, tile, _ = tiles_ref.shape
     me = lax.axis_index("row")
 
@@ -104,7 +104,7 @@
     def _(k):
         j = lax.rem(me + k, n_own)
         spread(blocks_ref[j], sources_ref, tile)
-        add_tiles(j, tiles_ref, pos_ref, count_ref, sources_ref, acc_ref)
+        add_tiles(j, tiles_ref, list_ref, sources_ref, acc_ref)
 
 
 def send_kernel(acc_ref, deg_ref, *outs):
@@ -116,7 +116,7 @@
     n = col_tiles // 2
     left = lower_half((tile, width))
     for k, out in enumerate(outs):
-        q = rep if k == 0 else target(steps(n_rep)[k - 1], rep)
+        q = rep if k == 0 else target(steps(n_rep, "partials")[k - 1], rep)
         for c in range(n):
             top = acc_ref[q * col_tiles + c]
             low = acc_ref[q * col_tiles + n + c]
@@ -129,12 +129,12 @@
 
 def last_kernel(step, *refs):
     acc_ref, sources_ref = refs[-2:]
-    tiles_ref, pos_ref, count_ref, block_ref, start_ref, deg_ref = refs[:6]
+    tiles_ref, list_ref, block_ref, start_ref, deg_ref = refs[:5]
     acc_ref[...] = start_ref[...]
     spread(block_ref[...], sources_ref, tiles_ref.shape[2])
     j = sender(step, lax.axis_index("row"))
-    add_tiles(j, tiles_ref, pos_ref, count_ref, sources_ref, acc_ref)
-    send_kernel(acc_ref, deg_ref, *refs[6:-2])
+    add_tiles(j, tiles_ref, list_ref, sources_ref, acc_ref)
+    send_kernel(acc_ref, deg_ref, *refs[5:-2])
 
 
 def copy_kernel(x_ref, out_ref):
@@ -207,9 +207,9 @@
     )
 
 
-def steps(n):
+def steps(n, phase):
     if n == 4:
-        return STEPS
+        return STEPS[phase]
     return [tuple(i ^ k for i in range(n)) for k in range(n - 1, 0, -1)]
 
 
@@ -231,7 +231,7 @@
     n = lax.axis_size(axis)
     if n > LONGEST:
         return lax.psum(x, axis)
-    parts = [lax.ppermute(x, axis, list(enumerate(step))) for step in steps(n)]
+    parts = [lax.ppermute(x, axis, list(enumerate(step))) for step in steps(n, axis)]
     return call(sum_kernel, shape(*x.shape), vmem(n))(x, *parts)
 
 
@@ -242,7 +242,9 @@
     half = rows // 2
     n_rep = lax.axis_size("rep")
     row_tiles = n_rep * col_tiles
-    pos, counts, tiles = pair_tiles[0], pair_count, tile_vals[0]
+    tiles = tile_vals[0]
+    live = jnp.arange(slots)[None, :] < pair_count[0][:, None]
+    slots_of = jnp.where(live, pair_tiles[0], -1)
 
     packed = call(
         pack_kernel,
@@ -252,12 +254,12 @@
     )(features)
     if n_own <= LONGEST:
         blocks = [
-            lax.ppermute(packed, "row", list(enumerate(step))) for step in steps(n_own)
+            lax.ppermute(packed, "row", list(enumerate(step))) for step in steps(n_own, "gather")
         ]
     else:
         blocks = [lax.all_gather(packed, "row")]
     sources = pltpu.VMEM((col_tiles, tile, width), bf16)
-    lists = vmem(3)
+    lists = vmem(2)
     cost = pl.CostEstimate(flops=10**8, bytes_accessed=3 * 10**6, transcendentals=0)
     total_shape = shape(row_tiles + 1, tile, width)
     total, degrees = call(
@@ -266,32 +268,32 @@
         lists + vmem(1),
         [sources],
         cost,
-    )(tiles, pos, counts, packed)
+    )(tiles, slots_of, packed)
     messages = [shape(half + 8, width)] * n_rep
     if n_own <= LONGEST:
-        for step, block in zip(steps(n_own)[:-1], blocks):
+        for step, block in zip(steps(n_own, "gather")[:-1], blocks):
             total = call(
                 functools.partial(fold_kernel, step),
                 total_shape,
                 lists + vmem(2),
                 [sources],
                 cost,
-                {4: 0},
-            )(tiles, pos, counts, block, total)
+                {3: 0},
+            )(tiles, slots_of, block, total)
         mine, *sends = call(
-            functools.partial(last_kernel, steps(n_own)[-1]),
+            functools.partial(last_kernel, steps(n_own, "gather")[-1]),
             messages,
             lists + vmem(3),
             [pltpu.VMEM(total_shape.shape, f32), sources],
-        )(tiles, pos, counts, blocks[-1], total, degrees)
+        )(tiles, slots_of, blocks[-1], total, degrees)
     else:
-        total = call(fold_all_kernel, total_shape, lists + vmem(2), [sources], cost, {4: 0})(
-            tiles, pos, counts, blocks[0], total
+        total = call(fold_all_kernel, total_shape, lists + vmem(2), [sources], cost, {3: 0})(
+            tiles, slots_of, blocks[0], total
         )
         mine, *sends = call(send_kernel, messages, vmem(2))(total, degrees)
     parts = [
         lax.ppermute(sent, "rep", list(enumerate(step)))
-        for step, sent in zip(steps(n_rep), sends)
+        for step, sent in zip(steps(n_rep, "partials"), sends)
     ]
     mine = call(sum_kernel, messages[0], vmem(n_rep))(mine, *parts)
     other = lax.ppermute(mine[:half], "feat", [(0, 1), (1, 0)])

time: 40.3 us -> 39.5 us (0.980)
  local copies, waits for them, and re-layouts: 3.94 us -> 2.64 us
  other arithmetic: 0 us -> 0.75 us
    unnamed x16 -> x12, local copies, waits for them, and re-layouts: 3.93 us -> 2.63 us
    select_n x0 -> x1, other arithmetic: none -> 0.75 us  [shards(): slots_of = jnp.where(live, pair_tiles[0], -1)]
    ppermute x6, waiting for transfers between devices: 6.32 us -> 5.6 us  [total_over(): lax.ppermute(x, axis, list(enumerate(step)))]
    ppermute x3, waiting for transfers between devices: 0.87 us -> 1.52 us  [shards(): lax.ppermute(packed, 'row', list(enumerate(step)))]
  transfers between devices with their start and end apart: 13 -> 13, of which waited for: 11 -> 10; matrix products, arithmetic and copies ran while one was open for 0% -> 2% of each run, Pallas kernels for 5% -> 5%
where the time goes in v4:
time: 39.5 us; the launch traced here: 39.3 us
  starting transfers between devices  19.1 us (48%)
  waiting for transfers between devices  12 us (30%)
  Pallas kernels  4.12 us (10%)
  local copies, waits for them, and re-layouts  2.64 us (7%)
  other arithmetic  0.75 us (2%)
  between operations  0.71 us (2%)
    ppermute x6, starting transfers between devices, total_over(): lax.ppermute(x, axis, list(enumerate(step)))  8.45 us
    ppermute x3, starting transfers between devices, shards(): lax.ppermute(packed, 'row', list(enumerate(step)))  6 us
    ppermute x6, waiting for transfers between devices, total_over(): lax.ppermute(x, axis, list(enumerate(step)))  5.6 us
    ppermute x3, starting transfers between devices, shards(): lax.ppermute(sent, 'rep', list(enumerate(step)))  4.54 us
    ppermute x3, waiting for transfers between devices, shards(): lax.ppermute(sent, 'rep', list(enumerate(step)))  3.52 us
    unnamed x12, local copies, waits for them, and re-layouts  2.63 us
    ppermute x3, waiting for transfers between devices, shards(): lax.ppermute(packed, 'row', list(enumerate(step)))  1.52 us
    ppermute x1, waiting for transfers between devices, shards(): other = lax.ppermute(mine[:half], 'feat', [(0, 1), (1, 0)])  1.33 us
  transfers between devices with their start and end apart: 13, of which 10 were waited for; matrix products, arithmetic and copies ran while one was open for 2% of the time, Pallas kernels for 5%

profile of v4, /device:TPU:0, one launch (start us, length us, event | category | flops | bytes accessed | tf_op | source)
XLA Modules:
  0.0 39.3 jit_solution(10825208501112743168)
XLA Ops:
  0.6 0.0 copy-start.2
  0.6 0.9 %copy-done.2 = bf16[512,128]{1,0:T(8,128)(2,1)S(1)} copy-done((bf16[512,128]{1,0:T(8,128)(2,1)S(1)}, bf16[512,128]{1,0:T(8,128)(2,1)}, u32[]{:S(2)}) %copy-start.2) | copy-done | bytes 131096
  1.5 0.1 shard_map.77.x_ref
  1.6 4.1 %collective-permute-start.2 = (bf16[256,128]{1,0:T(8,128)(2,1)S(1)}, bf16[256,128]{1,0:T(8,128)(2,1)S(1)}, u32[]{:S(2)}, u32[]{:S(2)}) collective-permute-start(bf16[256,128]{1,0:T(8,128)(2,1)S(1)} %shard_map.77.x_ref), channel_id=1, source_target_pairs={{0,16},{8,24},{16,8},{24,0},{1,17},{9,25},{17,9},{25,1},{2,18},{10... | collective-permute-start | bytes 196616 | tf_op jit(solution)/shard_map/ppermute | solution.py:257
  5.7 1.6 %collective-permute-start.1 = (bf16[256,128]{1,0:T(8,128)(2,1)S(1)}, bf16[256,128]{1,0:T(8,128)(2,1)S(1)}, u32[]{:S(2)}, u32[]{:S(2)}) collective-permute-start(bf16[256,128]{1,0:T(8,128)(2,1)S(1)} %shard_map.77.x_ref), channel_id=1, source_target_pairs={{0,8},{8,0},{16,24},{24,16},{1,9},{9,1},{17,25},{25,17},{2,10},{10... | collective-permute-start | bytes 196616 | tf_op jit(solution)/shard_map/ppermute | solution.py:257
  7.3 0.3 collective-permute-start
  7.6 0.8 %bitcast_select_fusion.list_ref.refs_1_ = s32[4,8]{1,0:T(4,128)S(1)} fusion(s32[1,4,8]{2,1,0:T(4,128)} %param.8, s32[4]{0:T(128)} %bitcast.8), kind=kLoop, calls=%fused_computation | loop fusion | flops 64 | bytes 272 | tf_op jit(solution)/shard_map/jit(_where)/select_n | solution.py:247
  8.4 0.0 copy-start
  8.4 1.2 %copy-done = bf16[1,4,8,128,128]{4,3,2,1,0:T(8,128)(2,1)S(1)} copy-done((bf16[1,4,8,128,128]{4,3,2,1,0:T(8,128)(2,1)S(1)}, bf16[1,4,8,128,128]{4,3,2,1,0:T(8,128)(2,1)}, u32[]{:S(2)}) %copy-start) | copy-done | bytes 1048600
  9.6 0.0 copy-start.1
  9.6 0.7 %shard_map.78 = (f32[17,128,128]{2,1,0:T(8,128)S(1)}, f32[16,128]{1,0:T(8,128)S(1)}) custom-call(bf16[4,8,128,128]{3,2,1,0:T(8,128)(2,1)S(1)} %bitcast.4, s32[4,8]{1,0:T(4,128)S(1)} %bitcast_select_fusion.list_ref.refs_1_, bf16[256,128]{1,0:T(8,128)(2,1)S(1)} %shard_map.77.x_ref), custom_call_target="tpu_custom_call" | custom-call | flops 100000000 | bytes 3000000 | tf_op jit(solution)/shard_map/pallas_call | solution.py:265
  10.3 0.0 collective-permute-done.2.block_ref
  10.3 0.5 %copy-done.1 = bf16[1,4,8,128,128]{4,3,2,1,0:T(8,128)(2,1)S(1)} copy-done((bf16[1,4,8,128,128]{4,3,2,1,0:T(8,128)(2,1)S(1)}, bf16[1,4,8,128,128]{4,3,2,1,0:T(8,128)(2,1)}, u32[]{:S(2)}) %copy-start.1) | copy-done | bytes 1048600
  10.8 0.3 shard_map.79.start_ref
  11.2 0.0 collective-permute-done.1.block_ref
  11.2 0.3 shard_map.80.refs_3_
  11.5 1.5 %collective-permute-done.refs_2_ = bf16[256,128]{1,0:T(8,128)(2,1)S(1)} collective-permute-done((bf16[256,128]{1,0:T(8,128)(2,1)S(1)}, bf16[256,128]{1,0:T(8,128)(2,1)S(1)}, u32[]{:S(2)}, u32[]{:S(2)}) %collective-permute-start) | collective-permute-done | bytes 65568 | tf_op jit(solution)/shard_map/ppermute | solution.py:257
  13.1 0.0 copy-start.3
  13.1 0.0 copy-start.4
  13.1 0.0 copy-start.5
  13.1 0.5 %shard_map.81 = (f32[264,128]{1,0:T(8,128)S(1)}, f32[264,128]{1,0:T(8,128)S(1)}, f32[264,128]{1,0:T(8,128)S(1)}, f32[264,128]{1,0:T(8,128)S(1)}) custom-call(bf16[4,8,128,128]{3,2,1,0:T(8,128)(2,1)S(1)} %bitcast.7, s32[4,8]{1,0:T(4,128)S(1)} %bitcast_select_fusion.list_ref.refs_1_, bf16[256,128]{1,0:T(8,128)(2,1)S(1)} %collective-permute-done.refs_2_, ...), custom_call_target="tpu_custom_call" | custom-call | tf_op jit(solution)/shard_map/pallas_call | solution.py:283
  13.6 2.5 %collective-permute-start.3 = (f32[264,128]{1,0:T(8,128)S(1)}, f32[264,128]{1,0:T(8,128)S(1)}, u32[]{:S(2)}, u32[]{:S(2)}) collective-permute-start(f32[264,128]{1,0:T(8,128)S(1)} %get-tuple-element.13), channel_id=1, source_target_pairs={{0,6},{2,4},{4,2},{6,0},{1,7},{3,5},{5,3},{7,1},{8,14},{10,12},{12... | collective-permute-start | bytes 405512 | tf_op jit(solution)/shard_map/ppermute | solution.py:295
  16.1 0.5 %collective-permute-start.4 = (f32[264,128]{1,0:T(8,128)S(1)}, f32[264,128]{1,0:T(8,128)S(1)}, u32[]{:S(2)}, u32[]{:S(2)}) collective-permute-start(f32[264,128]{1,0:T(8,128)S(1)} %get-tuple-element.14), channel_id=1, source_target_pairs={{0,2},{2,6},{4,0},{6,4},{1,3},{3,7},{5,1},{7,5},{8,10},{10,14},{12... | collective-permute-start | bytes 405512 | tf_op jit(solution)/shard_map/ppermute | solution.py:295
  16.7 1.5 %collective-permute-start.5 = (f32[264,128]{1,0:T(8,128)S(1)}, f32[264,128]{1,0:T(8,128)S(1)}, u32[]{:S(2)}, u32[]{:S(2)}) collective-permute-start(f32[264,128]{1,0:T(8,128)S(1)} %get-tuple-element.15), channel_id=1, source_target_pairs={{0,4},{2,0},{4,6},{6,2},{1,5},{3,1},{5,7},{7,3},{8,12},{10,8},{12,... | collective-permute-start | bytes 405512 | tf_op jit(solution)/shard_map/ppermute | solution.py:295
  18.1 1.6 %collective-permute-done.3.refs_1_ = f32[264,128]{1,0:T(8,128)S(1)} collective-permute-done((f32[264,128]{1,0:T(8,128)S(1)}, f32[264,128]{1,0:T(8,128)S(1)}, u32[]{:S(2)}, u32[]{:S(2)}) %collective-permute-start.3) | collective-permute-done | bytes 135200 | tf_op jit(solution)/shard_map/ppermute | solution.py:295
  19.7 1.4 %collective-permute-done.4.refs_2_ = f32[264,128]{1,0:T(8,128)S(1)} collective-permute-done((f32[264,128]{1,0:T(8,128)S(1)}, f32[264,128]{1,0:T(8,128)S(1)}, u32[]{:S(2)}, u32[]{:S(2)}) %collective-permute-start.4) | collective-permute-done | bytes 135200 | tf_op jit(solution)/shard_map/ppermute | solution.py:295
  21.2 0.5 %collective-permute-done.5.refs_3_ = f32[264,128]{1,0:T(8,128)S(1)} collective-permute-done((f32[264,128]{1,0:T(8,128)S(1)}, f32[264,128]{1,0:T(8,128)S(1)}, u32[]{:S(2)}, u32[]{:S(2)}) %collective-permute-start.5) | collective-permute-done | bytes 135200 | tf_op jit(solution)/shard_map/ppermute | solution.py:295
  21.7 0.1 shard_map.82.mine_ref
  21.7 0.1 collective-permute-start.6
  21.8 1.3 %collective-permute-done.6.other_ref = f32[256,128]{1,0:T(8,128)S(1)} collective-permute-done((f32[256,128]{1,0:T(8,128)S(1)}, f32[256,128]{1,0:T(8,128)S(1)}, u32[]{:S(2)}, u32[]{:S(2)}) %collective-permute-start.6) | collective-permute-done | bytes 131104 | tf_op jit(solution)/shard_map/ppermute | solution.py:299
  23.2 0.0 copy-done.3
  23.2 0.0 copy-done.4
  23.2 0.0 copy-done.5
  23.2 0.7 %shard_map.83 = (bf16[512,128]{1,0:T(8,128)(2,1)S(1)}, f32[128,128]{1,0:T(8,128)S(1)}) custom-call(f32[264,128]{1,0:T(8,128)S(1)} %shard_map.82.mine_ref, f32[256,128]{1,0:T(8,128)S(1)} %collective-permute-done.6.other_ref, bf16[512,128]{1,0:T(8,128)(2,1)S(1)} %copy-done.3, bf16[128,128]{1,0:T(8,128)(2,1)S(1)} %copy-done.5, bf16[512,128]{1,0:T(8,128)(2,1)S(1)} %copy-done.4), custom_call_target="tpu_custom_call" | custom-call | tf_op jit(solution)/shard_map/pallas_call | solution.py:301
  23.9 1.5 %collective-permute-start.7 = (f32[128,128]{1,0:T(8,128)S(1)}, f32[128,128]{1,0:T(8,128)S(1)}, u32[]{:S(2)}, u32[]{:S(2)}) collective-permute-start(f32[128,128]{1,0:T(8,128)S(1)} %get-tuple-element.17.refs_0_), channel_id=1, source_target_pairs={{0,4},{2,6},{4,2},{6,0},{1,5},{3,7},{5,3},{7,1},{8,12},{10,14},{12... | collective-permute-start | bytes 196616 | tf_op jit(solution)/shard_map/ppermute | solution.py:234
  25.4 0.5 %collective-permute-start.8 = (f32[128,128]{1,0:T(8,128)S(1)}, f32[128,128]{1,0:T(8,128)S(1)}, u32[]{:S(2)}, u32[]{:S(2)}) collective-permute-start(f32[128,128]{1,0:T(8,128)S(1)} %get-tuple-element.17.refs_0_), channel_id=1, source_target_pairs={{0,2},{2,0},{4,6},{6,4},{1,3},{3,1},{5,7},{7,5},{8,10},{10,8},{12,... | collective-permute-start | bytes 196616 | tf_op jit(solution)/shard_map/ppermute | solution.py:234
  25.9 2.1 %collective-permute-start.9 = (f32[128,128]{1,0:T(8,128)S(1)}, f32[128,128]{1,0:T(8,128)S(1)}, u32[]{:S(2)}, u32[]{:S(2)}) collective-permute-start(f32[128,128]{1,0:T(8,128)S(1)} %get-tuple-element.17.refs_0_), channel_id=1, source_target_pairs={{0,6},{2,4},{4,0},{6,2},{1,7},{3,5},{5,1},{7,3},{8,14},{10,12},{12... | collective-permute-start | bytes 196616 | tf_op jit(solution)/shard_map/ppermute | solution.py:234
  28.0 1.7 %collective-permute-done.7.refs_1_ = f32[128,128]{1,0:T(8,128)S(1)} collective-permute-done((f32[128,128]{1,0:T(8,128)S(1)}, f32[128,128]{1,0:T(8,128)S(1)}, u32[]{:S(2)}, u32[]{:S(2)}) %collective-permute-start.7) | collective-permute-done | bytes 65568 | tf_op jit(solution)/shard_map/ppermute | solution.py:234
  29.7 0.6 %collective-permute-done.8.refs_2_ = f32[128,128]{1,0:T(8,128)S(1)} collective-permute-done((f32[128,128]{1,0:T(8,128)S(1)}, f32[128,128]{1,0:T(8,128)S(1)}, u32[]{:S(2)}, u32[]{:S(2)}) %collective-permute-start.8) | collective-permute-done | bytes 65568 | tf_op jit(solution)/shard_map/ppermute | solution.py:234
  30.3 0.0 collective-permute-done.9.refs_3_
  30.4 2.8 %collective-permute-start.10 = (f32[128,128]{1,0:T(8,128)S(1)}, f32[128,128]{1,0:T(8,128)S(1)}, u32[]{:S(2)}, u32[]{:S(2)}) collective-permute-start(f32[128,128]{1,0:T(8,128)S(1)} %shard_map.85.refs_0_), channel_id=1, source_target_pairs={{0,16},{8,24},{16,8},{24,0},{1,17},{9,25},{17,9},{25,1},{2,18},{10... | collective-permute-start | bytes 196616 | tf_op jit(solution)/shard_map/ppermute | solution.py:234
  33.2 0.1 collective-permute-start.11
  33.3 1.4 %collective-permute-start.12 = (f32[128,128]{1,0:T(8,128)S(1)}, f32[128,128]{1,0:T(8,128)S(1)}, u32[]{:S(2)}, u32[]{:S(2)}) collective-permute-start(f32[128,128]{1,0:T(8,128)S(1)} %shard_map.85.refs_0_), channel_id=1, source_target_pairs={{0,24},{8,16},{16,0},{24,8},{1,25},{9,17},{17,1},{25,9},{2,26},{10... | collective-permute-start | bytes 196616 | tf_op jit(solution)/shard_map/ppermute | solution.py:234
  34.7 0.7 %shard_map.84 = bf16[512,128]{1,0:T(8,128)(2,1)} custom-call(bf16[512,128]{1,0:T(8,128)(2,1)S(1)} %get-tuple-element.16.x_ref), custom_call_target="tpu_custom_call" | custom-call | tf_op jit(solution)/shard_map/pallas_call | solution.py:308
  35.4 1.2 %collective-permute-done.10.refs_1_ = f32[128,128]{1,0:T(8,128)S(1)} collective-permute-done((f32[128,128]{1,0:T(8,128)S(1)}, f32[128,128]{1,0:T(8,128)S(1)}, u32[]{:S(2)}, u32[]{:S(2)}) %collective-permute-start.10) | collective-permute-done | bytes 65568 | tf_op jit(solution)/shard_map/ppermute | solution.py:234
  36.6 1.3 %collective-permute-done.11.refs_2_ = f32[128,128]{1,0:T(8,128)S(1)} collective-permute-done((f32[128,128]{1,0:T(8,128)S(1)}, f32[128,128]{1,0:T(8,128)S(1)}, u32[]{:S(2)}, u32[]{:S(2)}) %collective-permute-start.11) | collective-permute-done | bytes 65568 | tf_op jit(solution)/shard_map/ppermute | solution.py:234
  37.9 0.7 %collective-permute-done.12.refs_3_ = f32[128,128]{1,0:T(8,128)S(1)} collective-permute-done((f32[128,128]{1,0:T(8,128)S(1)}, f32[128,128]{1,0:T(8,128)S(1)}, u32[]{:S(2)}, u32[]{:S(2)}) %collective-permute-start.12) | collective-permute-done | bytes 65568 | tf_op jit(solution)/shard_map/ppermute | solution.py:234
  38.6 0.6 %shard_map.86 = f32[128,128]{1,0:T(8,128)} custom-call(f32[128,128]{1,0:T(8,128)S(1)} %shard_map.85.refs_0_, f32[128,128]{1,0:T(8,128)S(1)} %collective-permute-done.10.refs_1_, f32[128,128]{1,0:T(8,128)S(1)} %collective-permute-done.11.refs_2_, f32[128,128]{1,0:T(8,128)S(1)} %collective-permute-done.12.refs_3_), custom_call_target="tpu_custom_call" | custom-call | tf_op jit(solution)/shard_map/pallas_call | solution.py:235
  (2 shorter events, 0.0 us)
Async XLA Ops:
  0.6 0.9 %copy-start.2 = (bf16[512,128]{1,0:T(8,128)(2,1)S(1)}, bf16[512,128]{1,0:T(8,128)(2,1)}, u32[]{:S(2)}) copy-start(bf16[512,128]{1,0:T(8,128)(2,1)} %x_ref.3) | copy-start | bytes 393220
  1.6 8.7 %collective-permute-start.2 = (bf16[256,128]{1,0:T(8,128)(2,1)S(1)}, bf16[256,128]{1,0:T(8,128)(2,1)S(1)}, u32[]{:S(2)}, u32[]{:S(2)}) collective-permute-start(bf16[256,128]{1,0:T(8,128)(2,1)S(1)} %shard_map.77.x_ref), channel_id=1, source_target_pairs={{0,16},{8,24},{16,8},{24,0},{1,17},{9,25},{17,9},{25,1},{2,18},{10... | collective-permute-start | bytes 196616 | tf_op jit(solution)/shard_map/ppermute | solution.py:257
  5.7 5.5 %collective-permute-start.1 = (bf16[256,128]{1,0:T(8,128)(2,1)S(1)}, bf16[256,128]{1,0:T(8,128)(2,1)S(1)}, u32[]{:S(2)}, u32[]{:S(2)}) collective-permute-start(bf16[256,128]{1,0:T(8,128)(2,1)S(1)} %shard_map.77.x_ref), channel_id=1, source_target_pairs={{0,8},{8,0},{16,24},{24,16},{1,9},{9,1},{17,25},{25,17},{2,10},{10... | collective-permute-start | bytes 196616 | tf_op jit(solution)/shard_map/ppermute | solution.py:257
  7.3 5.8 %collective-permute-start = (bf16[256,128]{1,0:T(8,128)(2,1)S(1)}, bf16[256,128]{1,0:T(8,128)(2,1)S(1)}, u32[]{:S(2)}, u32[]{:S(2)}) collective-permute-start(bf16[256,128]{1,0:T(8,128)(2,1)S(1)} %shard_map.77.x_ref), channel_id=1, source_target_pairs={{0,24},{8,16},{16,0},{24,8},{1,25},{9,17},{17,1},{25,9},{2,26},{10... | collective-permute-start | bytes 196616 | tf_op jit(solution)/shard_map/ppermute | solution.py:257
  8.4 1.2 %copy-start = (bf16[1,4,8,128,128]{4,3,2,1,0:T(8,128)(2,1)S(1)}, bf16[1,4,8,128,128]{4,3,2,1,0:T(8,128)(2,1)}, u32[]{:S(2)}) copy-start(bf16[1,4,8,128,128]{4,3,2,1,0:T(8,128)(2,1)} %param.10) | copy-start | bytes 3145732
  9.6 1.2 %copy-start.1 = (bf16[1,4,8,128,128]{4,3,2,1,0:T(8,128)(2,1)S(1)}, bf16[1,4,8,128,128]{4,3,2,1,0:T(8,128)(2,1)}, u32[]{:S(2)}) copy-start(bf16[1,4,8,128,128]{4,3,2,1,0:T(8,128)(2,1)} %param.10) | copy-start | bytes 3145732
  13.1 10.1 %copy-start.3 = (bf16[512,128]{1,0:T(8,128)(2,1)S(1)}, bf16[512,128]{1,0:T(8,128)(2,1)}, u32[]{:S(2)}) copy-start(bf16[512,128]{1,0:T(8,128)(2,1)} %x_ref.3) | copy-start | bytes 393220
  13.1 10.1 %copy-start.4 = (bf16[512,128]{1,0:T(8,128)(2,1)S(1)}, bf16[512,128]{1,0:T(8,128)(2,1)}, u32[]{:S(2)}) copy-start(bf16[512,128]{1,0:T(8,128)(2,1)} %cot_ref.1) | copy-start | bytes 393220
  13.1 10.1 %copy-start.5 = (bf16[128,128]{1,0:T(8,128)(2,1)S(1)}, bf16[128,128]{1,0:T(8,128)(2,1)}, u32[]{:S(2)}) copy-start(bf16[128,128]{1,0:T(8,128)(2,1)} %w_ref.1) | copy-start | bytes 98308
  13.6 6.1 %collective-permute-start.3 = (f32[264,128]{1,0:T(8,128)S(1)}, f32[264,128]{1,0:T(8,128)S(1)}, u32[]{:S(2)}, u32[]{:S(2)}) collective-permute-start(f32[264,128]{1,0:T(8,128)S(1)} %get-tuple-element.13), channel_id=1, source_target_pairs={{0,6},{2,4},{4,2},{6,0},{1,7},{3,5},{5,3},{7,1},{8,14},{10,12},{12... | collective-permute-start | bytes 405512 | tf_op jit(solution)/shard_map/ppermute | solution.py:295
  16.1 5.1 %collective-permute-start.4 = (f32[264,128]{1,0:T(8,128)S(1)}, f32[264,128]{1,0:T(8,128)S(1)}, u32[]{:S(2)}, u32[]{:S(2)}) collective-permute-start(f32[264,128]{1,0:T(8,128)S(1)} %get-tuple-element.14), channel_id=1, source_target_pairs={{0,2},{2,6},{4,0},{6,4},{1,3},{3,7},{5,1},{7,5},{8,10},{10,14},{12... | collective-permute-start | bytes 405512 | tf_op jit(solution)/shard_map/ppermute | solution.py:295
  16.7 5.0 %collective-permute-start.5 = (f32[264,128]{1,0:T(8,128)S(1)}, f32[264,128]{1,0:T(8,128)S(1)}, u32[]{:S(2)}, u32[]{:S(2)}) collective-permute-start(f32[264,128]{1,0:T(8,128)S(1)} %get-tuple-element.15), channel_id=1, source_target_pairs={{0,4},{2,0},{4,6},{6,2},{1,5},{3,1},{5,7},{7,3},{8,12},{10,8},{12,... | collective-permute-start | bytes 405512 | tf_op jit(solution)/shard_map/ppermute | solution.py:295
  21.7 1.4 %collective-permute-start.6 = (f32[256,128]{1,0:T(8,128)S(1)}, f32[256,128]{1,0:T(8,128)S(1)}, u32[]{:S(2)}, u32[]{:S(2)}) collective-permute-start(f32[256,128]{1,0:T(8,128)S(1)} %slice.4), channel_id=1, source_target_pairs={{0,1},{1,0},{2,3},{3,2},{4,5},{5,4},{6,7},{7,6},{8,9},{9,8},{10,11... | collective-permute-start | bytes 393224 | tf_op jit(solution)/shard_map/ppermute | solution.py:299
  23.9 5.9 %collective-permute-start.7 = (f32[128,128]{1,0:T(8,128)S(1)}, f32[128,128]{1,0:T(8,128)S(1)}, u32[]{:S(2)}, u32[]{:S(2)}) collective-permute-start(f32[128,128]{1,0:T(8,128)S(1)} %get-tuple-element.17.refs_0_), channel_id=1, source_target_pairs={{0,4},{2,6},{4,2},{6,0},{1,5},{3,7},{5,3},{7,1},{8,12},{10,14},{12... | collective-permute-start | bytes 196616 | tf_op jit(solution)/shard_map/ppermute | solution.py:234
  25.4 4.9 %collective-permute-start.8 = (f32[128,128]{1,0:T(8,128)S(1)}, f32[128,128]{1,0:T(8,128)S(1)}, u32[]{:S(2)}, u32[]{:S(2)}) collective-permute-start(f32[128,128]{1,0:T(8,128)S(1)} %get-tuple-element.17.refs_0_), channel_id=1, source_target_pairs={{0,2},{2,0},{4,6},{6,4},{1,3},{3,1},{5,7},{7,5},{8,10},{10,8},{12,... | collective-permute-start | bytes 196616 | tf_op jit(solution)/shard_map/ppermute | solution.py:234
  25.9 4.4 %collective-permute-start.9 = (f32[128,128]{1,0:T(8,128)S(1)}, f32[128,128]{1,0:T(8,128)S(1)}, u32[]{:S(2)}, u32[]{:S(2)}) collective-permute-start(f32[128,128]{1,0:T(8,128)S(1)} %get-tuple-element.17.refs_0_), channel_id=1, source_target_pairs={{0,6},{2,4},{4,0},{6,2},{1,7},{3,5},{5,1},{7,3},{8,14},{10,12},{12... | collective-permute-start | bytes 196616 | tf_op jit(solution)/shard_map/ppermute | solution.py:234
  30.4 6.2 %collective-permute-start.10 = (f32[128,128]{1,0:T(8,128)S(1)}, f32[128,128]{1,0:T(8,128)S(1)}, u32[]{:S(2)}, u32[]{:S(2)}) collective-permute-start(f32[128,128]{1,0:T(8,128)S(1)} %shard_map.85.refs_0_), channel_id=1, source_target_pairs={{0,16},{8,24},{16,8},{24,0},{1,17},{9,25},{17,9},{25,1},{2,18},{10... | collective-permute-start | bytes 196616 | tf_op jit(solution)/shard_map/ppermute | solution.py:234
  33.2 4.7 %collective-permute-start.11 = (f32[128,128]{1,0:T(8,128)S(1)}, f32[128,128]{1,0:T(8,128)S(1)}, u32[]{:S(2)}, u32[]{:S(2)}) collective-permute-start(f32[128,128]{1,0:T(8,128)S(1)} %shard_map.85.refs_0_), channel_id=1, source_target_pairs={{0,8},{8,0},{16,24},{24,16},{1,9},{9,1},{17,25},{25,17},{2,10},{10... | collective-permute-start | bytes 196616 | tf_op jit(solution)/shard_map/ppermute | solution.py:234
  33.3 5.3 %collective-permute-start.12 = (f32[128,128]{1,0:T(8,128)S(1)}, f32[128,128]{1,0:T(8,128)S(1)}, u32[]{:S(2)}, u32[]{:S(2)}) collective-permute-start(f32[128,128]{1,0:T(8,128)S(1)} %shard_map.85.refs_0_), channel_id=1, source_target_pairs={{0,24},{8,16},{16,0},{24,8},{1,25},{9,17},{17,1},{25,9},{2,26},{10... | collective-permute-start | bytes 196616 | tf_op jit(solution)/shard_map/ppermute | solution.py:234

commit v5 on v4

--- a/solution.py
+++ b/solution.py
@@ -173,20 +173,23 @@
         [jnp.broadcast_to(turned[:, c : c + 1], (tile, 128)) for c in range(2 * half // tile)],
         axis=0,
     )
-    high, rest = split(agg)
+    both = jnp.concatenate(split(agg), axis=1)
     w = w_ref[...]
-    preact = jnp.dot(high, w, preferred_element_type=f32)
-    preact = scale * (preact + jnp.dot(rest, w, preferred_element_type=f32))
+    preact = scale * jnp.dot(both, jnp.concatenate([w, w], axis=0), preferred_element_type=f32)
     sig = 1.0 / (1.0 + jnp.exp(-preact))
     act_ref[...] = (preact * sig).astype(bf16)
     slopes = scale * cot_ref[...].astype(f32) * sig * (1.0 + preact * (1.0 - sig))
-    s_high, s_rest = split(slopes)
-
-    def turned_dot(a, b):
-        return lax.dot_general(a, b, (((0,), (0,)), ((), ())), preferred_element_type=f32)
-
+    width = agg.shape[1]
+    hidden = slopes.shape[1]
+    terms = lax.dot_general(
+        both,
+        jnp.concatenate(split(slopes), axis=1),
+        (((0,), (0,)), ((), ())),
+        preferred_element_type=f32,
+    )
     grad_ref[...] = (
-        turned_dot(high, s_high) + turned_dot(high, s_rest) + turned_dot(rest, s_high)
+        terms[:width, :hidden] + terms[:width, hidden:] + terms[width:, :hidden]
+        + terms[width:, hidden:]
     )
 
 

time: 39.5 us -> 39.4 us (level)
  no operation moved by 1% of the time
where the time goes in v5:
time: 39.4 us; the launch traced here: 39.2 us
  starting transfers between devices  19.1 us (48%)
  waiting for transfers between devices  12 us (30%)
  Pallas kernels  4.01 us (10%)
  local copies, waits for them, and re-layouts  2.64 us (7%)
  other arithmetic  0.75 us (2%)
  between operations  0.72 us (2%)
    ppermute x6, starting transfers between devices, total_over(): lax.ppermute(x, axis, list(enumerate(step)))  8.44 us
    ppermute x3, starting transfers between devices, shards(): lax.ppermute(packed, 'row', list(enumerate(step)))  6 us
    ppermute x6, waiting for transfers between devices, total_over(): lax.ppermute(x, axis, list(enumerate(step)))  5.61 us
    ppermute x3, starting transfers between devices, shards(): lax.ppermute(sent, 'rep', list(enumerate(step)))  4.54 us
    ppermute x3, waiting for transfers between devices, shards(): lax.ppermute(sent, 'rep', list(enumerate(step)))  3.52 us
    unnamed x12, local copies, waits for them, and re-layouts  2.63 us
    ppermute x3, waiting for transfers between devices, shards(): lax.ppermute(packed, 'row', list(enumerate(step)))  1.52 us
    ppermute x1, waiting for transfers between devices, shards(): other = lax.ppermute(mine[:half], 'feat', [(0, 1), (1, 0)])  1.33 us
  transfers between devices with their start and end apart: 13, of which 10 were waited for; matrix products, arithmetic and copies ran while one was open for 2% of the time, Pallas kernels for 5%

profile of v5, /device:TPU:0, one launch (start us, length us, event | category | flops | bytes accessed | tf_op | source)
XLA Modules:
  0.0 39.2 jit_solution(12871109669733659907)
XLA Ops:
  0.6 0.0 copy-start.2
  0.6 0.9 %copy-done.2 = bf16[512,128]{1,0:T(8,128)(2,1)S(1)} copy-done((bf16[512,128]{1,0:T(8,128)(2,1)S(1)}, bf16[512,128]{1,0:T(8,128)(2,1)}, u32[]{:S(2)}) %copy-start.2) | copy-done | bytes 131096
  1.5 0.1 shard_map.77.x_ref
  1.6 4.1 %collective-permute-start.2 = (bf16[256,128]{1,0:T(8,128)(2,1)S(1)}, bf16[256,128]{1,0:T(8,128)(2,1)S(1)}, u32[]{:S(2)}, u32[]{:S(2)}) collective-permute-start(bf16[256,128]{1,0:T(8,128)(2,1)S(1)} %shard_map.77.x_ref), channel_id=1, source_target_pairs={{0,16},{8,24},{16,8},{24,0},{1,17},{9,25},{17,9},{25,1},{2,18},{10... | collective-permute-start | bytes 196616 | tf_op jit(solution)/shard_map/ppermute | solution.py:260
  5.7 1.6 %collective-permute-start.1 = (bf16[256,128]{1,0:T(8,128)(2,1)S(1)}, bf16[256,128]{1,0:T(8,128)(2,1)S(1)}, u32[]{:S(2)}, u32[]{:S(2)}) collective-permute-start(bf16[256,128]{1,0:T(8,128)(2,1)S(1)} %shard_map.77.x_ref), channel_id=1, source_target_pairs={{0,8},{8,0},{16,24},{24,16},{1,9},{9,1},{17,25},{25,17},{2,10},{10... | collective-permute-start | bytes 196616 | tf_op jit(solution)/shard_map/ppermute | solution.py:260
  7.3 0.3 collective-permute-start
  7.6 0.8 %bitcast_select_fusion.list_ref.refs_1_ = s32[4,8]{1,0:T(4,128)S(1)} fusion(s32[1,4,8]{2,1,0:T(4,128)} %param.8, s32[4]{0:T(128)} %bitcast.8), kind=kLoop, calls=%fused_computation | loop fusion | flops 64 | bytes 272 | tf_op jit(solution)/shard_map/jit(_where)/select_n | solution.py:250
  8.4 0.0 copy-start
  8.4 1.2 %copy-done = bf16[1,4,8,128,128]{4,3,2,1,0:T(8,128)(2,1)S(1)} copy-done((bf16[1,4,8,128,128]{4,3,2,1,0:T(8,128)(2,1)S(1)}, bf16[1,4,8,128,128]{4,3,2,1,0:T(8,128)(2,1)}, u32[]{:S(2)}) %copy-start) | copy-done | bytes 1048600
  9.6 0.0 copy-start.1
  9.6 0.7 %shard_map.78 = (f32[17,128,128]{2,1,0:T(8,128)S(1)}, f32[16,128]{1,0:T(8,128)S(1)}) custom-call(bf16[4,8,128,128]{3,2,1,0:T(8,128)(2,1)S(1)} %bitcast.4, s32[4,8]{1,0:T(4,128)S(1)} %bitcast_select_fusion.list_ref.refs_1_, bf16[256,128]{1,0:T(8,128)(2,1)S(1)} %shard_map.77.x_ref), custom_call_target="tpu_custom_call" | custom-call | flops 100000000 | bytes 3000000 | tf_op jit(solution)/shard_map/pallas_call | solution.py:268
  10.3 0.0 collective-permute-done.2.block_ref
  10.3 0.5 %copy-done.1 = bf16[1,4,8,128,128]{4,3,2,1,0:T(8,128)(2,1)S(1)} copy-done((bf16[1,4,8,128,128]{4,3,2,1,0:T(8,128)(2,1)S(1)}, bf16[1,4,8,128,128]{4,3,2,1,0:T(8,128)(2,1)}, u32[]{:S(2)}) %copy-start.1) | copy-done | bytes 1048600
  10.8 0.3 shard_map.79.start_ref
  11.2 0.0 collective-permute-done.1.block_ref
  11.2 0.3 shard_map.80.refs_3_
  11.5 1.5 %collective-permute-done.refs_2_ = bf16[256,128]{1,0:T(8,128)(2,1)S(1)} collective-permute-done((bf16[256,128]{1,0:T(8,128)(2,1)S(1)}, bf16[256,128]{1,0:T(8,128)(2,1)S(1)}, u32[]{:S(2)}, u32[]{:S(2)}) %collective-permute-start) | collective-permute-done | bytes 65568 | tf_op jit(solution)/shard_map/ppermute | solution.py:260
  13.1 0.0 copy-start.3
  13.1 0.0 copy-start.4
  13.1 0.0 copy-start.5
  13.1 0.5 %shard_map.81 = (f32[264,128]{1,0:T(8,128)S(1)}, f32[264,128]{1,0:T(8,128)S(1)}, f32[264,128]{1,0:T(8,128)S(1)}, f32[264,128]{1,0:T(8,128)S(1)}) custom-call(bf16[4,8,128,128]{3,2,1,0:T(8,128)(2,1)S(1)} %bitcast.7, s32[4,8]{1,0:T(4,128)S(1)} %bitcast_select_fusion.list_ref.refs_1_, bf16[256,128]{1,0:T(8,128)(2,1)S(1)} %collective-permute-done.refs_2_, ...), custom_call_target="tpu_custom_call" | custom-call | tf_op jit(solution)/shard_map/pallas_call | solution.py:286
  13.6 2.5 %collective-permute-start.3 = (f32[264,128]{1,0:T(8,128)S(1)}, f32[264,128]{1,0:T(8,128)S(1)}, u32[]{:S(2)}, u32[]{:S(2)}) collective-permute-start(f32[264,128]{1,0:T(8,128)S(1)} %get-tuple-element.13), channel_id=1, source_target_pairs={{0,6},{2,4},{4,2},{6,0},{1,7},{3,5},{5,3},{7,1},{8,14},{10,12},{12... | collective-permute-start | bytes 405512 | tf_op jit(solution)/shard_map/ppermute | solution.py:298
  16.1 0.5 %collective-permute-start.4 = (f32[264,128]{1,0:T(8,128)S(1)}, f32[264,128]{1,0:T(8,128)S(1)}, u32[]{:S(2)}, u32[]{:S(2)}) collective-permute-start(f32[264,128]{1,0:T(8,128)S(1)} %get-tuple-element.14), channel_id=1, source_target_pairs={{0,2},{2,6},{4,0},{6,4},{1,3},{3,7},{5,1},{7,5},{8,10},{10,14},{12... | collective-permute-start | bytes 405512 | tf_op jit(solution)/shard_map/ppermute | solution.py:298
  16.7 1.5 %collective-permute-start.5 = (f32[264,128]{1,0:T(8,128)S(1)}, f32[264,128]{1,0:T(8,128)S(1)}, u32[]{:S(2)}, u32[]{:S(2)}) collective-permute-start(f32[264,128]{1,0:T(8,128)S(1)} %get-tuple-element.15), channel_id=1, source_target_pairs={{0,4},{2,0},{4,6},{6,2},{1,5},{3,1},{5,7},{7,3},{8,12},{10,8},{12,... | collective-permute-start | bytes 405512 | tf_op jit(solution)/shard_map/ppermute | solution.py:298
  18.1 1.6 %collective-permute-done.3.refs_1_ = f32[264,128]{1,0:T(8,128)S(1)} collective-permute-done((f32[264,128]{1,0:T(8,128)S(1)}, f32[264,128]{1,0:T(8,128)S(1)}, u32[]{:S(2)}, u32[]{:S(2)}) %collective-permute-start.3) | collective-permute-done | bytes 135200 | tf_op jit(solution)/shard_map/ppermute | solution.py:298
  19.7 1.4 %collective-permute-done.4.refs_2_ = f32[264,128]{1,0:T(8,128)S(1)} collective-permute-done((f32[264,128]{1,0:T(8,128)S(1)}, f32[264,128]{1,0:T(8,128)S(1)}, u32[]{:S(2)}, u32[]{:S(2)}) %collective-permute-start.4) | collective-permute-done | bytes 135200 | tf_op jit(solution)/shard_map/ppermute | solution.py:298
  21.2 0.5 %collective-permute-done.5.refs_3_ = f32[264,128]{1,0:T(8,128)S(1)} collective-permute-done((f32[264,128]{1,0:T(8,128)S(1)}, f32[264,128]{1,0:T(8,128)S(1)}, u32[]{:S(2)}, u32[]{:S(2)}) %collective-permute-start.5) | collective-permute-done | bytes 135200 | tf_op jit(solution)/shard_map/ppermute | solution.py:298
  21.7 0.1 shard_map.82.mine_ref
  21.7 0.1 collective-permute-start.6
  21.8 1.3 %collective-permute-done.6.other_ref = f32[256,128]{1,0:T(8,128)S(1)} collective-permute-done((f32[256,128]{1,0:T(8,128)S(1)}, f32[256,128]{1,0:T(8,128)S(1)}, u32[]{:S(2)}, u32[]{:S(2)}) %collective-permute-start.6) | collective-permute-done | bytes 131104 | tf_op jit(solution)/shard_map/ppermute | solution.py:302
  23.2 0.0 copy-done.3
  23.2 0.0 copy-done.4
  23.2 0.0 copy-done.5
  23.2 0.6 %shard_map.83 = (bf16[512,128]{1,0:T(8,128)(2,1)S(1)}, f32[128,128]{1,0:T(8,128)S(1)}) custom-call(f32[264,128]{1,0:T(8,128)S(1)} %shard_map.82.mine_ref, f32[256,128]{1,0:T(8,128)S(1)} %collective-permute-done.6.other_ref, bf16[512,128]{1,0:T(8,128)(2,1)S(1)} %copy-done.3, bf16[128,128]{1,0:T(8,128)(2,1)S(1)} %copy-done.5, bf16[512,128]{1,0:T(8,128)(2,1)S(1)} %copy-done.4), custom_call_target="tpu_custom_call" | custom-call | tf_op jit(solution)/shard_map/pallas_call | solution.py:304
  23.8 1.5 %collective-permute-start.7 = (f32[128,128]{1,0:T(8,128)S(1)}, f32[128,128]{1,0:T(8,128)S(1)}, u32[]{:S(2)}, u32[]{:S(2)}) collective-permute-start(f32[128,128]{1,0:T(8,128)S(1)} %get-tuple-element.17.refs_0_), channel_id=1, source_target_pairs={{0,4},{2,6},{4,2},{6,0},{1,5},{3,7},{5,3},{7,1},{8,12},{10,14},{12... | collective-permute-start | bytes 196616 | tf_op jit(solution)/shard_map/ppermute | solution.py:237
  25.3 0.5 %collective-permute-start.8 = (f32[128,128]{1,0:T(8,128)S(1)}, f32[128,128]{1,0:T(8,128)S(1)}, u32[]{:S(2)}, u32[]{:S(2)}) collective-permute-start(f32[128,128]{1,0:T(8,128)S(1)} %get-tuple-element.17.refs_0_), channel_id=1, source_target_pairs={{0,2},{2,0},{4,6},{6,4},{1,3},{3,1},{5,7},{7,5},{8,10},{10,8},{12,... | collective-permute-start | bytes 196616 | tf_op jit(solution)/shard_map/ppermute | solution.py:237
  25.8 2.1 %collective-permute-start.9 = (f32[128,128]{1,0:T(8,128)S(1)}, f32[128,128]{1,0:T(8,128)S(1)}, u32[]{:S(2)}, u32[]{:S(2)}) collective-permute-start(f32[128,128]{1,0:T(8,128)S(1)} %get-tuple-element.17.refs_0_), channel_id=1, source_target_pairs={{0,6},{2,4},{4,0},{6,2},{1,7},{3,5},{5,1},{7,3},{8,14},{10,12},{12... | collective-permute-start | bytes 196616 | tf_op jit(solution)/shard_map/ppermute | solution.py:237
  27.9 1.8 %collective-permute-done.7.refs_1_ = f32[128,128]{1,0:T(8,128)S(1)} collective-permute-done((f32[128,128]{1,0:T(8,128)S(1)}, f32[128,128]{1,0:T(8,128)S(1)}, u32[]{:S(2)}, u32[]{:S(2)}) %collective-permute-start.7) | collective-permute-done | bytes 65568 | tf_op jit(solution)/shard_map/ppermute | solution.py:237
  29.6 0.6 %collective-permute-done.8.refs_2_ = f32[128,128]{1,0:T(8,128)S(1)} collective-permute-done((f32[128,128]{1,0:T(8,128)S(1)}, f32[128,128]{1,0:T(8,128)S(1)}, u32[]{:S(2)}, u32[]{:S(2)}) %collective-permute-start.8) | collective-permute-done | bytes 65568 | tf_op jit(solution)/shard_map/ppermute | solution.py:237
  30.2 0.0 collective-permute-done.9.refs_3_
  30.3 2.8 %collective-permute-start.10 = (f32[128,128]{1,0:T(8,128)S(1)}, f32[128,128]{1,0:T(8,128)S(1)}, u32[]{:S(2)}, u32[]{:S(2)}) collective-permute-start(f32[128,128]{1,0:T(8,128)S(1)} %shard_map.85.refs_0_), channel_id=1, source_target_pairs={{0,16},{8,24},{16,8},{24,0},{1,17},{9,25},{17,9},{25,1},{2,18},{10... | collective-permute-start | bytes 196616 | tf_op jit(solution)/shard_map/ppermute | solution.py:237
  33.1 0.1 collective-permute-start.11
  33.2 1.4 %collective-permute-start.12 = (f32[128,128]{1,0:T(8,128)S(1)}, f32[128,128]{1,0:T(8,128)S(1)}, u32[]{:S(2)}, u32[]{:S(2)}) collective-permute-start(f32[128,128]{1,0:T(8,128)S(1)} %shard_map.85.refs_0_), channel_id=1, source_target_pairs={{0,24},{8,16},{16,0},{24,8},{1,25},{9,17},{17,1},{25,9},{2,26},{10... | collective-permute-start | bytes 196616 | tf_op jit(solution)/shard_map/ppermute | solution.py:237
  34.6 0.7 %shard_map.84 = bf16[512,128]{1,0:T(8,128)(2,1)} custom-call(bf16[512,128]{1,0:T(8,128)(2,1)S(1)} %get-tuple-element.16.x_ref), custom_call_target="tpu_custom_call" | custom-call | tf_op jit(solution)/shard_map/pallas_call | solution.py:311
  35.3 1.2 %collective-permute-done.10.refs_1_ = f32[128,128]{1,0:T(8,128)S(1)} collective-permute-done((f32[128,128]{1,0:T(8,128)S(1)}, f32[128,128]{1,0:T(8,128)S(1)}, u32[]{:S(2)}, u32[]{:S(2)}) %collective-permute-start.10) | collective-permute-done | bytes 65568 | tf_op jit(solution)/shard_map/ppermute | solution.py:237
  36.5 1.3 %collective-permute-done.11.refs_2_ = f32[128,128]{1,0:T(8,128)S(1)} collective-permute-done((f32[128,128]{1,0:T(8,128)S(1)}, f32[128,128]{1,0:T(8,128)S(1)}, u32[]{:S(2)}, u32[]{:S(2)}) %collective-permute-start.11) | collective-permute-done | bytes 65568 | tf_op jit(solution)/shard_map/ppermute | solution.py:237
  37.8 0.7 %collective-permute-done.12.refs_3_ = f32[128,128]{1,0:T(8,128)S(1)} collective-permute-done((f32[128,128]{1,0:T(8,128)S(1)}, f32[128,128]{1,0:T(8,128)S(1)}, u32[]{:S(2)}, u32[]{:S(2)}) %collective-permute-start.12) | collective-permute-done | bytes 65568 | tf_op jit(solution)/shard_map/ppermute | solution.py:237
  38.5 0.6 %shard_map.86 = f32[128,128]{1,0:T(8,128)} custom-call(f32[128,128]{1,0:T(8,128)S(1)} %shard_map.85.refs_0_, f32[128,128]{1,0:T(8,128)S(1)} %collective-permute-done.10.refs_1_, f32[128,128]{1,0:T(8,128)S(1)} %collective-permute-done.11.refs_2_, f32[128,128]{1,0:T(8,128)S(1)} %collective-permute-done.12.refs_3_), custom_call_target="tpu_custom_call" | custom-call | tf_op jit(solution)/shard_map/pallas_call | solution.py:238
  (2 shorter events, 0.0 us)
Async XLA Ops:
  0.6 0.9 %copy-start.2 = (bf16[512,128]{1,0:T(8,128)(2,1)S(1)}, bf16[512,128]{1,0:T(8,128)(2,1)}, u32[]{:S(2)}) copy-start(bf16[512,128]{1,0:T(8,128)(2,1)} %x_ref.3) | copy-start | bytes 393220
  1.6 8.7 %collective-permute-start.2 = (bf16[256,128]{1,0:T(8,128)(2,1)S(1)}, bf16[256,128]{1,0:T(8,128)(2,1)S(1)}, u32[]{:S(2)}, u32[]{:S(2)}) collective-permute-start(bf16[256,128]{1,0:T(8,128)(2,1)S(1)} %shard_map.77.x_ref), channel_id=1, source_target_pairs={{0,16},{8,24},{16,8},{24,0},{1,17},{9,25},{17,9},{25,1},{2,18},{10... | collective-permute-start | bytes 196616 | tf_op jit(solution)/shard_map/ppermute | solution.py:260
  5.7 5.5 %collective-permute-start.1 = (bf16[256,128]{1,0:T(8,128)(2,1)S(1)}, bf16[256,128]{1,0:T(8,128)(2,1)S(1)}, u32[]{:S(2)}, u32[]{:S(2)}) collective-permute-start(bf16[256,128]{1,0:T(8,128)(2,1)S(1)} %shard_map.77.x_ref), channel_id=1, source_target_pairs={{0,8},{8,0},{16,24},{24,16},{1,9},{9,1},{17,25},{25,17},{2,10},{10... | collective-permute-start | bytes 196616 | tf_op jit(solution)/shard_map/ppermute | solution.py:260
  7.3 5.8 %collective-permute-start = (bf16[256,128]{1,0:T(8,128)(2,1)S(1)}, bf16[256,128]{1,0:T(8,128)(2,1)S(1)}, u32[]{:S(2)}, u32[]{:S(2)}) collective-permute-start(bf16[256,128]{1,0:T(8,128)(2,1)S(1)} %shard_map.77.x_ref), channel_id=1, source_target_pairs={{0,24},{8,16},{16,0},{24,8},{1,25},{9,17},{17,1},{25,9},{2,26},{10... | collective-permute-start | bytes 196616 | tf_op jit(solution)/shard_map/ppermute | solution.py:260
  8.4 1.2 %copy-start = (bf16[1,4,8,128,128]{4,3,2,1,0:T(8,128)(2,1)S(1)}, bf16[1,4,8,128,128]{4,3,2,1,0:T(8,128)(2,1)}, u32[]{:S(2)}) copy-start(bf16[1,4,8,128,128]{4,3,2,1,0:T(8,128)(2,1)} %param.10) | copy-start | bytes 3145732
  9.6 1.2 %copy-start.1 = (bf16[1,4,8,128,128]{4,3,2,1,0:T(8,128)(2,1)S(1)}, bf16[1,4,8,128,128]{4,3,2,1,0:T(8,128)(2,1)}, u32[]{:S(2)}) copy-start(bf16[1,4,8,128,128]{4,3,2,1,0:T(8,128)(2,1)} %param.10) | copy-start | bytes 3145732
  13.1 10.1 %copy-start.3 = (bf16[512,128]{1,0:T(8,128)(2,1)S(1)}, bf16[512,128]{1,0:T(8,128)(2,1)}, u32[]{:S(2)}) copy-start(bf16[512,128]{1,0:T(8,128)(2,1)} %x_ref.3) | copy-start | bytes 393220
  13.1 10.1 %copy-start.4 = (bf16[512,128]{1,0:T(8,128)(2,1)S(1)}, bf16[512,128]{1,0:T(8,128)(2,1)}, u32[]{:S(2)}) copy-start(bf16[512,128]{1,0:T(8,128)(2,1)} %cot_ref.1) | copy-start | bytes 393220
  13.1 10.1 %copy-start.5 = (bf16[128,128]{1,0:T(8,128)(2,1)S(1)}, bf16[128,128]{1,0:T(8,128)(2,1)}, u32[]{:S(2)}) copy-start(bf16[128,128]{1,0:T(8,128)(2,1)} %w_ref.1) | copy-start | bytes 98308
  13.6 6.1 %collective-permute-start.3 = (f32[264,128]{1,0:T(8,128)S(1)}, f32[264,128]{1,0:T(8,128)S(1)}, u32[]{:S(2)}, u32[]{:S(2)}) collective-permute-start(f32[264,128]{1,0:T(8,128)S(1)} %get-tuple-element.13), channel_id=1, source_target_pairs={{0,6},{2,4},{4,2},{6,0},{1,7},{3,5},{5,3},{7,1},{8,14},{10,12},{12... | collective-permute-start | bytes 405512 | tf_op jit(solution)/shard_map/ppermute | solution.py:298
  16.1 5.1 %collective-permute-start.4 = (f32[264,128]{1,0:T(8,128)S(1)}, f32[264,128]{1,0:T(8,128)S(1)}, u32[]{:S(2)}, u32[]{:S(2)}) collective-permute-start(f32[264,128]{1,0:T(8,128)S(1)} %get-tuple-element.14), channel_id=1, source_target_pairs={{0,2},{2,6},{4,0},{6,4},{1,3},{3,7},{5,1},{7,5},{8,10},{10,14},{12... | collective-permute-start | bytes 405512 | tf_op jit(solution)/shard_map/ppermute | solution.py:298
  16.7 5.0 %collective-permute-start.5 = (f32[264,128]{1,0:T(8,128)S(1)}, f32[264,128]{1,0:T(8,128)S(1)}, u32[]{:S(2)}, u32[]{:S(2)}) collective-permute-start(f32[264,128]{1,0:T(8,128)S(1)} %get-tuple-element.15), channel_id=1, source_target_pairs={{0,4},{2,0},{4,6},{6,2},{1,5},{3,1},{5,7},{7,3},{8,12},{10,8},{12,... | collective-permute-start | bytes 405512 | tf_op jit(solution)/shard_map/ppermute | solution.py:298
  21.7 1.4 %collective-permute-start.6 = (f32[256,128]{1,0:T(8,128)S(1)}, f32[256,128]{1,0:T(8,128)S(1)}, u32[]{:S(2)}, u32[]{:S(2)}) collective-permute-start(f32[256,128]{1,0:T(8,128)S(1)} %slice.4), channel_id=1, source_target_pairs={{0,1},{1,0},{2,3},{3,2},{4,5},{5,4},{6,7},{7,6},{8,9},{9,8},{10,11... | collective-permute-start | bytes 393224 | tf_op jit(solution)/shard_map/ppermute | solution.py:302
  23.8 5.9 %collective-permute-start.7 = (f32[128,128]{1,0:T(8,128)S(1)}, f32[128,128]{1,0:T(8,128)S(1)}, u32[]{:S(2)}, u32[]{:S(2)}) collective-permute-start(f32[128,128]{1,0:T(8,128)S(1)} %get-tuple-element.17.refs_0_), channel_id=1, source_target_pairs={{0,4},{2,6},{4,2},{6,0},{1,5},{3,7},{5,3},{7,1},{8,12},{10,14},{12... | collective-permute-start | bytes 196616 | tf_op jit(solution)/shard_map/ppermute | solution.py:237
  25.3 4.9 %collective-permute-start.8 = (f32[128,128]{1,0:T(8,128)S(1)}, f32[128,128]{1,0:T(8,128)S(1)}, u32[]{:S(2)}, u32[]{:S(2)}) collective-permute-start(f32[128,128]{1,0:T(8,128)S(1)} %get-tuple-element.17.refs_0_), channel_id=1, source_target_pairs={{0,2},{2,0},{4,6},{6,4},{1,3},{3,1},{5,7},{7,5},{8,10},{10,8},{12,... | collective-permute-start | bytes 196616 | tf_op jit(solution)/shard_map/ppermute | solution.py:237
  25.8 4.4 %collective-permute-start.9 = (f32[128,128]{1,0:T(8,128)S(1)}, f32[128,128]{1,0:T(8,128)S(1)}, u32[]{:S(2)}, u32[]{:S(2)}) collective-permute-start(f32[128,128]{1,0:T(8,128)S(1)} %get-tuple-element.17.refs_0_), channel_id=1, source_target_pairs={{0,6},{2,4},{4,0},{6,2},{1,7},{3,5},{5,1},{7,3},{8,14},{10,12},{12... | collective-permute-start | bytes 196616 | tf_op jit(solution)/shard_map/ppermute | solution.py:237
  30.3 6.2 %collective-permute-start.10 = (f32[128,128]{1,0:T(8,128)S(1)}, f32[128,128]{1,0:T(8,128)S(1)}, u32[]{:S(2)}, u32[]{:S(2)}) collective-permute-start(f32[128,128]{1,0:T(8,128)S(1)} %shard_map.85.refs_0_), channel_id=1, source_target_pairs={{0,16},{8,24},{16,8},{24,0},{1,17},{9,25},{17,9},{25,1},{2,18},{10... | collective-permute-start | bytes 196616 | tf_op jit(solution)/shard_map/ppermute | solution.py:237
  33.1 4.7 %collective-permute-start.11 = (f32[128,128]{1,0:T(8,128)S(1)}, f32[128,128]{1,0:T(8,128)S(1)}, u32[]{:S(2)}, u32[]{:S(2)}) collective-permute-start(f32[128,128]{1,0:T(8,128)S(1)} %shard_map.85.refs_0_), channel_id=1, source_target_pairs={{0,8},{8,0},{16,24},{24,16},{1,9},{9,1},{17,25},{25,17},{2,10},{10... | collective-permute-start | bytes 196616 | tf_op jit(solution)/shard_map/ppermute | solution.py:237
  33.2 5.3 %collective-permute-start.12 = (f32[128,128]{1,0:T(8,128)S(1)}, f32[128,128]{1,0:T(8,128)S(1)}, u32[]{:S(2)}, u32[]{:S(2)}) collective-permute-start(f32[128,128]{1,0:T(8,128)S(1)} %shard_map.85.refs_0_), channel_id=1, source_target_pairs={{0,24},{8,16},{16,0},{24,8},{1,25},{9,17},{17,1},{25,9},{2,26},{10... | collective-permute-start | bytes 196616 | tf_op jit(solution)/shard_map/ppermute | solution.py:237

commit v6 on v5

--- a/solution.py
+++ b/solution.py
@@ -153,29 +153,43 @@
     return high, (x - high.astype(f32)).astype(bf16)
 
 
-def layer_kernel(mine_ref, other_ref, x_ref, w_ref, cot_ref, act_ref, grad_ref):
-    half = other_ref.shape[0]
-    width = other_ref.shape[1]
+def unpack(x, core):
+    width = x.shape[1]
+    moved = pltpu.roll(x, width // 2, 1)
+    first = core == 0
+    here = lower_half(x.shape) == first
+    top = jnp.where(here, jnp.where(first, x, moved), 0.0)
+    low = jnp.where(here, jnp.where(first, moved, x), 0.0)
+    return jnp.concatenate([top, low], axis=0)
+
+
+def before_kernel(mine_ref, x_ref, w_ref, agg_ref, scale_ref, preact_ref):
+    half = x_ref.shape[0] // 2
     tile = 128
-    first = lax.axis_index("feat") == 0
-    mine = mine_ref[:half]
-    other = other_ref[...]
-    here = jnp.where(first, mine, other)
-    there = jnp.where(first, other, mine)
-    left = lower_half(here.shape)
-    top = jnp.where(left, here, pltpu.roll(there, width // 2, 1)) + x_ref[:half].astype(f32)
-    low = jnp.where(left, pltpu.roll(here, width // 2, 1), there) + x_ref[half:].astype(f32)
-    agg = jnp.concatenate([top, low], axis=0)
+    agg = unpack(mine_ref[:half], lax.axis_index("feat")) + x_ref[...].astype(f32)
+    agg_ref[...] = agg
     scales = lax.rsqrt(mine_ref[half:] + 1.0)
-    rows = scales.shape[0]
-    turned = jnp.concatenate([scales] * (128 // rows), axis=0).T
-    scale = jnp.concatenate(
-        [jnp.broadcast_to(turned[:, c : c + 1], (tile, 128)) for c in range(2 * half // tile)],
-        axis=0,
-    )
+    turned = jnp.concatenate([scales] * (128 // scales.shape[0]), axis=0).T
+    for c in range(2 * half // tile):
+        scale_ref[c * tile : (c + 1) * tile] = jnp.broadcast_to(turned[:, c : c + 1], (tile, 128))
     both = jnp.concatenate(split(agg), axis=1)
     w = w_ref[...]
-    preact = scale * jnp.dot(both, jnp.concatenate([w, w], axis=0), preferred_element_type=f32)
+    preact_ref[...] = jnp.dot(both, jnp.concatenate([w, w], axis=0), preferred_element_type=f32)
+
+
+def layer_kernel(
+    other_ref, agg_ref, scale_ref, preact_ref, w_ref, cot_ref, act_ref, grad_ref
+):
+    other = unpack(other_ref[...], 1 - lax.axis_index("feat"))
+    w = w_ref[...]
+    both = jnp.concatenate(split(other), axis=1)
+    preact = scale_ref[...] * (
+        preact_ref[...]
+        + jnp.dot(both, jnp.concatenate([w, w], axis=0), preferred_element_type=f32)
+    )
+    scale = scale_ref[...]
+    agg = agg_ref[...] + other
+    both = jnp.concatenate(split(agg), axis=1)
     sig = 1.0 / (1.0 + jnp.exp(-preact))
     act_ref[...] = (preact * sig).astype(bf16)
     slopes = scale * cot_ref[...].astype(f32) * sig * (1.0 + preact * (1.0 - sig))
@@ -301,11 +315,17 @@
     mine = call(sum_kernel, messages[0], vmem(n_rep))(mine, *parts)
     other = lax.ppermute(mine[:half], "feat", [(0, 1), (1, 0)])
     activated_shape = shape(rows, weight.shape[1], dtype=bf16)
+    agg, scale, preact = call(
+        before_kernel,
+        [shape(rows, width), shape(rows, width), shape(rows, weight.shape[1])],
+        vmem(3),
+        cost=pl.CostEstimate(flops=10**8, bytes_accessed=3 * 10**6, transcendentals=0),
+    )(mine, features, weight)
     activated, grad = call(
         layer_kernel,
         [activated_shape, shape(width, weight.shape[1])],
-        vmem(5),
-    )(mine, other, features, weight, cotangent)
+        vmem(6),
+    )(other, agg, scale, preact, weight, cotangent)
     grad = total_over(grad, "rep")
     grad = total_over(grad, "row")
     activated = call(copy_kernel, activated_shape, vmem(1))(activated)

time: 39.4 us -> 39.4 us (level)
  waiting for transfers between devices: 12 us -> 11.6 us
  transfers between devices with their start and end apart: 13 -> 13, of which waited for: 10 -> 10; matrix products, arithmetic and copies ran while one was open for 2% -> 2% of each run, Pallas kernels for 5% -> 6%
where the time goes in v6:
time: 39.4 us; the launch traced here: 39.1 us
  starting transfers between devices  19.1 us (48%)
  waiting for transfers between devices  11.6 us (29%)
  Pallas kernels  4.29 us (11%)
  local copies, waits for them, and re-layouts  2.65 us (7%)
  other arithmetic  0.75 us (2%)
  between operations  0.74 us (2%)
    ppermute x6, starting transfers between devices, total_over(): lax.ppermute(x, axis, list(enumerate(step)))  8.44 us
    ppermute x3, starting transfers between devices, shards(): lax.ppermute(packed, 'row', list(enumerate(step)))  6 us
    ppermute x6, waiting for transfers between devices, total_over(): lax.ppermute(x, axis, list(enumerate(step)))  5.61 us
    ppermute x3, starting transfers between devices, shards(): lax.ppermute(sent, 'rep', list(enumerate(step)))  4.54 us
    ppermute x3, waiting for transfers between devices, shards(): lax.ppermute(sent, 'rep', list(enumerate(step)))  3.52 us
    unnamed x12, local copies, waits for them, and re-layouts  2.64 us
    ppermute x3, waiting for transfers between devices, shards(): lax.ppermute(packed, 'row', list(enumerate(step)))  1.52 us
    ppermute x1, waiting for transfers between devices, shards(): other = lax.ppermute(mine[:half], 'feat', [(0, 1), (1, 0)])  0.99 us
  transfers between devices with their start and end apart: 13, of which 10 were waited for; matrix products, arithmetic and copies ran while one was open for 2% of the time, Pallas kernels for 6%

profile of v6, /device:TPU:0, one launch (start us, length us, event | category | flops | bytes accessed | tf_op | source)
XLA Modules:
  0.0 39.1 jit_solution(479127143404112794)
XLA Ops:
  0.6 0.0 copy-start.3
  0.6 0.9 %copy-done.3 = bf16[512,128]{1,0:T(8,128)(2,1)S(1)} copy-done((bf16[512,128]{1,0:T(8,128)(2,1)S(1)}, bf16[512,128]{1,0:T(8,128)(2,1)}, u32[]{:S(2)}) %copy-start.3) | copy-done | bytes 131096
  1.5 0.1 shard_map.77.x_ref
  1.6 4.1 %collective-permute-start.2 = (bf16[256,128]{1,0:T(8,128)(2,1)S(1)}, bf16[256,128]{1,0:T(8,128)(2,1)S(1)}, u32[]{:S(2)}, u32[]{:S(2)}) collective-permute-start(bf16[256,128]{1,0:T(8,128)(2,1)S(1)} %shard_map.77.x_ref), channel_id=1, source_target_pairs={{0,16},{8,24},{16,8},{24,0},{1,17},{9,25},{17,9},{25,1},{2,18},{10... | collective-permute-start | bytes 196616 | tf_op jit(solution)/shard_map/ppermute | solution.py:274
  5.7 1.6 %collective-permute-start.1 = (bf16[256,128]{1,0:T(8,128)(2,1)S(1)}, bf16[256,128]{1,0:T(8,128)(2,1)S(1)}, u32[]{:S(2)}, u32[]{:S(2)}) collective-permute-start(bf16[256,128]{1,0:T(8,128)(2,1)S(1)} %shard_map.77.x_ref), channel_id=1, source_target_pairs={{0,8},{8,0},{16,24},{24,16},{1,9},{9,1},{17,25},{25,17},{2,10},{10... | collective-permute-start | bytes 196616 | tf_op jit(solution)/shard_map/ppermute | solution.py:274
  7.3 0.3 collective-permute-start
  7.6 0.8 %bitcast_select_fusion.list_ref.refs_1_ = s32[4,8]{1,0:T(4,128)S(1)} fusion(s32[1,4,8]{2,1,0:T(4,128)} %param.8, s32[4]{0:T(128)} %bitcast.8), kind=kLoop, calls=%fused_computation | loop fusion | flops 64 | bytes 272 | tf_op jit(solution)/shard_map/jit(_where)/select_n | solution.py:264
  8.4 0.0 copy-start
  8.4 1.2 %copy-done = bf16[1,4,8,128,128]{4,3,2,1,0:T(8,128)(2,1)S(1)} copy-done((bf16[1,4,8,128,128]{4,3,2,1,0:T(8,128)(2,1)S(1)}, bf16[1,4,8,128,128]{4,3,2,1,0:T(8,128)(2,1)}, u32[]{:S(2)}) %copy-start) | copy-done | bytes 1048600
  9.6 0.0 copy-start.1
  9.6 0.7 %shard_map.78 = (f32[17,128,128]{2,1,0:T(8,128)S(1)}, f32[16,128]{1,0:T(8,128)S(1)}) custom-call(bf16[4,8,128,128]{3,2,1,0:T(8,128)(2,1)S(1)} %bitcast.4, s32[4,8]{1,0:T(4,128)S(1)} %bitcast_select_fusion.list_ref.refs_1_, bf16[256,128]{1,0:T(8,128)(2,1)S(1)} %shard_map.77.x_ref), custom_call_target="tpu_custom_call" | custom-call | flops 100000000 | bytes 3000000 | tf_op jit(solution)/shard_map/pallas_call | solution.py:282
  10.3 0.0 collective-permute-done.2.block_ref
  10.3 0.5 %copy-done.1 = bf16[1,4,8,128,128]{4,3,2,1,0:T(8,128)(2,1)S(1)} copy-done((bf16[1,4,8,128,128]{4,3,2,1,0:T(8,128)(2,1)S(1)}, bf16[1,4,8,128,128]{4,3,2,1,0:T(8,128)(2,1)}, u32[]{:S(2)}) %copy-start.1) | copy-done | bytes 1048600
  10.8 0.3 shard_map.79.start_ref
  11.2 0.0 collective-permute-done.1.block_ref
  11.2 0.3 shard_map.80.refs_3_
  11.5 1.5 %collective-permute-done.refs_2_ = bf16[256,128]{1,0:T(8,128)(2,1)S(1)} collective-permute-done((bf16[256,128]{1,0:T(8,128)(2,1)S(1)}, bf16[256,128]{1,0:T(8,128)(2,1)S(1)}, u32[]{:S(2)}, u32[]{:S(2)}) %collective-permute-start) | collective-permute-done | bytes 65568 | tf_op jit(solution)/shard_map/ppermute | solution.py:274
  13.1 0.0 copy-start.4
  13.1 0.0 copy-start.5
  13.1 0.5 %shard_map.81 = (f32[264,128]{1,0:T(8,128)S(1)}, f32[264,128]{1,0:T(8,128)S(1)}, f32[264,128]{1,0:T(8,128)S(1)}, f32[264,128]{1,0:T(8,128)S(1)}) custom-call(bf16[4,8,128,128]{3,2,1,0:T(8,128)(2,1)S(1)} %bitcast.7, s32[4,8]{1,0:T(4,128)S(1)} %bitcast_select_fusion.list_ref.refs_1_, bf16[256,128]{1,0:T(8,128)(2,1)S(1)} %collective-permute-done.refs_2_, ...), custom_call_target="tpu_custom_call" | custom-call | tf_op jit(solution)/shard_map/pallas_call | solution.py:300
  13.6 0.0 copy-start.2
  13.6 2.5 %collective-permute-start.3 = (f32[264,128]{1,0:T(8,128)S(1)}, f32[264,128]{1,0:T(8,128)S(1)}, u32[]{:S(2)}, u32[]{:S(2)}) collective-permute-start(f32[264,128]{1,0:T(8,128)S(1)} %get-tuple-element.16), channel_id=1, source_target_pairs={{0,6},{2,4},{4,2},{6,0},{1,7},{3,5},{5,3},{7,1},{8,14},{10,12},{12... | collective-permute-start | bytes 405512 | tf_op jit(solution)/shard_map/ppermute | solution.py:312
  16.1 0.5 %collective-permute-start.4 = (f32[264,128]{1,0:T(8,128)S(1)}, f32[264,128]{1,0:T(8,128)S(1)}, u32[]{:S(2)}, u32[]{:S(2)}) collective-permute-start(f32[264,128]{1,0:T(8,128)S(1)} %get-tuple-element.17), channel_id=1, source_target_pairs={{0,2},{2,6},{4,0},{6,4},{1,3},{3,7},{5,1},{7,5},{8,10},{10,14},{12... | collective-permute-start | bytes 405512 | tf_op jit(solution)/shard_map/ppermute | solution.py:312
  16.7 1.5 %collective-permute-start.5 = (f32[264,128]{1,0:T(8,128)S(1)}, f32[264,128]{1,0:T(8,128)S(1)}, u32[]{:S(2)}, u32[]{:S(2)}) collective-permute-start(f32[264,128]{1,0:T(8,128)S(1)} %get-tuple-element.18), channel_id=1, source_target_pairs={{0,4},{2,0},{4,6},{6,2},{1,5},{3,1},{5,7},{7,3},{8,12},{10,8},{12,... | collective-permute-start | bytes 405512 | tf_op jit(solution)/shard_map/ppermute | solution.py:312
  18.2 1.6 %collective-permute-done.3.refs_1_ = f32[264,128]{1,0:T(8,128)S(1)} collective-permute-done((f32[264,128]{1,0:T(8,128)S(1)}, f32[264,128]{1,0:T(8,128)S(1)}, u32[]{:S(2)}, u32[]{:S(2)}) %collective-permute-start.3) | collective-permute-done | bytes 135200 | tf_op jit(solution)/shard_map/ppermute | solution.py:312
  19.7 1.4 %collective-permute-done.4.refs_2_ = f32[264,128]{1,0:T(8,128)S(1)} collective-permute-done((f32[264,128]{1,0:T(8,128)S(1)}, f32[264,128]{1,0:T(8,128)S(1)}, u32[]{:S(2)}, u32[]{:S(2)}) %collective-permute-start.4) | collective-permute-done | bytes 135200 | tf_op jit(solution)/shard_map/ppermute | solution.py:312
  21.2 0.5 %collective-permute-done.5.refs_3_ = f32[264,128]{1,0:T(8,128)S(1)} collective-permute-done((f32[264,128]{1,0:T(8,128)S(1)}, f32[264,128]{1,0:T(8,128)S(1)}, u32[]{:S(2)}, u32[]{:S(2)}) %collective-permute-start.5) | collective-permute-done | bytes 135200 | tf_op jit(solution)/shard_map/ppermute | solution.py:312
  21.7 0.1 shard_map.82.mine_ref
  21.7 0.1 collective-permute-start.6
  21.8 0.0 copy-done.4
  21.8 0.0 copy-done.5
  21.8 0.3 shard_map.83
  22.2 1.0 %collective-permute-done.6.other_ref = f32[256,128]{1,0:T(8,128)S(1)} collective-permute-done((f32[256,128]{1,0:T(8,128)S(1)}, f32[256,128]{1,0:T(8,128)S(1)}, u32[]{:S(2)}, u32[]{:S(2)}) %collective-permute-start.6) | collective-permute-done | bytes 131104 | tf_op jit(solution)/shard_map/ppermute | solution.py:316
  23.2 0.0 copy-done.2
  23.2 0.6 %shard_map.84 = (bf16[512,128]{1,0:T(8,128)(2,1)S(1)}, f32[128,128]{1,0:T(8,128)S(1)}) custom-call(f32[256,128]{1,0:T(8,128)S(1)} %collective-permute-done.6.other_ref, f32[512,128]{1,0:T(8,128)S(1)} %get-tuple-element.19.agg_ref, f32[512,128]{1,0:T(8,128)S(1)} %get-tuple-element.20.scale_ref, f32[512,128]{1,0:T(8,128)S(1)} %get-tuple-element.21.preact_ref, ...), custom_call_target="tpu_custom_call" | custom-call | tf_op jit(solution)/shard_map/pallas_call | solution.py:324
  23.7 1.5 %collective-permute-start.7 = (f32[128,128]{1,0:T(8,128)S(1)}, f32[128,128]{1,0:T(8,128)S(1)}, u32[]{:S(2)}, u32[]{:S(2)}) collective-permute-start(f32[128,128]{1,0:T(8,128)S(1)} %get-tuple-element.23.refs_0_), channel_id=1, source_target_pairs={{0,4},{2,6},{4,2},{6,0},{1,5},{3,7},{5,3},{7,1},{8,12},{10,14},{12... | collective-permute-start | bytes 196616 | tf_op jit(solution)/shard_map/ppermute | solution.py:251
  25.3 0.5 %collective-permute-start.8 = (f32[128,128]{1,0:T(8,128)S(1)}, f32[128,128]{1,0:T(8,128)S(1)}, u32[]{:S(2)}, u32[]{:S(2)}) collective-permute-start(f32[128,128]{1,0:T(8,128)S(1)} %get-tuple-element.23.refs_0_), channel_id=1, source_target_pairs={{0,2},{2,0},{4,6},{6,4},{1,3},{3,1},{5,7},{7,5},{8,10},{10,8},{12,... | collective-permute-start | bytes 196616 | tf_op jit(solution)/shard_map/ppermute | solution.py:251
  25.8 2.1 %collective-permute-start.9 = (f32[128,128]{1,0:T(8,128)S(1)}, f32[128,128]{1,0:T(8,128)S(1)}, u32[]{:S(2)}, u32[]{:S(2)}) collective-permute-start(f32[128,128]{1,0:T(8,128)S(1)} %get-tuple-element.23.refs_0_), channel_id=1, source_target_pairs={{0,6},{2,4},{4,0},{6,2},{1,7},{3,5},{5,1},{7,3},{8,14},{10,12},{12... | collective-permute-start | bytes 196616 | tf_op jit(solution)/shard_map/ppermute | solution.py:251
  27.9 1.7 %collective-permute-done.7.refs_1_ = f32[128,128]{1,0:T(8,128)S(1)} collective-permute-done((f32[128,128]{1,0:T(8,128)S(1)}, f32[128,128]{1,0:T(8,128)S(1)}, u32[]{:S(2)}, u32[]{:S(2)}) %collective-permute-start.7) | collective-permute-done | bytes 65568 | tf_op jit(solution)/shard_map/ppermute | solution.py:251
  29.6 0.6 %collective-permute-done.8.refs_2_ = f32[128,128]{1,0:T(8,128)S(1)} collective-permute-done((f32[128,128]{1,0:T(8,128)S(1)}, f32[128,128]{1,0:T(8,128)S(1)}, u32[]{:S(2)}, u32[]{:S(2)}) %collective-permute-start.8) | collective-permute-done | bytes 65568 | tf_op jit(solution)/shard_map/ppermute | solution.py:251
  30.2 0.0 collective-permute-done.9.refs_3_
  30.3 2.8 %collective-permute-start.10 = (f32[128,128]{1,0:T(8,128)S(1)}, f32[128,128]{1,0:T(8,128)S(1)}, u32[]{:S(2)}, u32[]{:S(2)}) collective-permute-start(f32[128,128]{1,0:T(8,128)S(1)} %shard_map.86.refs_0_), channel_id=1, source_target_pairs={{0,16},{8,24},{16,8},{24,0},{1,17},{9,25},{17,9},{25,1},{2,18},{10... | collective-permute-start | bytes 196616 | tf_op jit(solution)/shard_map/ppermute | solution.py:251
  33.0 0.1 collective-permute-start.11
  33.2 1.4 %collective-permute-start.12 = (f32[128,128]{1,0:T(8,128)S(1)}, f32[128,128]{1,0:T(8,128)S(1)}, u32[]{:S(2)}, u32[]{:S(2)}) collective-permute-start(f32[128,128]{1,0:T(8,128)S(1)} %shard_map.86.refs_0_), channel_id=1, source_target_pairs={{0,24},{8,16},{16,0},{24,8},{1,25},{9,17},{17,1},{25,9},{2,26},{10... | collective-permute-start | bytes 196616 | tf_op jit(solution)/shard_map/ppermute | solution.py:251
  34.6 0.7 %shard_map.85 = bf16[512,128]{1,0:T(8,128)(2,1)} custom-call(bf16[512,128]{1,0:T(8,128)(2,1)S(1)} %get-tuple-element.22.x_ref), custom_call_target="tpu_custom_call" | custom-call | tf_op jit(solution)/shard_map/pallas_call | solution.py:331
  35.2 1.2 %collective-permute-done.10.refs_1_ = f32[128,128]{1,0:T(8,128)S(1)} collective-permute-done((f32[128,128]{1,0:T(8,128)S(1)}, f32[128,128]{1,0:T(8,128)S(1)}, u32[]{:S(2)}, u32[]{:S(2)}) %collective-permute-start.10) | collective-permute-done | bytes 65568 | tf_op jit(solution)/shard_map/ppermute | solution.py:251
  36.5 1.3 %collective-permute-done.11.refs_2_ = f32[128,128]{1,0:T(8,128)S(1)} collective-permute-done((f32[128,128]{1,0:T(8,128)S(1)}, f32[128,128]{1,0:T(8,128)S(1)}, u32[]{:S(2)}, u32[]{:S(2)}) %collective-permute-start.11) | collective-permute-done | bytes 65568 | tf_op jit(solution)/shard_map/ppermute | solution.py:251
  37.8 0.7 %collective-permute-done.12.refs_3_ = f32[128,128]{1,0:T(8,128)S(1)} collective-permute-done((f32[128,128]{1,0:T(8,128)S(1)}, f32[128,128]{1,0:T(8,128)S(1)}, u32[]{:S(2)}, u32[]{:S(2)}) %collective-permute-start.12) | collective-permute-done | bytes 65568 | tf_op jit(solution)/shard_map/ppermute | solution.py:251
  38.5 0.6 %shard_map.87 = f32[128,128]{1,0:T(8,128)} custom-call(f32[128,128]{1,0:T(8,128)S(1)} %shard_map.86.refs_0_, f32[128,128]{1,0:T(8,128)S(1)} %collective-permute-done.10.refs_1_, f32[128,128]{1,0:T(8,128)S(1)} %collective-permute-done.11.refs_2_, f32[128,128]{1,0:T(8,128)S(1)} %collective-permute-done.12.refs_3_), custom_call_target="tpu_custom_call" | custom-call | tf_op jit(solution)/shard_map/pallas_call | solution.py:252
  (2 shorter events, 0.0 us)
Async XLA Ops:
  0.6 0.9 %copy-start.3 = (bf16[512,128]{1,0:T(8,128)(2,1)S(1)}, bf16[512,128]{1,0:T(8,128)(2,1)}, u32[]{:S(2)}) copy-start(bf16[512,128]{1,0:T(8,128)(2,1)} %x_ref.3) | copy-start | bytes 393220
  1.6 8.7 %collective-permute-start.2 = (bf16[256,128]{1,0:T(8,128)(2,1)S(1)}, bf16[256,128]{1,0:T(8,128)(2,1)S(1)}, u32[]{:S(2)}, u32[]{:S(2)}) collective-permute-start(bf16[256,128]{1,0:T(8,128)(2,1)S(1)} %shard_map.77.x_ref), channel_id=1, source_target_pairs={{0,16},{8,24},{16,8},{24,0},{1,17},{9,25},{17,9},{25,1},{2,18},{10... | collective-permute-start | bytes 196616 | tf_op jit(solution)/shard_map/ppermute | solution.py:274
  5.7 5.5 %collective-permute-start.1 = (bf16[256,128]{1,0:T(8,128)(2,1)S(1)}, bf16[256,128]{1,0:T(8,128)(2,1)S(1)}, u32[]{:S(2)}, u32[]{:S(2)}) collective-permute-start(bf16[256,128]{1,0:T(8,128)(2,1)S(1)} %shard_map.77.x_ref), channel_id=1, source_target_pairs={{0,8},{8,0},{16,24},{24,16},{1,9},{9,1},{17,25},{25,17},{2,10},{10... | collective-permute-start | bytes 196616 | tf_op jit(solution)/shard_map/ppermute | solution.py:274
  7.3 5.8 %collective-permute-start = (bf16[256,128]{1,0:T(8,128)(2,1)S(1)}, bf16[256,128]{1,0:T(8,128)(2,1)S(1)}, u32[]{:S(2)}, u32[]{:S(2)}) collective-permute-start(bf16[256,128]{1,0:T(8,128)(2,1)S(1)} %shard_map.77.x_ref), channel_id=1, source_target_pairs={{0,24},{8,16},{16,0},{24,8},{1,25},{9,17},{17,1},{25,9},{2,26},{10... | collective-permute-start | bytes 196616 | tf_op jit(solution)/shard_map/ppermute | solution.py:274
  8.4 1.2 %copy-start = (bf16[1,4,8,128,128]{4,3,2,1,0:T(8,128)(2,1)S(1)}, bf16[1,4,8,128,128]{4,3,2,1,0:T(8,128)(2,1)}, u32[]{:S(2)}) copy-start(bf16[1,4,8,128,128]{4,3,2,1,0:T(8,128)(2,1)} %param.10) | copy-start | bytes 3145732
  9.6 1.2 %copy-start.1 = (bf16[1,4,8,128,128]{4,3,2,1,0:T(8,128)(2,1)S(1)}, bf16[1,4,8,128,128]{4,3,2,1,0:T(8,128)(2,1)}, u32[]{:S(2)}) copy-start(bf16[1,4,8,128,128]{4,3,2,1,0:T(8,128)(2,1)} %param.10) | copy-start | bytes 3145732
  13.1 8.8 %copy-start.4 = (bf16[512,128]{1,0:T(8,128)(2,1)S(1)}, bf16[512,128]{1,0:T(8,128)(2,1)}, u32[]{:S(2)}) copy-start(bf16[512,128]{1,0:T(8,128)(2,1)} %x_ref.3) | copy-start | bytes 393220
  13.1 8.8 %copy-start.5 = (bf16[128,128]{1,0:T(8,128)(2,1)S(1)}, bf16[128,128]{1,0:T(8,128)(2,1)}, u32[]{:S(2)}) copy-start(bf16[128,128]{1,0:T(8,128)(2,1)} %w_ref.3) | copy-start | bytes 98308
  13.6 9.6 %copy-start.2 = (bf16[512,128]{1,0:T(8,128)(2,1)S(1)}, bf16[512,128]{1,0:T(8,128)(2,1)}, u32[]{:S(2)}) copy-start(bf16[512,128]{1,0:T(8,128)(2,1)} %cot_ref.1) | copy-start | bytes 393220
  13.6 6.1 %collective-permute-start.3 = (f32[264,128]{1,0:T(8,128)S(1)}, f32[264,128]{1,0:T(8,128)S(1)}, u32[]{:S(2)}, u32[]{:S(2)}) collective-permute-start(f32[264,128]{1,0:T(8,128)S(1)} %get-tuple-element.16), channel_id=1, source_target_pairs={{0,6},{2,4},{4,2},{6,0},{1,7},{3,5},{5,3},{7,1},{8,14},{10,12},{12... | collective-permute-start | bytes 405512 | tf_op jit(solution)/shard_map/ppermute | solution.py:312
  16.1 5.1 %collective-permute-start.4 = (f32[264,128]{1,0:T(8,128)S(1)}, f32[264,128]{1,0:T(8,128)S(1)}, u32[]{:S(2)}, u32[]{:S(2)}) collective-permute-start(f32[264,128]{1,0:T(8,128)S(1)} %get-tuple-element.17), channel_id=1, source_target_pairs={{0,2},{2,6},{4,0},{6,4},{1,3},{3,7},{5,1},{7,5},{8,10},{10,14},{12... | collective-permute-start | bytes 405512 | tf_op jit(solution)/shard_map/ppermute | solution.py:312
  16.7 5.0 %collective-permute-start.5 = (f32[264,128]{1,0:T(8,128)S(1)}, f32[264,128]{1,0:T(8,128)S(1)}, u32[]{:S(2)}, u32[]{:S(2)}) collective-permute-start(f32[264,128]{1,0:T(8,128)S(1)} %get-tuple-element.18), channel_id=1, source_target_pairs={{0,4},{2,0},{4,6},{6,2},{1,5},{3,1},{5,7},{7,3},{8,12},{10,8},{12,... | collective-permute-start | bytes 405512 | tf_op jit(solution)/shard_map/ppermute | solution.py:312
  21.7 1.4 %collective-permute-start.6 = (f32[256,128]{1,0:T(8,128)S(1)}, f32[256,128]{1,0:T(8,128)S(1)}, u32[]{:S(2)}, u32[]{:S(2)}) collective-permute-start(f32[256,128]{1,0:T(8,128)S(1)} %slice.4), channel_id=1, source_target_pairs={{0,1},{1,0},{2,3},{3,2},{4,5},{5,4},{6,7},{7,6},{8,9},{9,8},{10,11... | collective-permute-start | bytes 393224 | tf_op jit(solution)/shard_map/ppermute | solution.py:316
  23.7 5.9 %collective-permute-start.7 = (f32[128,128]{1,0:T(8,128)S(1)}, f32[128,128]{1,0:T(8,128)S(1)}, u32[]{:S(2)}, u32[]{:S(2)}) collective-permute-start(f32[128,128]{1,0:T(8,128)S(1)} %get-tuple-element.23.refs_0_), channel_id=1, source_target_pairs={{0,4},{2,6},{4,2},{6,0},{1,5},{3,7},{5,3},{7,1},{8,12},{10,14},{12... | collective-permute-start | bytes 196616 | tf_op jit(solution)/shard_map/ppermute | solution.py:251
  25.3 4.9 %collective-permute-start.8 = (f32[128,128]{1,0:T(8,128)S(1)}, f32[128,128]{1,0:T(8,128)S(1)}, u32[]{:S(2)}, u32[]{:S(2)}) collective-permute-start(f32[128,128]{1,0:T(8,128)S(1)} %get-tuple-element.23.refs_0_), channel_id=1, source_target_pairs={{0,2},{2,0},{4,6},{6,4},{1,3},{3,1},{5,7},{7,5},{8,10},{10,8},{12,... | collective-permute-start | bytes 196616 | tf_op jit(solution)/shard_map/ppermute | solution.py:251
  25.8 4.5 %collective-permute-start.9 = (f32[128,128]{1,0:T(8,128)S(1)}, f32[128,128]{1,0:T(8,128)S(1)}, u32[]{:S(2)}, u32[]{:S(2)}) collective-permute-start(f32[128,128]{1,0:T(8,128)S(1)} %get-tuple-element.23.refs_0_), channel_id=1, source_target_pairs={{0,6},{2,4},{4,0},{6,2},{1,7},{3,5},{5,1},{7,3},{8,14},{10,12},{12... | collective-permute-start | bytes 196616 | tf_op jit(solution)/shard_map/ppermute | solution.py:251
  30.3 6.2 %collective-permute-start.10 = (f32[128,128]{1,0:T(8,128)S(1)}, f32[128,128]{1,0:T(8,128)S(1)}, u32[]{:S(2)}, u32[]{:S(2)}) collective-permute-start(f32[128,128]{1,0:T(8,128)S(1)} %shard_map.86.refs_0_), channel_id=1, source_target_pairs={{0,16},{8,24},{16,8},{24,0},{1,17},{9,25},{17,9},{25,1},{2,18},{10... | collective-permute-start | bytes 196616 | tf_op jit(solution)/shard_map/ppermute | solution.py:251
  33.0 4.7 %collective-permute-start.11 = (f32[128,128]{1,0:T(8,128)S(1)}, f32[128,128]{1,0:T(8,128)S(1)}, u32[]{:S(2)}, u32[]{:S(2)}) collective-permute-start(f32[128,128]{1,0:T(8,128)S(1)} %shard_map.86.refs_0_), channel_id=1, source_target_pairs={{0,8},{8,0},{16,24},{24,16},{1,9},{9,1},{17,25},{25,17},{2,10},{10... | collective-permute-start | bytes 196616 | tf_op jit(solution)/shard_map/ppermute | solution.py:251
  33.2 5.3 %collective-permute-start.12 = (f32[128,128]{1,0:T(8,128)S(1)}, f32[128,128]{1,0:T(8,128)S(1)}, u32[]{:S(2)}, u32[]{:S(2)}) collective-permute-start(f32[128,128]{1,0:T(8,128)S(1)} %shard_map.86.refs_0_), channel_id=1, source_target_pairs={{0,24},{8,16},{16,0},{24,8},{1,25},{9,17},{17,1},{25,9},{2,26},{10... | collective-permute-start | bytes 196616 | tf_op jit(solution)/shard_map/ppermute | solution.py:251
